TPU v7x, 32 devices: a whole 2x2x4 slice. The times are simulated.
32 devices in a mesh: items: 4 (over y, x), strips: 8 (over z, core).
Axes of the slice: x: 2, y: 2, z: 4, core: 2. Of those that a mesh axis runs over, the one named last changes fastest.
Arguments:
- latents: bfloat16 [8, 64, 64, 768], P('items', 'strips'), may hold values from -24 to 24
- timesteps: int32 [8], P('items'), may hold values from 0 to 999
- labels: int32 [8], P('items'), may hold values from 0 to 1000
- time_in_weight: bfloat16 [256, 768], replicated, may hold values from -0.375 to 0.375
- time_in_bias: bfloat16 [768], replicated, may hold values from -3 to 3
- time_out_weight: bfloat16 [768, 768], replicated, may hold values from -0.21875 to 0.21875
- time_out_bias: bfloat16 [768], replicated, may hold values from -3 to 3
- label_table: bfloat16 [768, 1001], replicated, may hold values from -6 to 6
- ada_weight: bfloat16 [768, 4608], replicated, may hold values from -0.3125 to 0.3125
- ada_bias: bfloat16 [4608], replicated, may hold values from -3 to 3
- down_kernel: bfloat16 [768, 9], replicated, may hold values from -2 to 2
- down_bias: bfloat16 [768], replicated, may hold values from -3 to 3
- input_weight: bfloat16 [768, 2304], replicated, may hold values from -0.21875 to 0.21875
- query_bias: bfloat16 [768], replicated, may hold values from -3 to 3
- value_bias: bfloat16 [768], replicated, may hold values from -0.625 to 0.625
- output_weight: bfloat16 [768, 768], replicated, may hold values from -2.5 to 2.5
- output_bias: bfloat16 [768], replicated, may hold values from -3 to 3
- expand_weight: bfloat16 [768, 3072], replicated, may hold values from -0.21875 to 0.21875
- expand_bias: bfloat16 [3072], replicated, may hold values from -3 to 3
- mixer_kernel: bfloat16 [3072, 9], replicated, may hold values from -2 to 2
- mixer_bias: bfloat16 [3072], replicated, may hold values from -3 to 3
- shrink_weight: bfloat16 [3072, 768], replicated, may hold values from -0.109375 to 0.109375
- shrink_bias: bfloat16 [768], replicated, may hold values from -6 to 6
- cotangent: bfloat16 [8, 64, 64, 768], P('items', 'strips'), may hold values from -6 to 6
Outputs:
- result: bfloat16 [8, 64, 64, 768], P('items', 'strips')
- grad_latents: bfloat16 [8, 64, 64, 768], P('items', 'strips')
- grad_time_in_weight: float32 [256, 768], P(('items', 'strips'))
- grad_time_in_bias: float32 [768], P(('items', 'strips'))
- grad_time_out_weight: float32 [768, 768], P(('items', 'strips'))
- grad_time_out_bias: float32 [768], P(('items', 'strips'))
- grad_label_table: float32 [768, 1001], P(('items', 'strips'))
- grad_ada_weight: float32 [768, 4608], P(('items', 'strips'))
- grad_ada_bias: float32 [4608], P(('items', 'strips'))
- grad_down_kernel: float32 [768, 9], P(('items', 'strips'))
- grad_down_bias: float32 [768], P(('items', 'strips'))
- grad_input_weight: float32 [768, 2304], P(('items', 'strips'))
- grad_query_bias: float32 [768], P(('items', 'strips'))
- grad_value_bias: float32 [768], P(('items', 'strips'))
- grad_output_weight: float32 [768, 768], P(('items', 'strips'))
- grad_output_bias: float32 [768], P(('items', 'strips'))
- grad_expand_weight: float32 [768, 3072], P(('items', 'strips'))
- grad_expand_bias: float32 [3072], P(('items', 'strips'))
- grad_mixer_kernel: float32 [3072, 9], P(('items', 'strips'))
- grad_mixer_bias: float32 [3072], P(('items', 'strips'))
- grad_shrink_weight: float32 [3072, 768], P(('items', 'strips'))
- grad_shrink_bias: float32 [768], P(('items', 'strips'))
All inputs are finite; a program needn't handle non-finite values.
Results may differ from a plain program's by a relative error of at most 0.025.
Values may be sent and summed in bfloat16 or wider, within the bound.
No kernel may reach another device: no remote copies, remote signals or barrier semaphores. Data moves between devices by JAX's collectives and lax.ppermute only.
A program may use at most 384 MiB of HBM per device.

v0:
```python
from functools import partial
import math

import jax
import jax.numpy as jnp
from jax import lax
from jax.sharding import PartitionSpec as P

HEADS = 12
HEAD_DIM = 64


highest = lax.Precision.HIGHEST
epsilon = 1e-06


def with_halo(cells, sides, width):
    for axis, dim in sides:
        count = lax.axis_size(axis)
        ends = count - 1
        head = lax.slice_in_dim(cells, 0, width, axis=dim)
        tail = lax.slice_in_dim(cells, cells.shape[dim] - width, cells.shape[dim], axis=dim)
        cells = jnp.concatenate(
            [
                lax.ppermute(tail, axis, [(i, (i + 1) % count) for i in range(ends)]),
                cells,
                lax.ppermute(head, axis, [((i + 1) % count, i) for i in range(ends)]),
            ],
            axis=dim,
        )
    return cells


def layer_norm(value):
    center = value - jnp.mean(value, axis=-1, keepdims=True)
    spread = jnp.mean(center * center, axis=-1, keepdims=True)
    return center * lax.rsqrt(spread + epsilon)


def time_features(timesteps, halves):
    frequency = jnp.exp(-math.log(10000.0) * jnp.arange(halves, dtype=jnp.float32) / halves)
    phase = timesteps.astype(jnp.float32)[:, None] * frequency[None, :]
    return jnp.concatenate([jnp.cos(phase), jnp.sin(phase)], axis=1)


def condition(
    timesteps,
    labels,
    time_in_weight,
    time_in_bias,
    time_out_weight,
    time_out_bias,
    label_table,
    ada_weight,
    ada_bias,
):
    sinus = time_features(timesteps, time_in_weight.shape[0] // 2)
    inner = jax.nn.silu(jnp.dot(sinus, time_in_weight, precision=highest) + time_in_bias)
    time_vector = jnp.dot(inner, time_out_weight, precision=highest) + time_out_bias
    onehot = (labels[:, None] == jnp.arange(label_table.shape[1], dtype=jnp.int32)[None, :]).astype(
        jnp.float32
    )
    class_vector = lax.dot_general(onehot, label_table, (((1,), (1,)), ((), ())), precision=highest)
    cond_vector = time_vector + class_vector
    return jnp.dot(jax.nn.silu(cond_vector), ada_weight, precision=highest) + ada_bias


def pad_columns(array):
    return jnp.pad(array.astype(jnp.float32), ((0, 0), (0, 0), (1, 1), (0, 0)))


def depthwise_rows(wide, kernel, offset):
    rows = wide.shape[1] - 2
    columns = wide.shape[2]
    padded = pad_columns(wide)
    total = offset + jnp.zeros((wide.shape[0], rows, columns, wide.shape[3]), jnp.float32)
    for row_step in range(3):
        for column_step in range(3):
            total = (
                total
                + kernel[:, row_step * 3 + column_step]
                * padded[:, row_step : row_step + rows, column_step : column_step + columns, :]
            )
    return total


def depthwise_back(grad_wide, input_wide, kernel):
    rows = grad_wide.shape[1] - 2
    columns = grad_wide.shape[2]
    grad_padded = pad_columns(grad_wide)
    input_padded = pad_columns(input_wide)
    center = grad_padded[:, 1 : rows + 1, 1 : columns + 1, :]
    d_input = jnp.zeros_like(center)
    taps = []
    for row_step in range(3):
        for column_step in range(3):
            d_input = (
                d_input
                + kernel[:, row_step * 3 + column_step]
                * grad_padded[
                    :,
                    2 - row_step : 2 - row_step + rows,
                    2 - column_step : 2 - column_step + columns,
                    :,
                ]
            )
            taps.append(
                jnp.sum(
                    center
                    * input_padded[
                        :, row_step : row_step + rows, column_step : column_step + columns, :
                    ],
                    axis=(0, 1, 2),
                )
            )
    return (d_input, jnp.stack(taps, axis=1), jnp.sum(center, axis=(0, 1, 2)))


def to_groups(image):
    count, rows, columns, features = image.shape
    split = image.reshape(count, rows // 2, 2, columns // 2, 2, features).transpose(
        0, 2, 4, 1, 3, 5
    )
    return split.reshape(count, 4, rows // 2 * (columns // 2), features)


def from_groups(grouped, rows, columns):
    count, features = (grouped.shape[0], grouped.shape[3])
    split = grouped.reshape(count, 2, 2, rows // 2, columns // 2, features).transpose(
        0, 3, 1, 4, 2, 5
    )
    return split.reshape(count, rows, columns, features)


def split_heads(array):
    return array.reshape(array.shape[0], array.shape[1], array.shape[2], HEADS, HEAD_DIM)


def merge_heads(array):
    return array.reshape(array.shape[0], array.shape[1], array.shape[2], HEADS * HEAD_DIM)


def sum_joint(parts):
    return (
        lax.psum_scatter(parts[0], ("items", "strips"), scatter_dimension=0, tiled=True),
        lax.psum_scatter(parts[1], ("items", "strips"), scatter_dimension=0, tiled=True),
        lax.psum_scatter(parts[2], ("items", "strips"), scatter_dimension=0, tiled=True),
        lax.psum_scatter(parts[3], ("items", "strips"), scatter_dimension=0, tiled=True),
        lax.psum_scatter(parts[4], ("items", "strips"), scatter_dimension=0, tiled=True),
        lax.psum_scatter(parts[5], ("items", "strips"), scatter_dimension=0, tiled=True),
        lax.psum_scatter(parts[6], ("items", "strips"), scatter_dimension=0, tiled=True),
        lax.psum_scatter(parts[7], ("items", "strips"), scatter_dimension=0, tiled=True),
        lax.psum_scatter(parts[8], ("items", "strips"), scatter_dimension=0, tiled=True),
        lax.psum_scatter(parts[9], ("items", "strips"), scatter_dimension=0, tiled=True),
        lax.psum_scatter(parts[10], ("items", "strips"), scatter_dimension=0, tiled=True),
        lax.psum_scatter(parts[11], ("items", "strips"), scatter_dimension=0, tiled=True),
        lax.psum_scatter(parts[12], ("items", "strips"), scatter_dimension=0, tiled=True),
        lax.psum_scatter(parts[13], ("items", "strips"), scatter_dimension=0, tiled=True),
        lax.psum_scatter(parts[14], ("items", "strips"), scatter_dimension=0, tiled=True),
        lax.psum_scatter(parts[15], ("items", "strips"), scatter_dimension=0, tiled=True),
        lax.psum_scatter(parts[16], ("items", "strips"), scatter_dimension=0, tiled=True),
        lax.psum_scatter(parts[17], ("items", "strips"), scatter_dimension=0, tiled=True),
        lax.psum_scatter(parts[18], ("items", "strips"), scatter_dimension=0, tiled=True),
        lax.psum_scatter(parts[19], ("items", "strips"), scatter_dimension=0, tiled=True),
    )


def per_device(
    latents,
    timesteps,
    labels,
    time_in_weight,
    time_in_bias,
    time_out_weight,
    time_out_bias,
    label_table,
    ada_weight,
    ada_bias,
    down_kernel,
    down_bias,
    input_weight,
    query_bias,
    value_bias,
    output_weight,
    output_bias,
    expand_weight,
    expand_bias,
    mixer_kernel,
    mixer_bias,
    shrink_weight,
    shrink_bias,
    cotangent,
):
    count, rows, columns, features = latents.shape
    scale = 1.0 / math.sqrt(HEAD_DIM)
    bfloat = jnp.bfloat16
    single = jnp.float32
    cond_weights = tuple(
        (
            weight.astype(single)
            for weight in (
                time_in_weight,
                time_in_bias,
                time_out_weight,
                time_out_bias,
                label_table,
                ada_weight,
                ada_bias,
            )
        )
    )

    def modulate(w_time_in, b_time_in, w_time_out, b_time_out, table, w_ada, b_ada):
        return condition(
            timesteps, labels, w_time_in, b_time_in, w_time_out, b_time_out, table, w_ada, b_ada
        )

    modulation, cond_pullback = jax.vjp(modulate, *cond_weights)
    pieces = modulation.reshape(count, 6, 1, 1, features)
    shift_a, scale_a, gate_a = (pieces[:, 0], pieces[:, 1], pieces[:, 2])
    shift_b, scale_b, gate_b = (pieces[:, 3], pieces[:, 4], pieces[:, 5])
    image = latents.astype(single)
    norm_a = layer_norm(image)
    normed_a = (norm_a * (1.0 + scale_a) + shift_a).astype(bfloat)
    normed_wide = with_halo(normed_a, (("strips", 1),), 1)
    down_single = down_kernel.astype(single)
    reduced = depthwise_rows(normed_wide, down_single, down_bias.astype(single)).astype(bfloat)
    grouped = to_groups(reduced)
    projected = jnp.einsum("lgsd,de->lgse", grouped, input_weight, preferred_element_type=single)
    query = (projected[..., :features] + query_bias.astype(single)).astype(bfloat)
    key = projected[..., features : 2 * features].astype(bfloat)
    value = (projected[..., 2 * features :] + value_bias.astype(single)).astype(bfloat)
    keys_all, values_all = (
        lax.all_gather(key, "strips", axis=2, tiled=True),
        lax.all_gather(value, "strips", axis=2, tiled=True),
    )
    scores = (
        jnp.einsum(
            "lgqhe,lgkhe->lghqk",
            split_heads(query),
            split_heads(keys_all),
            preferred_element_type=single,
        )
        * scale
    )
    peak = jnp.max(scores, axis=-1, keepdims=True)
    logsum = peak + jnp.log(jnp.sum(jnp.exp(scores - peak), axis=-1, keepdims=True))
    softened = jnp.exp(scores - logsum)
    mixed = merge_heads(
        jnp.einsum(
            "lghqk,lgkhe->lgqhe",
            softened.astype(bfloat),
            split_heads(values_all),
            preferred_element_type=single,
        )
    ).astype(bfloat)
    attended = jnp.einsum(
        "lgsd,de->lgse", mixed, output_weight, preferred_element_type=single
    ) + output_bias.astype(single)
    attended_image = from_groups(attended, rows, columns)
    middle = image + gate_a * attended_image
    norm_b = layer_norm(middle)
    normed_b = (norm_b * (1.0 + scale_b) + shift_b).astype(bfloat)
    hidden = (
        jnp.einsum("lrcd,df->lrcf", normed_b, expand_weight, preferred_element_type=single)
        + expand_bias.astype(single)
    ).astype(bfloat)
    hidden_wide = with_halo(hidden, (("strips", 1),), 1)
    mixer_single = mixer_kernel.astype(single)
    conved = depthwise_rows(hidden_wide, mixer_single, mixer_bias.astype(single))
    activated = jax.nn.gelu(conved, approximate=True).astype(bfloat)
    branch = jnp.einsum(
        "lrcf,fd->lrcd", activated, shrink_weight, preferred_element_type=single
    ) + shrink_bias.astype(single)
    result = (middle + gate_b * branch).astype(bfloat)
    upstream = cotangent.astype(single)
    d_gate_b = jnp.sum(upstream * branch, axis=(1, 2))
    d_branch = (upstream * gate_b).astype(bfloat)
    grad_shrink_weight = jnp.einsum(
        "lrcf,lrcd->fd", activated, d_branch, preferred_element_type=single
    )
    grad_shrink_bias = jnp.sum(d_branch.astype(single), axis=(0, 1, 2))
    d_activated = jnp.einsum(
        "lrcd,fd->lrcf", d_branch, shrink_weight, preferred_element_type=single
    )
    gelu_pullback = jax.vjp(partial(jax.nn.gelu, approximate=True), conved)[1]
    d_conved = gelu_pullback(d_activated)[0].astype(bfloat)
    d_conved_wide = with_halo(d_conved, (("strips", 1),), 1)
    d_hidden_single, grad_mixer_kernel, grad_mixer_bias = depthwise_back(
        d_conved_wide, hidden_wide, mixer_single
    )
    d_hidden = d_hidden_single.astype(bfloat)
    grad_expand_weight = jnp.einsum(
        "lrcd,lrcf->df", normed_b, d_hidden, preferred_element_type=single
    )
    grad_expand_bias = jnp.sum(d_hidden.astype(single), axis=(0, 1, 2))
    d_normed_b = jnp.einsum("lrcf,df->lrcd", d_hidden, expand_weight, preferred_element_type=single)
    d_shift_b = jnp.sum(d_normed_b, axis=(1, 2))
    d_scale_b = jnp.sum(d_normed_b * norm_b, axis=(1, 2))
    norm_pullback_b = jax.vjp(layer_norm, middle)[1]
    d_middle = upstream + norm_pullback_b(d_normed_b * (1.0 + scale_b))[0]
    d_gate_a = jnp.sum(d_middle * attended_image, axis=(1, 2))
    d_attended = to_groups((d_middle * gate_a).astype(bfloat))
    grad_output_weight = jnp.einsum(
        "lgsd,lgse->de", mixed, d_attended, preferred_element_type=single
    )
    grad_output_bias = jnp.sum(d_attended.astype(single), axis=(0, 1, 2))
    d_mixed = jnp.einsum(
        "lgse,de->lgsd", d_attended, output_weight, preferred_element_type=single
    ).astype(bfloat)
    keys_back, values_back = (keys_all, values_all)
    scores_back = (
        jnp.einsum(
            "lgqhe,lgkhe->lghqk",
            split_heads(query),
            split_heads(keys_back),
            preferred_element_type=single,
        )
        * scale
    )
    soft_back = jnp.exp(scores_back - logsum)
    d_soft = jnp.einsum(
        "lgqhe,lgkhe->lghqk",
        split_heads(d_mixed),
        split_heads(values_back),
        preferred_element_type=single,
    )
    row_total = jnp.sum(soft_back * d_soft, axis=-1, keepdims=True)
    d_scores = (soft_back * (d_soft - row_total)).astype(bfloat)
    d_value_part = merge_heads(
        jnp.einsum(
            "lghqk,lgqhe->lgkhe",
            soft_back.astype(bfloat),
            split_heads(d_mixed),
            preferred_element_type=single,
        )
    )
    d_key_part = (
        merge_heads(
            jnp.einsum(
                "lghqk,lgqhe->lgkhe", d_scores, split_heads(query), preferred_element_type=single
            )
        )
        * scale
    )
    d_query = (
        merge_heads(
            jnp.einsum(
                "lghqk,lgkhe->lgqhe",
                d_scores,
                split_heads(keys_back),
                preferred_element_type=single,
            )
        )
        * scale
    ).astype(bfloat)
    d_key_sum, d_value_sum = (
        lax.psum_scatter(
            d_key_part.astype(jnp.bfloat16), "strips", scatter_dimension=2, tiled=True
        ).astype(jnp.float32),
        lax.psum_scatter(
            d_value_part.astype(jnp.bfloat16), "strips", scatter_dimension=2, tiled=True
        ).astype(jnp.float32),
    )
    d_key = d_key_sum.astype(bfloat)
    d_value = d_value_sum.astype(bfloat)
    d_projected = jnp.concatenate([d_query, d_key, d_value], axis=-1)
    grad_input_weight = jnp.einsum(
        "lgsd,lgse->de", grouped, d_projected, preferred_element_type=single
    )
    grad_query_bias = jnp.sum(d_query.astype(single), axis=(0, 1, 2))
    grad_value_bias = jnp.sum(d_value.astype(single), axis=(0, 1, 2))
    d_reduced = from_groups(
        jnp.einsum(
            "lgse,de->lgsd", d_projected, input_weight, preferred_element_type=single
        ).astype(bfloat),
        rows,
        columns,
    )
    d_reduced_wide = with_halo(d_reduced, (("strips", 1),), 1)
    d_normed_a, grad_down_kernel, grad_down_bias = depthwise_back(
        d_reduced_wide, normed_wide, down_single
    )
    d_shift_a = jnp.sum(d_normed_a, axis=(1, 2))
    d_scale_a = jnp.sum(d_normed_a * norm_a, axis=(1, 2))
    norm_pullback_a = jax.vjp(layer_norm, image)[1]
    grad_latents = (d_middle + norm_pullback_a(d_normed_a * (1.0 + scale_a))[0]).astype(bfloat)
    d_modulation = jnp.stack(
        [d_shift_a, d_scale_a, d_gate_a, d_shift_b, d_scale_b, d_gate_b], axis=1
    ).reshape(count, 6 * features)
    (
        grad_time_in_weight,
        grad_time_in_bias,
        grad_time_out_weight,
        grad_time_out_bias,
        grad_label_table,
        grad_ada_weight,
        grad_ada_bias,
    ) = cond_pullback(d_modulation)
    partials = (
        grad_time_in_weight,
        grad_time_in_bias,
        grad_time_out_weight,
        grad_time_out_bias,
        grad_label_table,
        grad_ada_weight,
        grad_ada_bias,
        grad_down_kernel,
        grad_down_bias,
        grad_input_weight,
        grad_query_bias,
        grad_value_bias,
        grad_output_weight,
        grad_output_bias,
        grad_expand_weight,
        grad_expand_bias,
        grad_mixer_kernel,
        grad_mixer_bias,
        grad_shrink_weight,
        grad_shrink_bias,
    )
    summed = sum_joint(partials)
    return (
        result,
        grad_latents,
        summed[0],
        summed[1],
        summed[2],
        summed[3],
        summed[4],
        summed[5],
        summed[6],
        summed[7],
        summed[8],
        summed[9],
        summed[10],
        summed[11],
        summed[12],
        summed[13],
        summed[14],
        summed[15],
        summed[16],
        summed[17],
        summed[18],
        summed[19],
    )


def solution(mesh):
    return jax.shard_map(
        per_device,
        mesh=mesh,
        in_specs=(
            P("items", "strips", None, None),
            P("items"),
            P("items"),
            P(),
            P(),
            P(),
            P(),
            P(),
            P(),
            P(),
            P(),
            P(),
            P(),
            P(),
            P(),
            P(),
            P(),
            P(),
            P(),
            P(),
            P(),
            P(),
            P(),
            P("items", "strips", None, None),
        ),
        out_specs=(
            P("items", "strips", None, None),
            P("items", "strips", None, None),
            P(("items", "strips"), None),
            P(("items", "strips")),
            P(("items", "strips"), None),
            P(("items", "strips")),
            P(("items", "strips"), None),
            P(("items", "strips"), None),
            P(("items", "strips")),
            P(("items", "strips"), None),
            P(("items", "strips")),
            P(("items", "strips"), None),
            P(("items", "strips")),
            P(("items", "strips")),
            P(("items", "strips"), None),
            P(("items", "strips")),
            P(("items", "strips"), None),
            P(("items", "strips")),
            P(("items", "strips"), None),
            P(("items", "strips")),
            P(("items", "strips"), None),
            P(("items", "strips")),
        ),
        check_vma=False,
    )
```

profile of v0, /device:TPU:0, one launch (start us, length us, event | category | flops | bytes accessed | tf_op | source)
XLA Modules:
  0.0 2099.0 jit_solution(15325136962877357744)
XLA Ops:
  70.3 110.2 %all-gather.5.cloned.1.call-done = bf16[2,4,1024,768]{3,2,1,0:T(8,128)(2,1)} async-done(((bf16[2,4,128,768]{3,2,1,0:T(8,128)(2,1)}), bf16[2,4,1024,768]{3,2,1,0:T(8,128)(2,1)}) %all-gather.5.cloned.1.call-update) | async-done | bytes 12582928 | tf_op jit(solution)/shard_map/all_gather | solution.py:234
  180.4 16.7 copy.101
  197.2 23.1 %multiply_reduce_fusion.1 = (f32[2,4,12,128]{3,2,1,0:T(8,128)S(1)}, f32[2,4,12,128,1024]{4,3,2,1,0:T(8,128)}) fusion(bf16[2,4,128,12,64]{2,4,3,1,0:T(8,128)(2,1)} %bitcast.174, bf16[2,4,1024,12,64]{2,4,3,1,0:T(8,128)(2,1)} %bitcast.162), kind=kOutput, calls=%fused_computation.4 | convolution fusion | flops 1635766272 | bytes 64536576 | tf_op jit(solution)/shard_map/lgqhe,lgkhe->lghqk/dot_general | solution.py:238
  220.3 21.1 %exponential_reduce_fusion = f32[2,4,12,128]{3,2,1,0:T(8,128)S(1)} fusion(f32[2,4,12,128,1024]{4,3,2,1,0:T(8,128)} %get-tuple-element.113, f32[2,4,12,128]{3,2,1,0:T(8,128)S(1)} %get-tuple-element.112), kind=kLoop, calls=%fused_computation.3 | loop fusion | flops 37736448 | bytes 50429952 | tf_op jit(solution)/shard_map/reduce_sum | solution.py:247
  242.0 55.6 %all-gather.3.cloned.1.call-done = bf16[2,4,1024,768]{3,2,1,0:T(8,128)(2,1)} async-done(((bf16[2,4,128,768]{3,2,1,0:T(8,128)(2,1)}), bf16[2,4,1024,768]{3,2,1,0:T(8,128)(2,1)}) %all-gather.3.cloned.1.call-update) | async-done | bytes 12582928 | tf_op jit(solution)/shard_map/all_gather | solution.py:235
  314.2 21.8 %fusion.69 = bf16[2,4,12,64,128]{4,3,2,1,0:T(8,128)(2,1)S(1)} fusion(bf16[2,4,1024,12,64]{2,4,3,1,0:T(8,128)(2,1)} %bitcast.164, f32[2,4,12,128,1024]{4,3,2,1,0:T(8,128)} %get-tuple-element.113, f32[2,4,12,128]{3,2,1,0:T(8,128)} %log_add_fusion), kind=kOutput, calls=%fused_computation.161 | convolution fusion | flops 1649147904 | bytes 64536576 | tf_op jit(solution)/shard_map/lghqk,lgkhe->lgqhe/dot_general | solution.py:250
  370.4 43.5 %multiply_add_fusion = f32[2,8,64,3072]{3,2,1,0:T(8,128)} fusion(f32[2,10,64,3072]{3,2,1,0:T(8,128)} %maximum_convert_fusion, f32[3072]{0:T(1024)S(1)} %bitcast.204, f32[3072]{0:T(1024)S(1)} %bitcast.202, f32[3072]{0:T(1024)S(1)} %bitcast.200, f32[3072]{0:T(1024)S(1)} %bitcast.198, f32[3072]{0:T(1024)S(1)} %bitcast.196, f32[3072]{0:T(1024)S(1)} %bitcast.194, ...), kind=kLoop, calls=%fused_computation.56 | loop fusion | flops 56623104 | bytes 66183168 | tf_op jit(solution)/shard_map/add | solution.py:80
  449.3 43.2 %convert_reduce_fusion = (f32[3072]{0:T(1024)}, bf16[2,8,64,3072]{3,2,1,0:T(8,128)(2,1)}) fusion(f32[3072]{0:T(1024)S(1)} %bitcast.205, f32[2,10,64,3072]{3,2,1,0:T(8,128)} %maximum_convert_fusion.1, f32[3072]{0:T(1024)S(1)} %bitcast.203, f32[3072]{0:T(1024)S(1)} %bitcast.201, f32[3072]{0:T(1024)S(1)} %bitcast.199, f32[3072]{0:T(1024)S(1)} %bitcast.197, ...), kind=kLoop, calls=%fused_computation.54 | loop fusion | flops 62911488 | bytes 59891712 | tf_op jit(solution)/shard_map/reduce_sum | solution.py:296
  531.0 24.6 %convolution_convert_fusion = bf16[2,4,12,64,1024]{4,3,2,1,0:T(8,128)(2,1)} fusion(bf16[2,4,128,12,64]{2,4,3,1,0:T(8,128)(2,1)} %bitcast.172, f32[2,4,12,128,1024]{4,3,2,1,0:T(8,128)} %get-tuple-element.113, f32[2,4,12,128]{3,2,1,0:T(8,128)} %log_add_fusion), kind=kOutput, calls=%fused_computation.60 | convolution fusion | flops 1654652928 | bytes 64536576 | tf_op jit(solution)/shard_map/lghqk,lgqhe->lgkhe/dot_general | solution.py:331
  555.6 16.7 copy.108
  572.3 37.7 %multiply_reduce_fusion = (f32[2,4,12,128]{3,2,1,0:T(8,128)}, f32[2,4,12,128,1024]{4,3,2,1,0:T(8,128)}) fusion(f32[2,4,12,128,1024]{4,3,2,1,0:T(8,128)} %get-tuple-element.113, f32[2,4,12,128]{3,2,1,0:T(8,128)} %log_add_fusion, bf16[2,4,128,12,64]{2,4,3,1,0:T(8,128)(2,1)} %bitcast.173, bf16[2,4,1024,12,64]{2,4,3,1,0:T(8,128)(2,1)} %bitcast.165), kind=kOutput, calls=%fused_computation.1 | convolution fusion | flops 1660932096 | bytes 114917376 | tf_op jit(solution)/shard_map/lgqhe,lgkhe->lghqk/dot_general | solution.py:322
  610.0 41.4 %multiply_convert_fusion = bf16[2,4,12,128,1024]{4,3,2,1,0:T(8,128)(2,1)} fusion(f32[2,4,12,128,1024]{4,3,2,1,0:T(8,128)} %get-tuple-element.116, f32[2,4,12,128,1024]{4,3,2,1,0:T(8,128)} %get-tuple-element.113, f32[2,4,12,128]{3,2,1,0:T(8,128)} %get-tuple-element.115, f32[2,4,12,128]{3,2,1,0:T(8,128)} %log_add_fusion), kind=kLoop, calls=%fused_computation | loop fusion | flops 62914560 | bytes 125927424 | tf_op jit(solution)/shard_map/convert_element_type | solution.py:329
  683.8 17.9 convert_reduce_fusion.5
  704.3 45.2 %multiply_reduce_fusion.2 = (f32[3072]{0:T(1024)S(1)}, f32[3072]{0:T(1024)}, f32[3072]{0:T(1024)}, f32[3072]{0:T(1024)}, f32[3072]{0:T(1024)}, /*index=5*/f32[30...) fusion(f32[2,10,64,3072]{3,2,1,0:T(8,128)} %maximum_convert_fusion, ...), kind=kLoop, calls=%fused_computation.45 | loop fusion | flops 59738112 | bytes 66183168 | tf_op jit(solution)/shard_map/reduce_sum | solution.py:108
  749.4 89.3 %reduce-scatter.15.cloned.1.call-done = bf16[2,4,128,768]{3,2,1,0:T(8,128)(2,1)} async-done(((bf16[2,4,1024,768]{3,2,1,0:T(8,128)(2,1)}), bf16[2,4,128,768]{3,2,1,0:T(8,128)(2,1)}) %reduce-scatter.15.cloned.1.call-update) | async-done | bytes 1572880 | tf_op jit(solution)/shard_map/reduce_scatter | solution.py:358
  980.3 118.4 %all-reduce.18.cloned.1.call-done = (f32[768]{0:T(1024)}, f32[768]{0:T(1024)}, f32[4608]{0:T(1024)}, f32[768,9]{0,1:T(8,128)}, f32[768]{0:T(1024)}, /*index=5*/f...) async-done(((f32[768]{0:T(1024)}, f32[768]{0:T(1024)}, f32[4608]{0:T(1024)}, f32[768,9]{0,1:T(8,128)}, ...) | async-done | bytes 92176
  1112.8 90.9 %reduce-scatter.29.cloned.1.call-done = f32[24,768]{1,0:T(8,128)} async-done(((f32[768,768]{1,0:T(8,128)}), f32[24,768]{1,0:T(8,128)}) %reduce-scatter.29.cloned.1.call-update) | async-done | bytes 73744 | tf_op jit(solution)/shard_map/reduce_scatter | solution.py:157
  1203.7 141.0 %reduce-scatter.33.cloned.1.call-done = f32[96,768]{1,0:T(8,128)} async-done(((f32[3072,768]{1,0:T(8,128)}), f32[96,768]{1,0:T(8,128)}) %reduce-scatter.33.cloned.1.call-update) | async-done | bytes 294928 | tf_op jit(solution)/shard_map/reduce_scatter | solution.py:163
  1344.7 142.3 %reduce-scatter.31.cloned.1.call-done = f32[24,3072]{1,0:T(8,128)} async-done(((f32[768,3072]{1,0:T(8,128)}), f32[24,3072]{1,0:T(8,128)}) %reduce-scatter.31.cloned.1.call-update) | async-done | bytes 294928 | tf_op jit(solution)/shard_map/reduce_scatter | solution.py:159
  1486.9 100.0 %reduce-scatter.19.cloned.1.call-done = f32[8,768]{1,0:T(8,128)} async-done(((f32[256,768]{1,0:T(8,128)}), f32[8,768]{1,0:T(8,128)}) %reduce-scatter.19.cloned.1.call-update) | async-done | bytes 24592 | tf_op jit(solution)/shard_map/reduce_scatter | solution.py:145
  1586.9 104.0 %reduce-scatter.21.cloned.1.call-done = f32[24,768]{1,0:T(8,128)} async-done(((f32[768,768]{1,0:T(8,128)}), f32[24,768]{1,0:T(8,128)}) %reduce-scatter.21.cloned.1.call-update) | async-done | bytes 73744 | tf_op jit(solution)/shard_map/reduce_scatter | solution.py:147
  1690.9 107.3 %reduce-scatter.23.cloned.1.call-done = f32[24,1001]{1,0:T(8,128)} async-done(((f32[768,1001]{1,0:T(8,128)}), f32[24,1001]{1,0:T(8,128)}) %reduce-scatter.23.cloned.1.call-update) | async-done | bytes 96112 | tf_op jit(solution)/shard_map/reduce_scatter | solution.py:149
  1798.2 125.4 %reduce-scatter.27.cloned.1.call-done = f32[24,2304]{1,0:T(8,128)} async-done(((f32[768,2304]{1,0:T(8,128)}), f32[24,2304]{1,0:T(8,128)}) %reduce-scatter.27.cloned.1.call-update) | async-done | bytes 221200 | tf_op jit(solution)/shard_map/reduce_scatter | solution.py:154
  1923.5 168.5 %reduce-scatter.25.cloned.1.call-done = f32[24,4608]{1,0:T(8,128)} async-done(((f32[768,4608]{1,0:T(8,128)}), f32[24,4608]{1,0:T(8,128)}) %reduce-scatter.25.cloned.1.call-update) | async-done | bytes 442384 | tf_op jit(solution)/shard_map/reduce_scatter | solution.py:150
  (333 shorter events, 377.8 us)
Async XLA Ops:
  7.2 173.2 %all-gather.5.cloned.1.call-start = ((), (), s32[]{:S(2)}) async-start(), calls=%async_computation.12 | async-start | bytes 14155776 | tf_op jit(solution)/shard_map/all_gather | solution.py:234
  28.8 3.9 collective-permute-start
  31.2 5.5 collective-permute-start.1
  59.5 238.1 %all-gather.3.cloned.1.call-start = ((), (), s32[]{:S(2)}) async-start(), calls=%async_computation.11 | async-start | bytes 14155776 | tf_op jit(solution)/shard_map/all_gather | solution.py:235
  65.0 684.4 %reduce-scatter.17.cloned.1.call-start = ((), (), s32[]{:S(2)}) async-start(), calls=%async_computation.14 | async-start | bytes 14155776 | tf_op jit(solution)/shard_map/reduce_scatter | solution.py:361
  351.5 152.2 %copy-start.4 = (f32[2,8,64,768]{3,2,1,0:T(8,128)}, f32[2,8,64,768]{3,2,1,0:T(8,128)S(1)}, u32[]{:S(2)}) copy-start(f32[2,8,64,768]{3,2,1,0:T(8,128)S(1)} %get-tuple-element.82) | copy-start | bytes 9437188
  351.6 150.8 %copy-start.31 = (f32[2,8,64]{2,1,0:T(8,128)}, f32[2,8,64]{2,1,0:T(8,128)S(1)}, u32[]{:S(2)}) copy-start(f32[2,8,64]{2,1,0:T(8,128)S(1)} %broadcast_multiply_fusion) | copy-start | bytes 12292
  358.2 4.1 collective-permute-start.2
  360.5 4.2 collective-permute-start.3
  428.2 12.9 collective-permute-start.4
  439.2 4.2 collective-permute-start.5
  572.3 266.5 %reduce-scatter.15.cloned.1.call-start = ((), (), s32[]{:S(2)}) async-start(), calls=%async_computation.13 | async-start | bytes 14155776 | tf_op jit(solution)/shard_map/reduce_scatter | solution.py:358
  683.7 289.0 %reduce-scatter.35.cloned.1.call-start = ((), (), s32[]{:S(2)}) async-start(), calls=%async_computation.23 | async-start | bytes 1622016
  854.4 15.9 collective-permute-start.6
  856.4 13.9 collective-permute-start.7
  867.3 231.3 %all-reduce.18.cloned.1.call-start = ((), (), s32[]{:S(2)}) async-start(), calls=%async_computation.24 | async-start | bytes 245760
  908.6 295.1 %reduce-scatter.29.cloned.1.call-start = ((), (), s32[]{:S(2)}) async-start(), calls=%async_computation.20 | async-start | bytes 2433024 | tf_op jit(solution)/shard_map/reduce_scatter | solution.py:157
  913.6 431.1 %reduce-scatter.33.cloned.1.call-start = ((), (), s32[]{:S(2)}) async-start(), calls=%async_computation.22 | async-start | bytes 9732096 | tf_op jit(solution)/shard_map/reduce_scatter | solution.py:163
  927.1 559.8 %reduce-scatter.31.cloned.1.call-start = ((), (), s32[]{:S(2)}) async-start(), calls=%async_computation.21 | async-start | bytes 9732096 | tf_op jit(solution)/shard_map/reduce_scatter | solution.py:159
  938.3 648.6 %reduce-scatter.19.cloned.1.call-start = ((), (), s32[]{:S(2)}) async-start(), calls=%async_computation.15 | async-start | bytes 811008 | tf_op jit(solution)/shard_map/reduce_scatter | solution.py:145
  940.8 750.0 %reduce-scatter.21.cloned.1.call-start = ((), (), s32[]{:S(2)}) async-start(), calls=%async_computation.16 | async-start | bytes 2433024 | tf_op jit(solution)/shard_map/reduce_scatter | solution.py:147
  945.1 853.1 %reduce-scatter.23.cloned.1.call-start = ((), (), s32[]{:S(2)}) async-start(), calls=%async_computation.17 | async-start | bytes 3244032 | tf_op jit(solution)/shard_map/reduce_scatter | solution.py:149
  948.9 974.6 %reduce-scatter.27.cloned.1.call-start = ((), (), s32[]{:S(2)}) async-start(), calls=%async_computation.19 | async-start | bytes 7299072 | tf_op jit(solution)/shard_map/reduce_scatter | solution.py:154
  958.0 1134.0 %reduce-scatter.25.cloned.1.call-start = ((), (), s32[]{:S(2)}) async-start(), calls=%async_computation.18 | async-start | bytes 14598144 | tf_op jit(solution)/shard_map/reduce_scatter | solution.py:150
  (78 other events, 817.7 us)
Sparse Core Ops, SparseCore 0:
  59.6 120.7 all-gather.4
  182.6 114.9 all-gather.2
  572.4 136.5 reduce-scatter.16
  711.2 127.5 reduce-scatter.14
  867.4 97.7 reduce-scatter.34
  971.5 127.1 all-reduce.17
  1105.4 98.2 reduce-scatter.28
  1210.1 134.4 reduce-scatter.32
  1352.1 134.7 reduce-scatter.30
  1492.4 94.4 reduce-scatter.18
  1592.8 98.0 reduce-scatter.20
  1697.6 100.5 reduce-scatter.22
  1805.4 118.1 reduce-scatter.26
  1930.0 161.9 reduce-scatter.24
where the time goes:
time: 2110 us; the launch traced here: 2100 us
  waiting for transfers between devices  1360 us (64%)
  matrix products  278 us (13%)
  other arithmetic  261 us (12%)
  local copies, waits for them, and re-layouts  158 us (7%)
  starting transfers between devices  24 us (1%)
    reduce_scatter x1, waiting for transfers between devices, sum_joint(): lax.psum_scatter(parts[5], ('items', 'strips'), scatter_dimension=0, tile...  168 us
    reduce_scatter x1, waiting for transfers between devices, sum_joint(): lax.psum_scatter(parts[14], ('items', 'strips'), scatter_dimension=0, til...  142 us
    reduce_scatter x1, waiting for transfers between devices, sum_joint(): lax.psum_scatter(parts[18], ('items', 'strips'), scatter_dimension=0, til...  141 us
    reduce_scatter x1, waiting for transfers between devices, sum_joint(): lax.psum_scatter(parts[9], ('items', 'strips'), scatter_dimension=0, tile...  125 us
    unnamed x16, waiting for transfers between devices  119 us
    all_gather x1, waiting for transfers between devices, per_device(): lax.all_gather(key, 'strips', axis=2, tiled=True)  110 us
    reduce_scatter x1, waiting for transfers between devices, sum_joint(): lax.psum_scatter(parts[4], ('items', 'strips'), scatter_dimension=0, tile...  107 us
    reduce_scatter x1, waiting for transfers between devices, sum_joint(): lax.psum_scatter(parts[2], ('items', 'strips'), scatter_dimension=0, tile...  104 us
  transfers between devices with their start and end apart: 22, of which 17 were waited for; matrix products, arithmetic and copies ran while one was open for 18% of the time, Pallas kernels for 0%

commit v1 on v0

v1 whole, which is shorter than its diff:
```python
from functools import partial
import math

import jax
import jax.numpy as jnp
from jax import lax
from jax.experimental import pallas as pl
from jax.experimental.pallas import tpu as pltpu
from jax.sharding import PartitionSpec as P

HEADS = 12
HEAD_DIM = 64
LANES = 128
COLUMN_PARTS = 4
CHUNKS = 2
VMEM_BYTES = 60 * 1024 * 1024

highest = lax.Precision.HIGHEST
epsilon = 1e-06
bfloat = jnp.bfloat16
single = jnp.float32
both = ("items", "strips")


def params():
    return pltpu.CompilerParams(vmem_limit_bytes=VMEM_BYTES)


def cost(flops, moved, exps=0):
    return pl.CostEstimate(flops=int(flops), bytes_accessed=int(moved), transcendentals=int(exps))


def dot(a, b):
    return lax.dot_general(a, b, (((1,), (0,)), ((), ())), preferred_element_type=single)


def dot_nt(a, b):
    return lax.dot_general(a, b, (((1,), (1,)), ((), ())), preferred_element_type=single)


def dot_tn(a, b):
    return lax.dot_general(a, b, (((0,), (0,)), ((), ())), preferred_element_type=single)


def column_order(columns, back):
    sub = columns // COLUMN_PARTS
    first = lax.broadcasted_iota(jnp.int32, (columns, columns), 0)
    second = lax.broadcasted_iota(jnp.int32, (columns, columns), 1)
    kept, column = (second, first) if back else (first, second)
    return (column == COLUMN_PARTS * (kept % sub) + kept // sub).astype(bfloat)


def norm_parts(value):
    center = value - jnp.mean(value, axis=-1, keepdims=True)
    inverse = lax.rsqrt(jnp.mean(center * center, axis=-1, keepdims=True) + epsilon)
    return center * inverse, inverse


def norm_back(normed, inverse, grad):
    return inverse * (
        grad
        - jnp.mean(grad, axis=-1, keepdims=True)
        - normed * jnp.mean(grad * normed, axis=-1, keepdims=True)
    )


def put_wide(ref, row, cells):
    sub = cells.shape[1]
    place = lax.broadcasted_iota(jnp.int32, cells.shape[1:], 0)
    ref[row, 1 : COLUMN_PARTS + 1] = cells
    ref[row, 0] = jnp.where(place == 0, 0.0, pltpu.roll(cells[COLUMN_PARTS - 1], 1, 0))
    ref[row, COLUMN_PARTS + 1] = jnp.where(
        place == sub - 1, 0.0, pltpu.roll(cells[0], sub - 1, 0)
    )


def conv_row(ref, row, taps, start):
    total = start
    for i in range(3):
        for j in range(3):
            total = total + taps[3 * i + j] * ref[row + i, j : j + COLUMN_PARTS]
    return total


def conv_back_row(ref, row, taps):
    total = None
    for i in range(3):
        for j in range(3):
            term = taps[3 * i + j] * ref[row + 2 - i, 2 - j : 2 - j + COLUMN_PARTS]
            total = term if total is None else total + term
    return total


def front_kernel(
    edge_ref, x_ref, top_ref, bottom_ref, scale_ref, shift_ref, taps_ref, bias_ref,
    grouped_ref, normed_ref, kept_ref, wide,
):
    rows, columns, features = x_ref.shape[1:]
    sub = columns // COLUMN_PARTS
    order = column_order(columns, False)
    scale = 1.0 + scale_ref[0]
    shift = shift_ref[0]

    def fill(row, raw, keep):
        cells = dot(order, raw)
        normed = (norm_parts(cells)[0] * scale + shift) * keep
        low = normed.astype(bfloat)
        normed_ref[0, row] = low
        put_wide(wide, row, low.astype(single).reshape(COLUMN_PARTS, sub, features))
        return cells

    fill(0, top_ref[0, 0], edge_ref[0])
    fill(rows + 1, bottom_ref[0, 0], edge_ref[1])

    @pl.loop(0, rows)
    def _(row):
        kept_ref[0, row] = fill(row + 1, x_ref[0, row], 1.0).astype(bfloat)

    taps = [taps_ref[t : t + 1] for t in range(9)]
    bias = bias_ref[...]

    @pl.loop(0, rows // 2)
    def _(pair):
        for a in range(2):
            for lane in range(0, features, LANES):
                at = pl.ds(lane, LANES)
                total = jnp.zeros((COLUMN_PARTS, sub, LANES), single) + bias[:, lane : lane + LANES]
                for i in range(3):
                    for j in range(3):
                        total = total + taps[3 * i + j][:, lane : lane + LANES] * wide[
                            pair * 2 + a + i, j : j + COLUMN_PARTS, :, at
                        ]
                low = total.astype(bfloat)
                for j in range(COLUMN_PARTS):
                    grouped_ref[
                        0, 2 * a + j % 2, pl.ds(pl.multiple_of((pair * 2 + j // 2) * sub, sub), sub), at
                    ] = low[j]


def front(edge, latents, top, bottom, scale, shift, taps, bias):
    count, rows, columns, features = latents.shape
    quarter = rows * columns // 4
    sub = columns // COLUMN_PARTS
    image = lambda r: pl.BlockSpec((1, r, columns, features), lambda l: (l, 0, 0, 0))
    vector = pl.BlockSpec((1, 1, features), lambda l: (l, 0, 0))
    return pl.pallas_call(
        front_kernel,
        grid=(count,),
        in_specs=[
            pl.BlockSpec(memory_space=pltpu.SMEM),
            image(rows), image(1), image(1), vector, vector,
            pl.BlockSpec((16, features), lambda l: (0, 0)),
            pl.BlockSpec((1, features), lambda l: (0, 0)),
        ],
        out_specs=[
            pl.BlockSpec((1, 4, quarter, features), lambda l: (l, 0, 0, 0)),
            image(rows + 2), image(rows),
        ],
        out_shape=[
            jax.ShapeDtypeStruct((count, 4, quarter, features), bfloat),
            jax.ShapeDtypeStruct((count, rows + 2, columns, features), bfloat),
            jax.ShapeDtypeStruct((count, rows, columns, features), bfloat),
        ],
        scratch_shapes=[pltpu.VMEM((rows + 2, COLUMN_PARTS + 2, sub, features), single)],
        compiler_params=params(),
        cost_estimate=cost(count * rows * columns * features * 150, count * rows * columns * features * 8),
        name="front",
    )(edge, latents, top, bottom, scale, shift, taps, bias)


def upstream_kernel(g_ref, top_ref, bottom_ref, gate_ref, kept_ref, branch_ref, bias_ref):
    rows, columns, features = g_ref.shape[1:]
    order = column_order(columns, False)
    gate = gate_ref[0]

    def low(raw):
        cells = dot(order, raw)
        return cells, (cells * gate).astype(bfloat)

    branch_ref[0, 0] = low(top_ref[0, 0])[1]
    branch_ref[0, rows + 1] = low(bottom_ref[0, 0])[1]

    def step(row, total):
        cells, grad = low(g_ref[0, row])
        kept_ref[0, row] = cells.astype(bfloat)
        branch_ref[0, row + 1] = grad
        return total + jnp.sum(grad.astype(single), axis=0, keepdims=True)

    bias_ref[0] = lax.fori_loop(0, rows, step, jnp.zeros((1, features), single))


def upstream_parts(cotangent, top, bottom, gate):
    count, rows, columns, features = cotangent.shape
    image = lambda r: pl.BlockSpec((1, r, columns, features), lambda l: (l, 0, 0, 0))
    vector = pl.BlockSpec((1, 1, features), lambda l: (l, 0, 0))
    return pl.pallas_call(
        upstream_kernel,
        grid=(count,),
        in_specs=[image(rows), image(1), image(1), vector],
        out_specs=[image(rows), image(rows + 2), vector],
        out_shape=[
            jax.ShapeDtypeStruct((count, rows, columns, features), bfloat),
            jax.ShapeDtypeStruct((count, rows + 2, columns, features), bfloat),
            jax.ShapeDtypeStruct((count, 1, features), single),
        ],
        compiler_params=params(),
        cost_estimate=cost(count * rows * columns * features * 130, count * rows * columns * features * 6),
        name="upstream",
    )(cotangent, top, bottom, gate)


QUERY_STEP = 256


def attend_kernel(
    x_ref, wq_ref, wk_ref, wv_ref, bq_ref, bv_ref, q_ref, k_ref, v_ref, mixed_ref, log_ref
):
    tokens = x_ref.shape[0]
    base = math.log2(math.e) / math.sqrt(HEAD_DIM)
    x = x_ref[...]
    q_ref[...] = (dot(x, wq_ref[...]) + bq_ref[...]).astype(bfloat)
    k_ref[...] = dot(x, wk_ref[...]).astype(bfloat)
    v_ref[...] = (dot(x, wv_ref[...]) + bv_ref[...]).astype(bfloat)
    keys = k_ref[...]
    values = v_ref[...].T
    lane = lax.broadcasted_iota(jnp.int32, (QUERY_STEP, LANES), 1)
    for at in range(0, tokens, QUERY_STEP):
        part = q_ref[at : at + QUERY_STEP]
        outs = []
        for head in range(LANES // HEAD_DIM):
            own = jnp.where(lane // HEAD_DIM == head, part, jnp.zeros_like(part))
            scores = dot_nt(keys, own)
            peak = jnp.max(scores, axis=0, keepdims=True) * base
            soft = jnp.exp2(scores * base - peak)
            total = jnp.sum(soft, axis=0, keepdims=True)
            log_ref[0, head : head + 1, at : at + QUERY_STEP] = peak + jnp.log2(total)
            out = dot(values[head * HEAD_DIM : (head + 1) * HEAD_DIM], soft.astype(bfloat))
            outs.append(out * (1.0 / total))
        mixed_ref[at : at + QUERY_STEP] = jnp.concatenate(outs, axis=0).T.astype(bfloat)


def attend(x, wq, wk, wv, bq, bv):
    tokens, features = x.shape
    width = wq.shape[1]
    pairs = width // LANES
    weight = pl.BlockSpec((features, LANES), lambda h: (0, h))
    bias = pl.BlockSpec((1, LANES), lambda h: (0, h))
    column = pl.BlockSpec((tokens, LANES), lambda h: (0, h))
    lows = jax.ShapeDtypeStruct((tokens, width), bfloat)
    return pl.pallas_call(
        attend_kernel,
        grid=(pairs,),
        in_specs=[pl.BlockSpec((tokens, features), lambda h: (0, 0)), weight, weight, weight, bias, bias],
        out_specs=[column] * 4 + [pl.BlockSpec((1, 2, tokens), lambda h: (h, 0, 0))],
        out_shape=[lows] * 4 + [jax.ShapeDtypeStruct((pairs, 2, tokens), single)],
        compiler_params=params(),
        cost_estimate=cost(
            6 * tokens * features * width + 16 * tokens * tokens * width,
            2 * tokens * features + 8 * tokens * width + 6 * features * width,
            2 * pairs * tokens * tokens,
        ),
        name="attend",
    )(x, wq, wk, wv, bq, bv)


def attend_back_kernel(
    q_ref, k_ref, v_ref, mixed_ref, grad_ref, log_ref, dq_ref, dk_ref, dv_ref, dk_sum, dv_sum
):
    tokens = q_ref.shape[0]
    scale = 1.0 / math.sqrt(HEAD_DIM)
    base = math.log2(math.e) * scale
    keys = k_ref[...]
    values = v_ref[...]
    keys_turned = keys.T
    lane = lax.broadcasted_iota(jnp.int32, (QUERY_STEP, LANES), 1)
    for at in range(0, tokens, QUERY_STEP):
        rows = slice(at, at + QUERY_STEP)
        part = q_ref[rows]
        grad = grad_ref[rows]
        shares = (grad.astype(single) * mixed_ref[rows].astype(single)).T
        outs = []
        for head in range(LANES // HEAD_DIM):
            mine = lane // HEAD_DIM == head
            own = jnp.where(mine, part, jnp.zeros_like(part))
            own_grad = jnp.where(mine, grad, jnp.zeros_like(grad))
            share = jnp.sum(
                shares[head * HEAD_DIM : (head + 1) * HEAD_DIM], axis=0, keepdims=True
            )
            soft = jnp.exp2(dot_nt(keys, own) * base - log_ref[0, head : head + 1, rows])
            d_scores = (soft * (dot_nt(values, own_grad) - share)).astype(bfloat)
            dv_part = dot(soft.astype(bfloat), own_grad)
            dk_part = dot(d_scores, own)
            if at == 0 and head == 0:
                dv_sum[...] = dv_part
                dk_sum[...] = dk_part
            else:
                dv_sum[...] += dv_part
                dk_sum[...] += dk_part
            outs.append(dot(keys_turned[head * HEAD_DIM : (head + 1) * HEAD_DIM], d_scores))
        dq_ref[rows] = (jnp.concatenate(outs, axis=0) * scale).T.astype(bfloat)
    dk_ref[...] = (dk_sum[...] * scale).astype(bfloat)
    dv_ref[...] = dv_sum[...].astype(bfloat)


def attend_back(q, k, v, mixed, grad, logs):
    tokens, width = q.shape
    pairs = width // LANES
    column = pl.BlockSpec((tokens, LANES), lambda h: (0, h))
    lows = jax.ShapeDtypeStruct((tokens, width), bfloat)
    return pl.pallas_call(
        attend_back_kernel,
        grid=(pairs,),
        in_specs=[column] * 5 + [pl.BlockSpec((1, 2, tokens), lambda h: (h, 0, 0))],
        out_specs=[column] * 3,
        out_shape=[lows] * 3,
        scratch_shapes=[pltpu.VMEM((tokens, LANES), single)] * 2,
        compiler_params=params(),
        cost_estimate=cost(
            40 * tokens * tokens * width, 16 * tokens * width, 2 * pairs * tokens * tokens
        ),
        name="attend_back",
    )(q, k, v, mixed, grad, logs)


def middle_kernel(
    parts, *refs
):
    mixed_refs = refs[:parts]
    weight_ref, bias_ref, x_ref, gate_ref, scale_ref, shift_ref = refs[parts : parts + 6]
    attended_ref, middle_ref, normed_ref, grouped = refs[parts + 6 :]
    rows, columns, features = x_ref.shape[1:]
    sub = columns // COLUMN_PARTS
    quarter = rows * columns // 4
    total = bias_ref[...]
    at = 0
    for ref in mixed_refs:
        width = ref.shape[-1]
        total = total + dot(ref[0].reshape(4 * quarter, width), weight_ref[at : at + width])
        at += width
    grouped[...] = total.reshape(4, quarter, features)
    gate = gate_ref[0]
    scale = 1.0 + scale_ref[0]
    shift = shift_ref[0]

    @pl.loop(0, rows // 2)
    def _(pair):
        for a in range(2):
            row = pair * 2 + a
            cells = jnp.concatenate(
                [
                    grouped[2 * a + j % 2, pl.ds(pl.multiple_of((pair * 2 + j // 2) * sub, sub), sub)]
                    for j in range(COLUMN_PARTS)
                ],
                axis=0,
            )
            attended_ref[0, row] = cells
            middle = x_ref[0, row].astype(single) + gate * cells
            middle_ref[0, row] = middle
            normed_ref[0, row] = (norm_parts(middle)[0] * scale + shift).astype(bfloat)


def middle_part(mixed, weight, bias, kept, gate, scale, shift):
    count, rows, columns, features = kept.shape
    quarter = rows * columns // 4
    image = pl.BlockSpec((1, rows, columns, features), lambda l: (l, 0, 0, 0))
    vector = pl.BlockSpec((1, 1, features), lambda l: (l, 0, 0))
    return pl.pallas_call(
        partial(middle_kernel, len(mixed)),
        grid=(count,),
        in_specs=[
            pl.BlockSpec((1, 4, quarter, m.shape[-1]), lambda l: (l, 0, 0, 0)) for m in mixed
        ]
        + [
            pl.BlockSpec((features, features), lambda l: (0, 0)),
            pl.BlockSpec((1, features), lambda l: (0, 0)),
            image, vector, vector, vector,
        ],
        out_specs=[image] * 3,
        out_shape=[
            jax.ShapeDtypeStruct(kept.shape, single),
            jax.ShapeDtypeStruct(kept.shape, single),
            jax.ShapeDtypeStruct(kept.shape, bfloat),
        ],
        scratch_shapes=[pltpu.VMEM((4, quarter, features), single)],
        compiler_params=params(),
        cost_estimate=cost(2 * kept.size * features, 14 * kept.size),
        name="middle",
    )(*mixed, weight, bias, kept, gate, scale, shift)


def feed_kernel(
    edge_ref, nb_ref, top_ref, bottom_ref, db_ref, we_ref, be_ref, taps_ref, bm_ref, ws_ref,
    branch_ref, e_ref, gws_ref, gwe_ref, small_ref,
    nb_wide, nb_turned, db_own, hidden, d_act, act, d_hid, wide, d_wide,
):
    count, rows, columns, features = nb_ref.shape
    sub = columns // COLUMN_PARTS
    block = we_ref.shape[1]
    own = rows * columns
    tall = (rows + 4) * columns
    mid = (rows + 2) * columns
    first = pl.program_id(0) == 0

    @pl.when(first)
    def _():
        for l in range(count):
            nb_wide[l * tall : l * tall + 2 * columns] = top_ref[l].reshape(2 * columns, features)
            nb_wide[l * tall + 2 * columns : (l + 1) * tall - 2 * columns] = nb_ref[l].reshape(
                own, features
            )
            nb_wide[(l + 1) * tall - 2 * columns : (l + 1) * tall] = bottom_ref[l].reshape(
                2 * columns, features
            )
            nb_turned[:, l * own : (l + 1) * own] = nb_ref[l].reshape(own, features).T
            db_own[l * own : (l + 1) * own] = db_ref[l, 1 : rows + 1].reshape(own, features)
        branch_ref[...] = jnp.zeros_like(branch_ref)
        e_ref[...] = jnp.zeros_like(e_ref)

    hidden[...] = dot(nb_wide[...], we_ref[...]) + be_ref[...]
    d_act[...] = dot_nt(db_ref[...].reshape(count * mid, features), ws_ref[...])
    small_ref[...] = jnp.zeros_like(small_ref)

    c0 = math.sqrt(2.0 / math.pi)
    c1 = c0 * 0.044715

    @pl.loop(0, count * (block // LANES))
    def _(index):
        l = index // (block // LANES)
        at = pl.ds(pl.multiple_of((index % (block // LANES)) * LANES, LANES), LANES)
        taps = [taps_ref[t : t + 1, at] for t in range(9)]
        bias = bm_ref[:, at]
        for row in range(rows + 4):
            cells = hidden[pl.ds(pl.multiple_of(l * tall + row * columns, columns), columns), at]
            cells = cells.astype(bfloat).astype(single)
            if row < 2:
                cells = cells * edge_ref[0]
            if row >= rows + 2:
                cells = cells * edge_ref[1]
            put_wide(wide, row, cells.reshape(COLUMN_PARTS, sub, LANES))
        start = jnp.zeros((COLUMN_PARTS, sub, LANES), single) + bias
        for row in range(rows + 2):
            v = conv_row(wide, row, taps, start)
            cube = (v * v) * c1
            half = 0.5 * jnp.tanh(v * (cube + c0)) + 0.5
            gelu = v * half
            slope = half + gelu * (1.0 - half) * (6.0 * cube + 2.0 * c0)
            if 1 <= row <= rows:
                act[pl.ds(pl.multiple_of(l * own + (row - 1) * columns, columns), columns), at] = (
                    gelu.reshape(columns, LANES).astype(bfloat)
                )
            grad = d_act[pl.ds(pl.multiple_of(l * mid + row * columns, columns), columns), at]
            grad = (grad.reshape(COLUMN_PARTS, sub, LANES) * slope).astype(bfloat).astype(single)
            put_wide(d_wide, row, grad)
        sums = [jnp.zeros((sub, LANES), single) for _ in range(11)]
        for row in range(rows):
            d_in = conv_back_row(d_wide, row, taps).astype(bfloat)
            d_hid[pl.ds(pl.multiple_of(l * own + row * columns, columns), columns), at] = (
                d_in.reshape(columns, LANES)
            )
            center = d_wide[row + 1, 1 : COLUMN_PARTS + 1]
            for i in range(3):
                for j in range(3):
                    sums[3 * i + j] += jnp.sum(
                        center * wide[row + 1 + i, j : j + COLUMN_PARTS], axis=0
                    )
            sums[9] += jnp.sum(center, axis=0)
            sums[10] += jnp.sum(d_in.astype(single), axis=0)
        for t in range(11):
            small_ref[t : t + 1, at] += jnp.sum(sums[t], axis=0, keepdims=True)

    branch_ref[...] += dot(act[...], ws_ref[...])
    e_ref[...] += dot_nt(d_hid[...], we_ref[...])
    gws_ref[...] = dot_tn(act[...], db_own[...]).astype(bfloat)
    gwe_ref[0] = dot(nb_turned[...], d_hid[...]).astype(bfloat)


def feed_forward(edge, nb, top, bottom, db, we, be, taps, bm, ws):
    count, rows, columns, features = nb.shape
    hidden = we.shape[1]
    block = features
    steps = hidden // block
    tokens = count * rows * columns
    tall = count * (rows + 4) * columns
    mid = count * (rows + 2) * columns
    sub = columns // COLUMN_PARTS
    whole = lambda a: pl.BlockSpec(a.shape, lambda s: (0,) * a.ndim)
    return pl.pallas_call(
        feed_kernel,
        grid=(steps,),
        in_specs=[
            pl.BlockSpec(memory_space=pltpu.SMEM),
            whole(nb), whole(top), whole(bottom), whole(db),
            pl.BlockSpec((features, block), lambda s: (0, s)),
            pl.BlockSpec((1, block), lambda s: (0, s)),
            pl.BlockSpec((16, block), lambda s: (0, s)),
            pl.BlockSpec((1, block), lambda s: (0, s)),
            pl.BlockSpec((block, features), lambda s: (s, 0)),
        ],
        out_specs=[
            pl.BlockSpec((tokens, features), lambda s: (0, 0)),
            pl.BlockSpec((tokens, features), lambda s: (0, 0)),
            pl.BlockSpec((block, features), lambda s: (s, 0)),
            pl.BlockSpec((1, features, block), lambda s: (s, 0, 0)),
            pl.BlockSpec((16, block), lambda s: (0, s)),
        ],
        out_shape=[
            jax.ShapeDtypeStruct((tokens, features), single),
            jax.ShapeDtypeStruct((tokens, features), single),
            jax.ShapeDtypeStruct((hidden, features), bfloat),
            jax.ShapeDtypeStruct((steps, features, block), bfloat),
            jax.ShapeDtypeStruct((16, hidden), single),
        ],
        scratch_shapes=[
            pltpu.VMEM((tall, features), bfloat),
            pltpu.VMEM((features, tokens), bfloat),
            pltpu.VMEM((tokens, features), bfloat),
            pltpu.VMEM((tall, block), single),
            pltpu.VMEM((mid, block), single),
            pltpu.VMEM((tokens, block), bfloat),
            pltpu.VMEM((tokens, block), bfloat),
            pltpu.VMEM((rows + 4, COLUMN_PARTS + 2, sub, LANES), single),
            pltpu.VMEM((rows + 2, COLUMN_PARTS + 2, sub, LANES), single),
        ],
        compiler_params=params(),
        cost_estimate=cost(
            2 * features * hidden * (tall + mid + 4 * tokens),
            8 * tokens * features + 8 * features * hidden,
            mid * hidden,
        ),
        name="feed_forward",
    )(edge, nb, top, bottom, db, we, be, taps, bm, ws)


def turn_kernel(parts, *refs):
    (
        branch_ref, e_ref, middle_ref, attended_ref, g_ref,
        gate_b_ref, scale_ref, gate_a_ref, bias_ref, weight_ref,
    ) = refs[:10]
    mixed_refs = refs[10 : 10 + parts]
    result_ref, d_middle_ref = refs[10 + parts : 12 + parts]
    d_mixed_refs = refs[12 + parts : 12 + 2 * parts]
    gw_ref, sums_ref, gw_sum, grouped = refs[12 + 2 * parts :]
    rows, columns, features = g_ref.shape[1:]
    sub = columns // COLUMN_PARTS
    quarter = rows * columns // 4
    back = column_order(columns, True)
    gate_b = gate_b_ref[0]
    scale = 1.0 + scale_ref[0]
    gate_a = gate_a_ref[0]

    def step(pair, sums):
        for a in range(2):
            row = pair * 2 + a
            at = pl.ds(pl.multiple_of(row * columns, columns), columns)
            branch = branch_ref[at] + bias_ref[...]
            middle = middle_ref[0, row]
            g = g_ref[0, row].astype(single)
            result = (middle + gate_b * branch).astype(bfloat)
            result_ref[0, row] = dot(back, result).astype(bfloat)
            normed, inverse = norm_parts(middle)
            e = e_ref[at]
            d_middle = g + norm_back(normed, inverse, e * scale)
            d_middle_ref[0, row] = d_middle
            low = (d_middle * gate_a).astype(bfloat)
            for j in range(COLUMN_PARTS):
                grouped[
                    2 * a + j % 2, pl.ds(pl.multiple_of((pair * 2 + j // 2) * sub, sub), sub)
                ] = low[j * sub : (j + 1) * sub]
            terms = (g * branch, e, e * normed, d_middle * attended_ref[0, row], low.astype(single))
            sums = tuple(
                s + jnp.sum(t.reshape(columns // 8, 8, features), axis=0) for s, t in zip(sums, terms)
            )
        return sums

    sums = lax.fori_loop(
        0, rows // 2, step, tuple(jnp.zeros((8, features), single) for _ in range(5))
    )
    for t in range(5):
        sums_ref[0, t : t + 1] = jnp.sum(sums[t], axis=0, keepdims=True)
    sums_ref[0, 5:8] = jnp.zeros((3, features), single)
    grad = grouped[...].reshape(4 * quarter, features)
    at = 0
    for mixed_ref, d_ref in zip(mixed_refs, d_mixed_refs):
        width = mixed_ref.shape[-1]
        piece = slice(at, at + width)
        d_ref[0] = dot_nt(grad, weight_ref[piece]).astype(bfloat).reshape(4, quarter, width)
        part = dot_tn(mixed_ref[0].reshape(4 * quarter, width), grad)

        @pl.when(pl.program_id(0) == 0)
        def _():
            gw_sum[piece] = part

        @pl.when(pl.program_id(0) > 0)
        def _():
            gw_sum[piece] += part

        at += width

    @pl.when(pl.program_id(0) == pl.num_programs(0) - 1)
    def _():
        gw_ref[...] = gw_sum[...].astype(bfloat)


def turn(branch, e, middle, attended, g, gate_b, scale, gate_a, bias, weight, mixed):
    count, rows, columns, features = g.shape
    quarter = rows * columns // 4
    own = rows * columns
    image = pl.BlockSpec((1, rows, columns, features), lambda l: (l, 0, 0, 0))
    flat = pl.BlockSpec((own, features), lambda l: (l, 0))
    vector = pl.BlockSpec((1, 1, features), lambda l: (l, 0, 0))
    groups = [pl.BlockSpec((1, 4, quarter, m.shape[-1]), lambda l: (l, 0, 0, 0)) for m in mixed]
    square = pl.BlockSpec((features, features), lambda l: (0, 0))
    return pl.pallas_call(
        partial(turn_kernel, len(mixed)),
        grid=(count,),
        in_specs=[flat, flat, image, image, image, vector, vector, vector]
        + [pl.BlockSpec((1, features), lambda l: (0, 0)), square]
        + groups,
        out_specs=[image, image] + groups + [square, pl.BlockSpec((1, 8, features), lambda l: (l, 0, 0))],
        out_shape=[
            jax.ShapeDtypeStruct(g.shape, bfloat),
            jax.ShapeDtypeStruct(g.shape, single),
        ]
        + [jax.ShapeDtypeStruct(m.shape, bfloat) for m in mixed]
        + [
            jax.ShapeDtypeStruct((features, features), bfloat),
            jax.ShapeDtypeStruct((count, 8, features), single),
        ],
        scratch_shapes=[
            pltpu.VMEM((features, features), single),
            pltpu.VMEM((4, quarter, features), bfloat),
        ],
        compiler_params=params(),
        cost_estimate=cost(4 * g.size * features, 26 * g.size),
        name="turn",
    )(branch, e, middle, attended, g, gate_b, scale, gate_a, bias, weight, *mixed)


def final_kernel(
    d_ref, top_ref, bottom_ref, normed_ref, x_ref, d_middle_ref, scale_ref, taps_ref,
    out_ref, taps_out_ref, sums_ref, wide, d_wide,
):
    rows, columns, features = x_ref.shape[1:]
    sub = columns // COLUMN_PARTS
    back = column_order(columns, True)
    scale = 1.0 + scale_ref[0]

    def piece(ref, a, start):
        parts = [
            ref[0, 2 * a + j % 2, pl.ds(pl.multiple_of(start + (j // 2) * sub, sub), sub)]
            for j in range(COLUMN_PARTS)
        ]
        return jnp.stack(parts, axis=0).astype(single)

    def halo(ref):
        parts = [
            ref[0, j % 2, pl.ds((j // 2) * sub, sub)] for j in range(COLUMN_PARTS)
        ]
        return jnp.stack(parts, axis=0).astype(single)

    put_wide(d_wide, 0, halo(top_ref))
    put_wide(d_wide, rows + 1, halo(bottom_ref))

    @pl.loop(0, rows // 2)
    def _(pair):
        for a in range(2):
            put_wide(d_wide, pair * 2 + a + 1, piece(d_ref, a, pair * 2 * sub))

    @pl.loop(0, rows + 2)
    def _(row):
        put_wide(wide, row, normed_ref[0, row].astype(single).reshape(COLUMN_PARTS, sub, features))

    @pl.when(pl.program_id(0) == 0)
    def _():
        taps_out_ref[...] = jnp.zeros_like(taps_out_ref)

    d_normed = wide
    for lane in range(0, features, LANES):
        at = pl.ds(lane, LANES)
        taps = [taps_ref[t : t + 1, at] for t in range(9)]

        def step(row, sums):
            total = None
            center = d_wide[row + 1, 1 : COLUMN_PARTS + 1, :, at]
            sums = list(sums)
            for i in range(3):
                for j in range(3):
                    term = taps[3 * i + j] * d_wide[row + 2 - i, 2 - j : 2 - j + COLUMN_PARTS, :, at]
                    total = term if total is None else total + term
                    sums[3 * i + j] = sums[3 * i + j] + jnp.sum(
                        center * wide[row + i, j : j + COLUMN_PARTS, :, at], axis=0
                    )
            sums[9] = sums[9] + jnp.sum(center, axis=0)
            d_normed[row, 1 : COLUMN_PARTS + 1, :, at] = total
            return tuple(sums)

        sums = lax.fori_loop(
            0, rows, step, tuple(jnp.zeros((sub, LANES), single) for _ in range(10))
        )
        for t in range(10):
            taps_out_ref[t : t + 1, at] += jnp.sum(sums[t], axis=0, keepdims=True)

    def last(row, sums):
        cells = d_normed[row, 1 : COLUMN_PARTS + 1].reshape(columns, features)
        normed, inverse = norm_parts(x_ref[0, row].astype(single))
        grad = d_middle_ref[0, row] + norm_back(normed, inverse, cells * scale)
        out_ref[0, row] = dot(back, grad.astype(bfloat)).astype(bfloat)
        return tuple(
            s + jnp.sum(t.reshape(columns // 8, 8, features), axis=0)
            for s, t in zip(sums, (cells, cells * normed))
        )

    sums = lax.fori_loop(0, rows, last, tuple(jnp.zeros((8, features), single) for _ in range(2)))
    for t in range(2):
        sums_ref[0, t : t + 1] = jnp.sum(sums[t], axis=0, keepdims=True)
    sums_ref[0, 2:8] = jnp.zeros((6, features), single)


def final(d_reduced, top, bottom, normed, kept, d_middle, scale, taps):
    count, rows, columns, features = kept.shape
    quarter = rows * columns // 4
    sub = columns // COLUMN_PARTS
    image = lambda r: pl.BlockSpec((1, r, columns, features), lambda l: (l, 0, 0, 0))
    vector = pl.BlockSpec((1, 1, features), lambda l: (l, 0, 0))
    side = pl.BlockSpec((1, 2, 2 * sub, features), lambda l: (l, 0, 0, 0))
    return pl.pallas_call(
        final_kernel,
        grid=(count,),
        in_specs=[
            pl.BlockSpec((1, 4, quarter, features), lambda l: (l, 0, 0, 0)),
            side, side, image(rows + 2), image(rows), image(rows), vector,
            pl.BlockSpec((16, features), lambda l: (0, 0)),
        ],
        out_specs=[
            image(rows),
            pl.BlockSpec((16, features), lambda l: (0, 0)),
            pl.BlockSpec((1, 8, features), lambda l: (l, 0, 0)),
        ],
        out_shape=[
            jax.ShapeDtypeStruct(kept.shape, bfloat),
            jax.ShapeDtypeStruct((16, features), single),
            jax.ShapeDtypeStruct((count, 8, features), single),
        ],
        scratch_shapes=[pltpu.VMEM((rows + 2, COLUMN_PARTS + 2, sub, features), single)] * 2,
        compiler_params=params(),
        cost_estimate=cost(kept.size * 180, kept.size * 12),
        name="final",
    )(d_reduced, top, bottom, normed, kept, d_middle, scale, taps)


def from_above(tail):
    count = lax.axis_size("strips")
    return lax.ppermute(tail, "strips", [(i, i + 1) for i in range(count - 1)])


def from_below(head):
    count = lax.axis_size("strips")
    return lax.ppermute(head, "strips", [(i + 1, i) for i in range(count - 1)])


def time_features(timesteps, halves):
    frequency = jnp.exp(-math.log(10000.0) * jnp.arange(halves, dtype=jnp.float32) / halves)
    phase = timesteps.astype(jnp.float32)[:, None] * frequency[None, :]
    return jnp.concatenate([jnp.cos(phase), jnp.sin(phase)], axis=1)


def exact(a, b):
    return jnp.dot(a, b, precision=highest)


def exact_nt(a, b):
    return lax.dot_general(a, b, (((1,), (1,)), ((), ())), precision=highest)


def exact_tn(a, b):
    return lax.dot_general(a, b, (((0,), (0,)), ((), ())), precision=highest)


def silu_slope(value):
    gate = jax.nn.sigmoid(value)
    return gate * (1.0 + value * (1.0 - gate))


def tap_rows(kernel):
    return jnp.pad(kernel.astype(single).T, ((0, 7), (0, 0)))


def per_device(
    latents,
    timesteps,
    labels,
    time_in_weight,
    time_in_bias,
    time_out_weight,
    time_out_bias,
    label_table,
    ada_weight,
    ada_bias,
    down_kernel,
    down_bias,
    input_weight,
    query_bias,
    value_bias,
    output_weight,
    output_bias,
    expand_weight,
    expand_bias,
    mixer_kernel,
    mixer_bias,
    shrink_weight,
    shrink_bias,
    cotangent,
):
    count, rows, columns, features = latents.shape
    strips = lax.axis_size("strips")
    items = lax.axis_size("items")
    devices = strips * items
    strip = lax.axis_index("strips")
    item = lax.axis_index("items")
    me = item * strips + strip
    sub = columns // COLUMN_PARTS
    quarter = rows * columns // 4
    groups = count * 4
    share = strips // groups
    width = features // share
    row_vector = lambda v: v.astype(single).reshape(1, -1)
    edge = jnp.stack([strip > 0, strip < strips - 1]).astype(single)

    all_times = lax.all_gather(timesteps, "items", axis=0, tiled=True)
    all_labels = lax.all_gather(labels, "items", axis=0, tiled=True)
    time_in, time_out, table, ada = (
        w.astype(single) for w in (time_in_weight, time_out_weight, label_table, ada_weight)
    )
    sinus = time_features(all_times, time_in_weight.shape[0] // 2)
    before = exact(sinus, time_in) + time_in_bias.astype(single)
    inner = jax.nn.silu(before)
    onehot = (all_labels[:, None] == jnp.arange(table.shape[1], dtype=jnp.int32)[None, :]).astype(
        single
    )
    cond = exact(inner, time_out) + time_out_bias.astype(single) + exact_nt(onehot, table)
    active = jax.nn.silu(cond)
    own_active = lax.dynamic_slice_in_dim(active, item * count, count, axis=0)
    modulation = exact(own_active, ada) + ada_bias.astype(single)
    shift_a, scale_a, gate_a, shift_b, scale_b, gate_b = (
        modulation[:, None, i * features : (i + 1) * features] for i in range(6)
    )

    ends = jnp.concatenate([latents[:, -1:], cotangent[:, -1:]], axis=1)
    starts = jnp.concatenate([latents[:, :1], cotangent[:, :1]], axis=1)
    above = from_above(ends)
    below = from_below(starts)

    down_taps = tap_rows(down_kernel)
    grouped, normed_a, kept = front(
        edge, latents, above[:, :1], below[:, :1], scale_a, shift_a, down_taps, row_vector(down_bias)
    )

    def spread(array):
        flat = array.reshape(groups, quarter, array.shape[-1])
        if share > 1:
            flat = jnp.repeat(flat, share, axis=0)
        got = lax.all_to_all(flat, "strips", 0, 0, tiled=True)
        return got.reshape(strips * quarter, array.shape[-1])

    def collect(array):
        flat = array.reshape(strips, quarter, array.shape[-1])
        return lax.all_to_all(flat, "strips", 0, 0, tiled=True)

    group = spread(grouped)
    g_kept, d_branch, grad_shrink_bias = upstream_parts(
        cotangent, above[:, 1:], below[:, 1:], gate_b
    )

    head_at = (strip % share) * width
    def own_columns(array, axis):
        return array if share == 1 else lax.dynamic_slice_in_dim(array, head_at, width, axis=axis)

    wq, wk, wv = (
        own_columns(input_weight[:, i * features : (i + 1) * features], 1) for i in range(3)
    )
    bq = own_columns(row_vector(query_bias), 1)
    bv = own_columns(row_vector(value_bias), 1)
    piece = width // CHUNKS
    saved = []
    mixed = []
    for c in range(CHUNKS):
        at = slice(c * piece, (c + 1) * piece)
        saved.append(attend(group, wq[:, at], wk[:, at], wv[:, at], bq[:, at], bv[:, at]))
        mixed.append(collect(saved[c][3]))
    if share == 1:
        mixed = [m.reshape(count, 4, quarter, piece) for m in mixed]
    else:
        joined = jnp.concatenate(mixed, axis=-1).reshape(groups, share, quarter, width)
        joined = joined.transpose(0, 2, 1, 3).reshape(count, 4, quarter, features)
        mixed = [joined]

    attended, middle, normed_b = middle_part(
        mixed, output_weight, row_vector(output_bias), kept, gate_a, scale_b, shift_b
    )
    branch, e, grad_shrink, grad_expand, feed_small = feed_forward(
        edge,
        normed_b,
        from_above(normed_b[:, -2:]),
        from_below(normed_b[:, :2]),
        d_branch,
        expand_weight,
        row_vector(expand_bias),
        tap_rows(mixer_kernel),
        row_vector(mixer_bias),
        shrink_weight,
    )
    turned = turn(
        branch, e, middle, attended, g_kept, gate_b, scale_b, gate_a, row_vector(shrink_bias),
        output_weight, mixed,
    )
    result, d_middle = turned[:2]
    d_mixed = turned[2:-2]
    grad_output, turn_sums = turned[-2:]

    hidden = expand_weight.shape[1]
    steps = hidden // features
    early = jnp.concatenate(
        [
            grad_shrink.reshape(devices, hidden // devices, features),
            grad_expand.reshape(steps, devices, features // devices, features)
            .transpose(1, 0, 2, 3)
            .reshape(devices, hidden // devices, features),
            grad_output.reshape(devices, features // devices, features),
        ],
        axis=1,
    )
    early_sum = lax.psum_scatter(early, both, scatter_dimension=0, tiled=False).astype(single)

    if share == 1:
        d_mixed = [spread(d) for d in d_mixed]
    else:
        parts = d_mixed[0].reshape(groups, quarter, share, width).transpose(0, 2, 1, 3)
        got = lax.all_to_all(parts.reshape(strips, quarter, width), "strips", 0, 0, tiled=True)
        got = got.reshape(strips * quarter, width)
        d_mixed = [got[:, c * piece : (c + 1) * piece] for c in range(CHUNKS)]
    grads = []
    for c in range(CHUNKS):
        q, k, v, out, logs = saved[c]
        grads.append(attend_back(q, k, v, out, d_mixed[c], logs))
    d_query, d_key, d_value = (
        jnp.concatenate([grads[c][i] for c in range(CHUNKS)], axis=1) for i in range(3)
    )
    d_projected = jnp.concatenate([d_query, d_key, d_value], axis=1)
    own_weight = jnp.concatenate([wq, wk, wv], axis=1)
    d_group = dot_nt(d_projected, own_weight).astype(bfloat)
    d_reduced = collect(d_group)
    if share > 1:
        d_reduced = jnp.sum(
            d_reduced.reshape(groups, share, quarter, features).astype(single), axis=1
        ).astype(bfloat)
    d_reduced = d_reduced.reshape(count, 4, quarter, features)
    grad_input = dot_tn(group, d_projected).astype(bfloat)
    d_query_sum = jnp.sum(d_query.astype(single), axis=0)
    d_value_sum = jnp.sum(d_value.astype(single), axis=0)
    if share > 1:
        zero = jnp.zeros((features, 3, features), bfloat)
        grad_input = lax.dynamic_update_slice(
            zero, grad_input.reshape(features, 3, width), (0, 0, head_at)
        ).reshape(features, 3 * features)
        flat = jnp.zeros((features,), single)
        d_query_sum = lax.dynamic_update_slice(flat, d_query_sum, (head_at,))
        d_value_sum = lax.dynamic_update_slice(flat, d_value_sum, (head_at,))
    late_sum = lax.psum_scatter(grad_input, both, scatter_dimension=0, tiled=True).astype(single)

    grad_latents, down_small, final_sums = final(
        d_reduced,
        from_above(d_reduced[:, 2:, -2 * sub :]),
        from_below(d_reduced[:, :2, : 2 * sub]),
        normed_a,
        kept,
        d_middle,
        scale_a,
        down_taps,
    )

    d_gate_b, d_shift_b, d_scale_b, d_gate_a, output_bias_part = (
        turn_sums[:, t] for t in range(5)
    )
    narrow = jnp.stack(
        [
            jnp.sum(output_bias_part, axis=0),
            jnp.sum(grad_shrink_bias[:, 0], axis=0),
            d_query_sum,
            d_value_sum,
        ]
    )
    narrow = jnp.concatenate([narrow, down_small[:10]], axis=0)
    small = jnp.concatenate(
        [
            feed_small[:11].reshape(11, devices, hidden // devices).transpose(1, 0, 2).reshape(devices, -1),
            narrow.reshape(14, devices, features // devices).transpose(1, 0, 2).reshape(devices, -1),
        ],
        axis=1,
    )
    small = jnp.sum(lax.all_to_all(small, both, 0, 0, tiled=True), axis=0)
    cut = 11 * (hidden // devices)
    feed_sum = small[:cut].reshape(11, hidden // devices)
    narrow_sum = small[cut:].reshape(14, features // devices)

    d_modulation = jnp.concatenate(
        [final_sums[:, 0], final_sums[:, 1], d_gate_a, d_shift_b, d_scale_b, d_gate_b], axis=1
    )
    d_modulation = jnp.sum(lax.all_gather(d_modulation, "strips", axis=0), axis=0)
    d_modulation = lax.all_gather(d_modulation, "items", axis=0, tiled=True)
    d_cond = exact_nt(d_modulation, ada) * silu_slope(cond)
    d_before = exact_nt(d_cond, time_out) * silu_slope(before)

    def mine(array):
        size = array.shape[-1] // devices
        return lax.dynamic_slice_in_dim(array, me * size, size, axis=array.ndim - 1)

    feed_rows = hidden // devices
    return (
        result,
        grad_latents,
        exact_tn(mine(sinus), d_before),
        jnp.sum(mine(d_before), axis=0),
        exact_tn(mine(inner), d_cond),
        jnp.sum(mine(d_cond), axis=0),
        exact_tn(mine(d_cond), onehot),
        exact_tn(mine(active), d_modulation),
        jnp.sum(mine(d_modulation), axis=0),
        narrow_sum[4:13].T,
        narrow_sum[13],
        late_sum,
        narrow_sum[2],
        narrow_sum[3],
        early_sum[2 * feed_rows :],
        narrow_sum[0],
        early_sum[feed_rows : 2 * feed_rows]
        .reshape(steps, features // devices, features)
        .transpose(1, 0, 2)
        .reshape(features // devices, hidden),
        feed_sum[10],
        feed_sum[:9].T,
        feed_sum[9],
        early_sum[:feed_rows],
        narrow_sum[1],
    )


def solution(mesh):
    image = P("items", "strips", None, None)
    split = P(both, None)
    line = P(both)
    return jax.shard_map(
        per_device,
        mesh=mesh,
        in_specs=(image, P("items"), P("items")) + (P(),) * 20 + (image,),
        out_specs=(
            image, image, split, line, split, line, split, split, line, split, line,
            split, line, line, split, line, split, line, split, line, split, line,
        ),
        check_vma=False,
    )
```

time: 2110 us -> 649 us (0.31)
  waiting for transfers between devices: 1360 us -> 198 us
  other arithmetic: 261 us -> 20.4 us
  matrix products: 278 us -> 41.3 us
  Pallas kernels: 0 us -> 219 us
  local copies, waits for them, and re-layouts: 158 us -> 44.3 us
  blocking collectives: 0 us -> 60.4 us
    reduce_scatter x10 -> x2, waiting for transfers between devices: 1070 us -> 100 us  [the longest x1 100 us: per_device(): lax.psum_scatter(early, both, scatter_dimension=0, tiled=False)]
    dot_general x28 -> x12, matrix products: 278 us -> 41.3 us  [the longest x3 10.8 us: exact_nt(): return lax.dot_general(a, b, (((1,), (1,)), ((), ())), precision=highest)]
    pallas_call x0 -> x10, Pallas kernels: none -> 219 us  [the longest x1 78.6 us: feed_forward(): pl.pallas_call(feed_kernel, grid=(steps,), in_specs=[pl.BlockSpec(memory_...]
    all_gather x2 -> x0, waiting for transfers between devices: 166 us -> none  [the longest x1 110 us: per_device(): lax.all_gather(key, 'strips', axis=2, tiled=True)]
    reduce_sum x14 -> x9, other arithmetic: 138 us -> 5.22 us  [the longest x1 1.69 us: per_device(): d_value_sum = jnp.sum(d_value.astype(single), axis=0)]
    unnamed x16 -> x2, waiting for transfers between devices: 119 us -> 0.03 us
    all_to_all x0 -> x6, waiting for transfers between devices: none -> 95.7 us  [the longest x3 62 us: collect(): return lax.all_to_all(flat, 'strips', 0, 0, tiled=True)]
    convert_element_type x20 -> x6, other arithmetic: 76 us -> 5.9 us  [the longest x1 1.62 us: per_device(): lax.psum_scatter(grad_input, both, scatter_dimension=0, tiled=True)]
  transfers between devices with their start and end apart: 22 -> 14, of which waited for: 17 -> 6; matrix products, arithmetic and copies ran while one was open for 18% -> 12% of each run, Pallas kernels for 0% -> 10%
where the time goes in v1:
time: 649 us; the launch traced here: 640 us
  Pallas kernels  219 us (34%)
  waiting for transfers between devices  198 us (31%)
  blocking collectives  60.4 us (9%)
  local copies, waits for them, and re-layouts  44.3 us (7%)
  matrix products  41.3 us (6%)
  starting transfers between devices  41 us (6%)
  other arithmetic  20.4 us (3%)
  between operations  15.8 us (2%)
    reduce_scatter x1, waiting for transfers between devices, per_device(): lax.psum_scatter(early, both, scatter_dimension=0, tiled=False)  100 us
    pallas_call x1, Pallas kernels, feed_forward(): pl.pallas_call(feed_kernel, grid=(steps,), in_specs=[pl.BlockSpec(memory_...  78.6 us
    all_to_all x3, waiting for transfers between devices, collect(): return lax.all_to_all(flat, 'strips', 0, 0, tiled=True)  62 us
    pallas_call x2, Pallas kernels, attend(): pl.pallas_call(attend_kernel, grid=(pairs,), in_specs=[pl.BlockSpec((toke...  45.1 us
    pallas_call x2, Pallas kernels, attend_back(): pl.pallas_call(attend_back_kernel, grid=(pairs,), in_specs=[column] * 5 +...  36.2 us
    all_to_all x2, waiting for transfers between devices, spread(): got = lax.all_to_all(flat, 'strips', 0, 0, tiled=True)  33.8 us
    all_to_all x1, blocking collectives, spread(): got = lax.all_to_all(flat, 'strips', 0, 0, tiled=True)  26.3 us
    pallas_call x1, Pallas kernels, final(): pl.pallas_call(final_kernel, grid=(count,), in_specs=[pl.BlockSpec((1, 4,...  17.7 us
  transfers between devices with their start and end apart: 14, of which 6 were waited for; matrix products, arithmetic and copies ran while one was open for 12% of the time, Pallas kernels for 10%

profile of v1, /device:TPU:0, one launch (start us, length us, event | category | flops | bytes accessed | tf_op | source)
XLA Modules:
  0.0 639.7 jit_solution(11396627708856758972)
XLA Ops:
  18.2 9.3 %all-reduce.4 = (s32[8]{0:T(128)S(1)}, s32[8]{0:T(128)}) all-reduce(s32[8]{0:T(128)S(1)} %dynamic-update-slice, s32[8]{0:T(128)S(1)} %dynamic-update-slice.1), channel_id=1, replica_groups=mesh['items'=4,'strips'=8] {'items'}, use_global_device_ids=true, to_apply=%add.2 | all-reduce | flops 16 | bytes 128
  34.4 5.9 convolution_add_fusion
  44.9 11.9 %front.1 = (bf16[2,4,128,768]{3,2,1,0:T(8,128)(2,1)}, bf16[2,10,64,768]{3,2,1,0:T(8,128)(2,1)}, bf16[2,8,64,768]{3,2,1,0:T(8,128)(2,1)}) custom-call(f32[2]{0:T(128)} %add_convert_fusion.edge_ref, bf16[2,8,64,768]{3,2,1,0:T(8,128)(2,1)} %x_ref.1, bf16[2,1,64,768]{3,2,1,0:T(8,128)(2,1)} %get-tuple-element.119.top_ref, ...), custom_call_target="tpu_custom_call" | custom-call | flops 117964800 | bytes 6291456 | tf_op jit(solution)/shard_map/front/pallas_call | solution.py:146
  66.1 33.4 %all-to-all-done = bf16[8,128,768]{2,1,0:T(8,128)(2,1)S(1)} async-done(((bf16[8,128,768]{2,1,0:T(8,128)(2,1)}), bf16[8,128,768]{2,1,0:T(8,128)(2,1)S(1)}, u32[]{:S(2)}, u32[]{:S(2)}) %all-to-all-start) | async-done | bytes 1572896 | tf_op jit(solution)/shard_map/all_to_all | solution.py:862
  100.6 22.5 %attend.3 = (bf16[1024,384]{1,0:T(8,128)(2,1)}, bf16[1024,384]{1,0:T(8,128)(2,1)}, bf16[1024,384]{1,0:T(8,128)(2,1)}, bf16[1024,384]{1,0:T(8,128)(2,1)}, f32[3,2,1024]{2,1,0:T(2,128)}) custom-call(bf16[1024,768]{1,0:T(8,128)(2,1)} %bitcast.104, bf16[768,384]{1,0:T(8,128)(2,1)} %get-tuple-element.104.wq_ref, bf16[768,384]{1,0:T(8,128)(2,1)} %get-tuple-element.103.wk_ref, ...), custom_call_target="tpu_custom_call" | custom-call | flops 8254390272 | bytes 6488064 | tf_op jit(solution)/shard_map/attend/pallas_call | solution.py:250
  127.2 22.5 %attend.2 = (bf16[1024,384]{1,0:T(8,128)(2,1)}, bf16[1024,384]{1,0:T(8,128)(2,1)}, bf16[1024,384]{1,0:T(8,128)(2,1)}, bf16[1024,384]{1,0:T(8,128)(2,1)}, f32[3,2,1024]{2,1,0:T(2,128)}) custom-call(bf16[1024,768]{1,0:T(8,128)(2,1)} %bitcast.105, bf16[768,384]{1,0:T(8,128)(2,1)} %get-tuple-element.107.wq_ref, bf16[768,384]{1,0:T(8,128)(2,1)} %get-tuple-element.106.wk_ref, ...), custom_call_target="tpu_custom_call" | custom-call | flops 8254390272 | bytes 6488064 | tf_op jit(solution)/shard_map/attend/pallas_call | solution.py:250
  149.8 5.2 all-to-all-start.1
  157.4 18.6 %all-to-all-done.1 = bf16[8,128,384]{2,1,0:T(8,128)(2,1)S(1)} async-done(((bf16[8,128,384]{2,1,0:T(8,128)(2,1)}), bf16[8,128,384]{2,1,0:T(8,128)(2,1)S(1)}, u32[]{:S(2)}, u32[]{:S(2)}) %all-to-all-start.1) | async-done | bytes 786464 | tf_op jit(solution)/shard_map/all_to_all | solution.py:867
  176.8 8.0 %middle.1 = (f32[2,8,64,768]{3,2,1,0:T(8,128)}, f32[2,8,64,768]{3,2,1,0:T(8,128)}, bf16[2,8,64,768]{3,2,1,0:T(8,128)(2,1)}) custom-call(bf16[2,4,128,384]{3,2,1,0:T(8,128)(2,1)} %bitcast.102, bf16[2,4,128,384]{3,2,1,0:T(8,128)(2,1)} %bitcast.100, bf16[768,768]{1,0:T(8,128)(2,1)} %refs_9_.1, f32[1,768]{1,0:T(1,128)} %reshape.242.refs_3_, ...), custom_call_target="tpu_custom_call" | custom-call | flops 1207959552 | bytes 11010048 | tf_op jit(solution)/shard_map/middle/pallas_call | solution.py:367
  192.1 5.6 upstream.1
  198.7 78.6 %feed_forward.1 = (f32[1024,768]{1,0:T(8,128)}, f32[1024,768]{1,0:T(8,128)}, bf16[3072,768]{1,0:T(8,128)(2,1)}, bf16[4,768,768]{2,1,0:T(8,128)(2,1)}, f32[16,3072]{1,0:T(8,128)}) custom-call(f32[2]{0:T(128)} %add_convert_fusion.edge_ref, bf16[2,8,64,768]{3,2,1,0:T(8,128)(2,1)} %get-tuple-element.65.nb_ref, bf16[2,2,64,768]{3,2,1,0:T(8,128)(2,1)} %copy-done.33, ...), custom_call_target="tpu_custom_call" | custom-call | flops 32614907904 | bytes 25165824 | tf_op jit(solution)/shard_map/feed_forward/pallas_call | solution.py:487
  277.2 15.6 %turn.1 = (bf16[2,8,64,768]{3,2,1,0:T(8,128)(2,1)}, f32[2,8,64,768]{3,2,1,0:T(8,128)}, bf16[2,4,128,384]{3,2,1,0:T(8,128)(2,1)}, bf16[2,4,128,384]{3,2,1,0:T(8,1...) custom-call(f32[1024,768]{1,0:T(8,128)} %get-tuple-element.67.refs_0_, f32[1024,768]{1,0:T(8,128)} %get-tuple-element.68.refs_1_, ...), custom_call_target="tpu_custom_call" | custom-call | flops 2415919104 | bytes 20447232 | tf_op jit(solution)/shard_map/turn/pallas_call | solution.py:613
  292.9 26.3 %all_to_all.39 = bf16[8,128,384]{2,1,0:T(8,128)(2,1)} all-to-all(bf16[8,128,384]{2,1,0:T(8,128)(2,1)} %bitcast.116), channel_id=1, replica_groups=mesh['items'=4,'strips'=8] {'strips'}, dimensions={0} | all-to-all | bytes 1572864 | tf_op jit(solution)/shard_map/all_to_all | solution.py:862
  323.0 18.1 %attend_back.2 = (bf16[1024,384]{1,0:T(8,128)(2,1)}, bf16[1024,384]{1,0:T(8,128)(2,1)}, bf16[1024,384]{1,0:T(8,128)(2,1)}) custom-call(bf16[1024,384]{1,0:T(8,128)(2,1)} %get-tuple-element.73.q_ref, bf16[1024,384]{1,0:T(8,128)(2,1)} %get-tuple-element.74.k_ref, bf16[1024,384]{1,0:T(8,128)(2,1)} %get-tuple-element.75.v_ref, ...), custom_call_target="tpu_custom_call" | custom-call | flops 16106127360 | bytes 6291456 | tf_op jit(solution)/shard_map/attend_back/pallas_call | solution.py:310
  344.6 18.1 %attend_back.3 = (bf16[1024,384]{1,0:T(8,128)(2,1)}, bf16[1024,384]{1,0:T(8,128)(2,1)}, bf16[1024,384]{1,0:T(8,128)(2,1)}) custom-call(bf16[1024,384]{1,0:T(8,128)(2,1)} %get-tuple-element.79.q_ref, bf16[1024,384]{1,0:T(8,128)(2,1)} %get-tuple-element.80.k_ref, bf16[1024,384]{1,0:T(8,128)(2,1)} %get-tuple-element.81.v_ref, ...), custom_call_target="tpu_custom_call" | custom-call | flops 16106127360 | bytes 6291456 | tf_op jit(solution)/shard_map/attend_back/pallas_call | solution.py:310
  369.2 7.9 %convolution_convert_fusion = bf16[768,2304]{1,0:T(8,128)(2,1)} fusion(bf16[1024,768]{1,0:T(8,128)(2,1)S(1)} %bitcast.106, bf16[1024,2304]{1,0:T(8,128)(2,1)} %constant_dynamic-update-slice_fusion), kind=kOutput, calls=%fused_computation.2 | convolution fusion | flops 3625648128 | bytes 9830400 | tf_op jit(solution)/shard_map/dot_general | solution.py:42
  386.4 8.6 %convolution_convert_fusion.1 = bf16[1024,768]{1,0:T(8,128)(2,1)} fusion(bf16[1024,2304]{1,0:T(8,128)(2,1)} %constant_dynamic-update-slice_fusion, bf16[768,2304]{1,0:T(8,128)(2,1)} %param.36), kind=kOutput, calls=%fused_computation.5 | convolution fusion | flops 3624665088 | bytes 9830400 | tf_op jit(solution)/shard_map/dot_general | solution.py:38
  403.7 43.4 %all-to-all-done.5 = bf16[8,128,768]{2,1,0:T(8,128)(2,1)S(1)} async-done(((bf16[8,128,768]{2,1,0:T(8,128)(2,1)}), bf16[8,128,768]{2,1,0:T(8,128)(2,1)S(1)}, u32[]{:S(2)}, u32[]{:S(2)}) %all-to-all-start.5) | async-done | bytes 1572896 | tf_op jit(solution)/shard_map/all_to_all | solution.py:867
  452.6 17.7 %final.1 = (bf16[2,8,64,768]{3,2,1,0:T(8,128)(2,1)}, f32[16,768]{1,0:T(8,128)}, f32[2,8,768]{2,1,0:T(8,128)}) custom-call(bf16[2,4,128,768]{3,2,1,0:T(8,128)(2,1)} %bitcast.95, bf16[2,2,32,768]{3,2,1,0:T(8,128)(2,1)} %copy-done.17, bf16[2,2,32,768]{3,2,1,0:T(8,128)(2,1)} %copy-done.18, bf16[2,10,64,768]{3,2,1,0:T(8,128)(2,1)} %get-tuple-element.89.normed_ref, ...), custom_call_target="tpu_custom_call" | custom-call | flops 141557760 | bytes 9437184 | tf_op jit(solution)/shard_map/final/pallas_call | solution.py:726
  474.1 8.1 %all-to-all-start.6 = ((f32[32,1,1392]{2,1,0:T(1,128)}), f32[32,1,1392]{2,1,0:T(1,128)S(1)}, u32[]{:S(2)}, u32[]{:S(2)}) async-start(f32[32,1,1392]{2,1,0:T(1,128)} %copy.93), calls=%async_computation.6 | async-start | bytes 360448 | tf_op jit(solution)/shard_map/all_to_all | solution.py:1000
  482.3 16.2 %all-gather.1 = f32[8,2,4608]{2,1,0:T(2,128)S(1)} all-gather(f32[1,2,4608]{2,1,0:T(2,128)S(1)} %bitcast.123), channel_id=2, replica_groups=mesh['items'=4,'strips'=8] {'strips'}, dimensions={0}, use_global_device_ids=true | all-gather | bytes 331776 | tf_op jit(solution)/shard_map/all_gather | solution.py:1008
  498.6 8.6 %all-gather.2 = f32[4,2,4608]{2,1,0:T(2,128)S(1)} all-gather(f32[1,2,4608]{2,1,0:T(2,128)S(1)} %bitcast.121), channel_id=1, replica_groups=mesh['items'=4,'strips'=8] {'items'}, dimensions={0}, use_global_device_ids=true | all-gather | bytes 184320 | tf_op jit(solution)/shard_map/all_gather | solution.py:1009
  507.3 8.1 %convolution_multiply_fusion.1 = f32[8,768]{1,0:T(8,128)S(1)} fusion(f32[8,4608]{1,0:T(8,128)S(1)} %reshape.259, bf16[768,4608]{1,0:T(8,128)(2,1)} %param.32, f32[8,768]{1,0:T(8,128)S(1)} %copy-done.19), kind=kOutput, calls=%fused_computation.8 | convolution fusion | flops 339787776 | bytes 7274496 | tf_op jit(solution)/shard_map/dot_general | solution.py:772
  528.3 100.1 %reduce-scatter.5.cloned.1.call-done = bf16[1,216,768]{2,1,0:T(8,128)(2,1)} async-done(((bf16[32,216,768]{2,1,0:T(8,128)(2,1)}), bf16[1,216,768]{2,1,0:T(8,128)(2,1)}) %reduce-scatter.5.cloned.1.call-update) | async-done | bytes 331792 | tf_op jit(solution)/shard_map/reduce_scatter | solution.py:932
  (200 shorter events, 105.6 us)
Async XLA Ops:
  7.2 25.6 %copy-start = (bf16[768,1001]{0,1:T(8,128)(2,1)S(1)}, bf16[768,1001]{0,1:T(8,128)(2,1)}, u32[]{:S(2)}) copy-start(bf16[768,1001]{0,1:T(8,128)(2,1)} %param.31) | copy-start | bytes 4612612
  7.2 25.0 %copy-start.3 = (bf16[768,768]{1,0:T(8,128)(2,1)S(1)}, bf16[768,768]{1,0:T(8,128)(2,1)}, u32[]{:S(2)}) copy-start(bf16[768,768]{1,0:T(8,128)(2,1)} %param.29) | copy-start | bytes 3538948
  9.4 33.9 %collective-permute-start.1 = (bf16[2,2,64,768]{3,2,1,0:T(8,128)(2,1)}, bf16[2,2,64,768]{3,2,1,0:T(8,128)(2,1)S(1)}, u32[]{:S(2)}, u32[]{:S(2)}) collective-permute-start(bf16[2,2,64,768]{3,2,1,0:T(8,128)(2,1)} %pad_maximum_fusion.2), channel_id=1, source_target_pairs={{1,0},{2,1},{3,2},{4,3},{5,4},{6,5},{7,6},{9,8},{10,9},{11,10},{12... | collective-permute-start | bytes 1179656 | tf_op jit(solution)/shard_map/ppermute | solution.py:758
  11.5 32.6 %collective-permute-start = (bf16[2,2,64,768]{3,2,1,0:T(8,128)(2,1)}, bf16[2,2,64,768]{3,2,1,0:T(8,128)(2,1)S(1)}, u32[]{:S(2)}, u32[]{:S(2)}) collective-permute-start(bf16[2,2,64,768]{3,2,1,0:T(8,128)(2,1)} %pad_maximum_fusion.1), channel_id=1, source_target_pairs={{0,1},{1,2},{2,3},{3,4},{4,5},{5,6},{6,7},{8,9},{9,10},{10,11},{11... | collective-permute-start | bytes 1179656 | tf_op jit(solution)/shard_map/ppermute | solution.py:753
  56.7 42.7 %all-to-all-start = ((bf16[8,128,768]{2,1,0:T(8,128)(2,1)}), bf16[8,128,768]{2,1,0:T(8,128)(2,1)S(1)}, u32[]{:S(2)}, u32[]{:S(2)}) async-start(bf16[8,128,768]{2,1,0:T(8,128)(2,1)} %bitcast.108), calls=%async_computation | async-start | bytes 3145728 | tf_op jit(solution)/shard_map/all_to_all | solution.py:862
  123.1 26.6 %all-to-all-start.2 = ((bf16[8,128,384]{2,1,0:T(8,128)(2,1)}), bf16[8,128,384]{2,1,0:T(8,128)(2,1)S(1)}, u32[]{:S(2)}, u32[]{:S(2)}) async-start(bf16[8,128,384]{2,1,0:T(8,128)(2,1)} %bitcast.112), calls=%async_computation.2 | async-start | bytes 1572864 | tf_op jit(solution)/shard_map/all_to_all | solution.py:867
  127.1 29.6 %copy-start.31 = (bf16[768]{0:T(1024)(128)(2,1)S(1)}, bf16[768]{0:T(1024)(128)(2,1)}, u32[]{:S(2)}) copy-start(bf16[768]{0:T(1024)(128)(2,1)} %param.40) | copy-start | bytes 4612
  149.7 26.3 %copy-start.5 = (bf16[8,128,384]{2,1,0:T(8,128)(2,1)}, bf16[8,128,384]{2,1,0:T(8,128)(2,1)S(1)}, u32[]{:S(2)}) copy-start(bf16[8,128,384]{2,1,0:T(8,128)(2,1)S(1)} %all-to-all-done.2) | copy-start | bytes 2359300
  149.7 39.9 %copy-start.24 = (bf16[3072]{0:T(1024)(128)(2,1)S(1)}, bf16[3072]{0:T(1024)(128)(2,1)}, u32[]{:S(2)}) copy-start(bf16[3072]{0:T(1024)(128)(2,1)} %param.42) | copy-start | bytes 18436
  149.7 40.5 %copy-start.25 = (bf16[3072]{0:T(1024)(128)(2,1)S(1)}, bf16[3072]{0:T(1024)(128)(2,1)}, u32[]{:S(2)}) copy-start(bf16[3072]{0:T(1024)(128)(2,1)} %param.44) | copy-start | bytes 18436
  149.7 41.1 %copy-start.32 = (bf16[768]{0:T(1024)(128)(2,1)S(1)}, bf16[768]{0:T(1024)(128)(2,1)}, u32[]{:S(2)}) copy-start(bf16[768]{0:T(1024)(128)(2,1)} %param.46) | copy-start | bytes 4612
  149.8 41.7 %copy-start.20 = (bf16[3072,9]{0,1:T(8,128)(2,1)S(1)}, bf16[3072,9]{0,1:T(8,128)(2,1)}, u32[]{:S(2)}) copy-start(bf16[3072,9]{0,1:T(8,128)(2,1)} %param.43) | copy-start | bytes 165892
  149.8 26.2 %all-to-all-start.1 = ((bf16[8,128,384]{2,1,0:T(8,128)(2,1)}), bf16[8,128,384]{2,1,0:T(8,128)(2,1)S(1)}, u32[]{:S(2)}, u32[]{:S(2)}) async-start(bf16[8,128,384]{2,1,0:T(8,128)(2,1)} %bitcast.113), calls=%async_computation.1 | async-start | bytes 1572864 | tf_op jit(solution)/shard_map/all_to_all | solution.py:867
  186.0 11.8 %collective-permute-start.2 = (bf16[2,2,64,768]{3,2,1,0:T(8,128)(2,1)S(1)}, bf16[2,2,64,768]{3,2,1,0:T(8,128)(2,1)S(1)}, u32[]{:S(2)}, u32[]{:S(2)}) collective-permute-start(bf16[2,2,64,768]{3,2,1,0:T(8,128)(2,1)S(1)} %get-tuple-element.111), channel_id=1, source_target_pairs={{0,1},{1,2},{2,3},{3,4},{4,5},{5,6},{6,7},{8,9},{9,10},{10,11},{11... | collective-permute-start | bytes 1179656 | tf_op jit(solution)/shard_map/ppermute | solution.py:753
  187.6 10.2 %collective-permute-start.3 = (bf16[2,2,64,768]{3,2,1,0:T(8,128)(2,1)S(1)}, bf16[2,2,64,768]{3,2,1,0:T(8,128)(2,1)S(1)}, u32[]{:S(2)}, u32[]{:S(2)}) collective-permute-start(bf16[2,2,64,768]{3,2,1,0:T(8,128)(2,1)S(1)} %get-tuple-element.110), channel_id=1, source_target_pairs={{1,0},{2,1},{3,2},{4,3},{5,4},{6,5},{7,6},{9,8},{10,9},{11,10},{12... | collective-permute-start | bytes 1179656 | tf_op jit(solution)/shard_map/ppermute | solution.py:758
  319.2 24.5 %all-to-all-start.4 = ((bf16[8,128,384]{2,1,0:T(8,128)(2,1)}), bf16[8,128,384]{2,1,0:T(8,128)(2,1)S(1)}, u32[]{:S(2)}, u32[]{:S(2)}) async-start(bf16[8,128,384]{2,1,0:T(8,128)(2,1)} %bitcast.114), calls=%async_computation.4 | async-start | bytes 1572864 | tf_op jit(solution)/shard_map/all_to_all | solution.py:862
  322.8 203.9 %reduce-scatter.3.cloned.1.call-start = ((), (), s32[]{:S(2)}) async-start(), calls=%async_computation.9 | async-start | bytes 3649536 | tf_op jit(solution)/shard_map/reduce_scatter | solution.py:968
  377.2 251.2 %reduce-scatter.5.cloned.1.call-start = ((), (), s32[]{:S(2)}) async-start(), calls=%async_computation.10 | async-start | bytes 10948608 | tf_op jit(solution)/shard_map/reduce_scatter | solution.py:932
  395.0 52.0 %all-to-all-start.5 = ((bf16[8,128,768]{2,1,0:T(8,128)(2,1)}), bf16[8,128,768]{2,1,0:T(8,128)(2,1)S(1)}, u32[]{:S(2)}, u32[]{:S(2)}) async-start(bf16[8,128,768]{2,1,0:T(8,128)(2,1)} %bitcast.107), calls=%async_computation.5 | async-start | bytes 3145728 | tf_op jit(solution)/shard_map/all_to_all | solution.py:867
  447.1 2.9 collective-permute-start.4
  448.6 3.3 collective-permute-start.5
  470.3 37.0 %copy-start.19 = (f32[8,768]{1,0:T(8,128)S(1)}, f32[8,768]{1,0:T(8,128)}, u32[]{:S(2)}) copy-start(f32[8,768]{1,0:T(8,128)} %get-tuple-element.140) | copy-start | bytes 73732
  474.1 49.9 %all-to-all-start.6 = ((f32[32,1,1392]{2,1,0:T(1,128)}), f32[32,1,1392]{2,1,0:T(1,128)S(1)}, u32[]{:S(2)}, u32[]{:S(2)}) async-start(f32[32,1,1392]{2,1,0:T(1,128)} %copy.93), calls=%async_computation.6 | async-start | bytes 360448 | tf_op jit(solution)/shard_map/all_to_all | solution.py:1000
  507.3 125.1 %copy-start.1 = (bf16[768,1001]{0,1:T(8,128)(2,1)S(1)}, bf16[768,1001]{0,1:T(8,128)(2,1)}, u32[]{:S(2)}) copy-start(bf16[768,1001]{0,1:T(8,128)(2,1)} %param.31) | copy-start | bytes 4612612
  (27 other events, 193.9 us)
Sparse Core Ops, SparseCore 0:
  377.3 104.1 reduce-scatter.2
  487.5 140.8 reduce-scatter.4

commit v2 on v1

--- a/solution.py
+++ b/solution.py
@@ -209,7 +209,8 @@
     )(cotangent, top, bottom, gate)
 
 
-QUERY_STEP = 256
+QUERY_STEP = 512
+QUERY_STEP_BACK = 256
 
 
 def attend_kernel(
@@ -239,18 +240,20 @@
         mixed_ref[at : at + QUERY_STEP] = jnp.concatenate(outs, axis=0).T.astype(bfloat)
 
 
-def attend(x, wq, wk, wv, bq, bv):
+def attend(x, weights, biases, first, width):
     tokens, features = x.shape
-    width = wq.shape[1]
     pairs = width // LANES
-    weight = pl.BlockSpec((features, LANES), lambda h: (0, h))
-    bias = pl.BlockSpec((1, LANES), lambda h: (0, h))
+    start = first // LANES
+    stride = weights.shape[1] // 3 // LANES
+    weight = lambda i: pl.BlockSpec((features, LANES), lambda h: (0, i * stride + start + h))
+    bias = lambda i: pl.BlockSpec((1, LANES), lambda h: (0, i * stride + start + h))
     column = pl.BlockSpec((tokens, LANES), lambda h: (0, h))
     lows = jax.ShapeDtypeStruct((tokens, width), bfloat)
     return pl.pallas_call(
         attend_kernel,
         grid=(pairs,),
-        in_specs=[pl.BlockSpec((tokens, features), lambda h: (0, 0)), weight, weight, weight, bias, bias],
+        in_specs=[pl.BlockSpec((tokens, features), lambda h: (0, 0))]
+        + [weight(0), weight(1), weight(2), bias(0), bias(1)],
         out_specs=[column] * 4 + [pl.BlockSpec((1, 2, tokens), lambda h: (h, 0, 0))],
         out_shape=[lows] * 4 + [jax.ShapeDtypeStruct((pairs, 2, tokens), single)],
         compiler_params=params(),
@@ -260,7 +263,7 @@
             2 * pairs * tokens * tokens,
         ),
         name="attend",
-    )(x, wq, wk, wv, bq, bv)
+    )(x, weights, weights, weights, biases, biases)
 
 
 def attend_back_kernel(
@@ -272,9 +275,9 @@
     keys = k_ref[...]
     values = v_ref[...]
     keys_turned = keys.T
-    lane = lax.broadcasted_iota(jnp.int32, (QUERY_STEP, LANES), 1)
-    for at in range(0, tokens, QUERY_STEP):
-        rows = slice(at, at + QUERY_STEP)
+    lane = lax.broadcasted_iota(jnp.int32, (QUERY_STEP_BACK, LANES), 1)
+    for at in range(0, tokens, QUERY_STEP_BACK):
+        rows = slice(at, at + QUERY_STEP_BACK)
         part = q_ref[rows]
         grad = grad_ref[rows]
         shares = (grad.astype(single) * mixed_ref[rows].astype(single)).T
@@ -322,6 +325,87 @@
     )(q, k, v, mixed, grad, logs)
 
 
+def regroup_kernel(*refs):
+    parts, weight_ref, out_ref = refs[:-2], refs[-2], refs[-1]
+    count = len(parts) // 3
+    piece = parts[0].shape[1]
+    third = weight_ref.shape[1] // 3
+    total = None
+    for c in range(count):
+        for i in range(3):
+            at = i * third + c * piece
+            term = dot_nt(parts[3 * c + i][...], weight_ref[:, at : at + piece])
+            total = term if total is None else total + term
+    out_ref[...] = total.astype(bfloat)
+
+
+def regroup(parts, weight):
+    tokens, piece = parts[0].shape
+    features = weight.shape[0]
+    step = min(256, tokens)
+    return pl.pallas_call(
+        regroup_kernel,
+        grid=(tokens // step,),
+        in_specs=[pl.BlockSpec((step, piece), lambda t: (t, 0))] * len(parts)
+        + [pl.BlockSpec(weight.shape, lambda t: (0, 0))],
+        out_specs=pl.BlockSpec((step, features), lambda t: (t, 0)),
+        out_shape=jax.ShapeDtypeStruct((tokens, features), bfloat),
+        compiler_params=params(),
+        cost_estimate=cost(2 * tokens * features * weight.shape[1], 2 * tokens * features * 4),
+        name="regroup",
+    )(*parts, weight)
+
+
+def input_grad_kernel(*refs):
+    x_ref, other_ref = refs[0], refs[1]
+    parts = refs[2:-2]
+    out_ref, sums_ref = refs[-2:]
+    count = len(parts) // 3
+    tokens, piece = parts[0].shape
+    third = count * piece
+    turned = x_ref[...].T
+    for c in range(count):
+        for i in range(3):
+            at = i * third + c * piece
+            out_ref[:, at : at + piece] = dot(turned, parts[3 * c + i][...]).astype(bfloat)
+    out_ref[:, 3 * third :] = other_ref[...]
+
+    @pl.when(pl.program_id(0) == 0)
+    def _():
+        ones = jnp.ones((16, tokens), bfloat)
+        for c in range(count):
+            for i in (0, 2):
+                total = dot(ones, parts[3 * c + i][...])
+                sums_ref[:, i // 2 * third + c * piece : i // 2 * third + (c + 1) * piece] = total[:8]
+
+
+def input_grad(x, other, parts):
+    tokens, features = x.shape
+    piece = parts[0].shape[1]
+    third = piece * len(parts) // 3
+    step = 256
+    return pl.pallas_call(
+        input_grad_kernel,
+        grid=(features // step,),
+        in_specs=[
+            pl.BlockSpec((tokens, step), lambda t: (0, t)),
+            pl.BlockSpec((step, other.shape[1]), lambda t: (t, 0)),
+        ]
+        + [pl.BlockSpec((tokens, piece), lambda t: (0, 0))] * len(parts),
+        out_specs=[
+            pl.BlockSpec((step, 3 * third + other.shape[1]), lambda t: (t, 0)),
+            pl.BlockSpec((8, 2 * third), lambda t: (0, 0)),
+        ],
+        out_shape=[
+            jax.ShapeDtypeStruct((features, 3 * third + other.shape[1]), bfloat),
+            jax.ShapeDtypeStruct((8, 2 * third), single),
+        ],
+        compiler_params=params(),
+        cost_estimate=cost(6 * tokens * features * third, 2 * tokens * features * 5),
+        name="input_grad",
+    )(x, other, *parts)
+
+
 def middle_kernel(
     parts, *refs
 ):
@@ -388,10 +472,33 @@
     )(*mixed, weight, bias, kept, gate, scale, shift)
 
 
+def feed_upstream_kernel(db_ref, ws_ref, out_ref):
+    out_ref[...] = dot_nt(db_ref[...], ws_ref[...]).astype(bfloat)
+
+
+def feed_upstream(db, ws):
+    count, tall, columns, features = db.shape
+    hidden = ws.shape[0]
+    lines = count * tall * columns
+    return pl.pallas_call(
+        feed_upstream_kernel,
+        grid=(hidden // features,),
+        in_specs=[
+            pl.BlockSpec((lines, features), lambda s: (0, 0)),
+            pl.BlockSpec((features, features), lambda s: (s, 0)),
+        ],
+        out_specs=pl.BlockSpec((lines, features), lambda s: (0, s)),
+        out_shape=jax.ShapeDtypeStruct((lines, hidden), bfloat),
+        compiler_params=params(),
+        cost_estimate=cost(2 * lines * features * hidden, 2 * lines * (features + hidden)),
+        name="feed_upstream",
+    )(db.reshape(lines, features), ws)
+
+
 def feed_kernel(
-    edge_ref, nb_ref, top_ref, bottom_ref, db_ref, we_ref, be_ref, taps_ref, bm_ref, ws_ref,
-    branch_ref, e_ref, gws_ref, gwe_ref, small_ref,
-    nb_wide, nb_turned, db_own, hidden, d_act, act, d_hid, wide, d_wide,
+    edge_ref, nb_ref, top_ref, bottom_ref, d_act_ref, we_ref, be_ref, ws_ref, taps_ref, bm_ref,
+    branch_ref, e_ref, act_ref, d_hid_ref, small_ref,
+    nb_wide, hidden, wide, d_wide,
 ):
     count, rows, columns, features = nb_ref.shape
     sub = columns // COLUMN_PARTS
@@ -399,9 +506,8 @@
     own = rows * columns
     tall = (rows + 4) * columns
     mid = (rows + 2) * columns
-    first = pl.program_id(0) == 0
-
-    @pl.when(first)
+
+    @pl.when(pl.program_id(0) == 0)
     def _():
         for l in range(count):
             nb_wide[l * tall : l * tall + 2 * columns] = top_ref[l].reshape(2 * columns, features)
@@ -411,13 +517,10 @@
             nb_wide[(l + 1) * tall - 2 * columns : (l + 1) * tall] = bottom_ref[l].reshape(
                 2 * columns, features
             )
-            nb_turned[:, l * own : (l + 1) * own] = nb_ref[l].reshape(own, features).T
-            db_own[l * own : (l + 1) * own] = db_ref[l, 1 : rows + 1].reshape(own, features)
         branch_ref[...] = jnp.zeros_like(branch_ref)
         e_ref[...] = jnp.zeros_like(e_ref)
 
-    hidden[...] = dot(nb_wide[...], we_ref[...]) + be_ref[...]
-    d_act[...] = dot_nt(db_ref[...].reshape(count * mid, features), ws_ref[...])
+    hidden[...] = (dot(nb_wide[...], we_ref[...]) + be_ref[...]).astype(bfloat)
     small_ref[...] = jnp.zeros_like(small_ref)
 
     c0 = math.sqrt(2.0 / math.pi)
@@ -431,7 +534,7 @@
         bias = bm_ref[:, at]
         for row in range(rows + 4):
             cells = hidden[pl.ds(pl.multiple_of(l * tall + row * columns, columns), columns), at]
-            cells = cells.astype(bfloat).astype(single)
+            cells = cells.astype(single)
             if row < 2:
                 cells = cells * edge_ref[0]
             if row >= rows + 2:
@@ -445,16 +548,16 @@
             gelu = v * half
             slope = half + gelu * (1.0 - half) * (6.0 * cube + 2.0 * c0)
             if 1 <= row <= rows:
-                act[pl.ds(pl.multiple_of(l * own + (row - 1) * columns, columns), columns), at] = (
-                    gelu.reshape(columns, LANES).astype(bfloat)
-                )
-            grad = d_act[pl.ds(pl.multiple_of(l * mid + row * columns, columns), columns), at]
-            grad = (grad.reshape(COLUMN_PARTS, sub, LANES) * slope).astype(bfloat).astype(single)
-            put_wide(d_wide, row, grad)
+                act_ref[
+                    pl.ds(pl.multiple_of(l * own + (row - 1) * columns, columns), columns), at
+                ] = gelu.reshape(columns, LANES).astype(bfloat)
+            grad = d_act_ref[pl.ds(pl.multiple_of(l * mid + row * columns, columns), columns), at]
+            grad = grad.astype(single).reshape(COLUMN_PARTS, sub, LANES) * slope
+            put_wide(d_wide, row, grad.astype(bfloat).astype(single))
         sums = [jnp.zeros((sub, LANES), single) for _ in range(11)]
         for row in range(rows):
             d_in = conv_back_row(d_wide, row, taps).astype(bfloat)
-            d_hid[pl.ds(pl.multiple_of(l * own + row * columns, columns), columns), at] = (
+            d_hid_ref[pl.ds(pl.multiple_of(l * own + row * columns, columns), columns), at] = (
                 d_in.reshape(columns, LANES)
             )
             center = d_wide[row + 1, 1 : COLUMN_PARTS + 1]
@@ -468,13 +571,11 @@
         for t in range(11):
             small_ref[t : t + 1, at] += jnp.sum(sums[t], axis=0, keepdims=True)
 
-    branch_ref[...] += dot(act[...], ws_ref[...])
-    e_ref[...] += dot_nt(d_hid[...], we_ref[...])
-    gws_ref[...] = dot_tn(act[...], db_own[...]).astype(bfloat)
-    gwe_ref[0] = dot(nb_turned[...], d_hid[...]).astype(bfloat)
-
-
-def feed_forward(edge, nb, top, bottom, db, we, be, taps, bm, ws):
+    branch_ref[...] += dot(act_ref[...], ws_ref[...])
+    e_ref[...] += dot_nt(d_hid_ref[...], we_ref[...])
+
+
+def feed_forward(edge, nb, top, bottom, d_act, we, be, taps, bm, ws):
     count, rows, columns, features = nb.shape
     hidden = we.shape[1]
     block = features
@@ -484,51 +585,82 @@
     mid = count * (rows + 2) * columns
     sub = columns // COLUMN_PARTS
     whole = lambda a: pl.BlockSpec(a.shape, lambda s: (0,) * a.ndim)
+    column = lambda n: pl.BlockSpec((n, block), lambda s: (0, s))
+    flat = pl.BlockSpec((tokens, features), lambda s: (0, 0))
     return pl.pallas_call(
         feed_kernel,
         grid=(steps,),
         in_specs=[
             pl.BlockSpec(memory_space=pltpu.SMEM),
-            whole(nb), whole(top), whole(bottom), whole(db),
-            pl.BlockSpec((features, block), lambda s: (0, s)),
-            pl.BlockSpec((1, block), lambda s: (0, s)),
-            pl.BlockSpec((16, block), lambda s: (0, s)),
-            pl.BlockSpec((1, block), lambda s: (0, s)),
+            whole(nb), whole(top), whole(bottom),
+            column(mid), column(features), column(1),
             pl.BlockSpec((block, features), lambda s: (s, 0)),
-        ],
-        out_specs=[
-            pl.BlockSpec((tokens, features), lambda s: (0, 0)),
-            pl.BlockSpec((tokens, features), lambda s: (0, 0)),
-            pl.BlockSpec((block, features), lambda s: (s, 0)),
-            pl.BlockSpec((1, features, block), lambda s: (s, 0, 0)),
-            pl.BlockSpec((16, block), lambda s: (0, s)),
-        ],
+            column(16), column(1),
+        ],
+        out_specs=[flat, flat, column(tokens), column(tokens), column(16)],
         out_shape=[
             jax.ShapeDtypeStruct((tokens, features), single),
             jax.ShapeDtypeStruct((tokens, features), single),
-            jax.ShapeDtypeStruct((hidden, features), bfloat),
-            jax.ShapeDtypeStruct((steps, features, block), bfloat),
+            jax.ShapeDtypeStruct((tokens, hidden), bfloat),
+            jax.ShapeDtypeStruct((tokens, hidden), bfloat),
             jax.ShapeDtypeStruct((16, hidden), single),
         ],
         scratch_shapes=[
             pltpu.VMEM((tall, features), bfloat),
-            pltpu.VMEM((features, tokens), bfloat),
-            pltpu.VMEM((tokens, features), bfloat),
-            pltpu.VMEM((tall, block), single),
-            pltpu.VMEM((mid, block), single),
-            pltpu.VMEM((tokens, block), bfloat),
-            pltpu.VMEM((tokens, block), bfloat),
+            pltpu.VMEM((tall, block), bfloat),
             pltpu.VMEM((rows + 4, COLUMN_PARTS + 2, sub, LANES), single),
             pltpu.VMEM((rows + 2, COLUMN_PARTS + 2, sub, LANES), single),
         ],
         compiler_params=params(),
         cost_estimate=cost(
-            2 * features * hidden * (tall + mid + 4 * tokens),
-            8 * tokens * features + 8 * features * hidden,
+            2 * features * hidden * (tall + 2 * tokens),
+            8 * tokens * features + 8 * features * hidden + 6 * tokens * hidden,
             mid * hidden,
         ),
         name="feed_forward",
-    )(edge, nb, top, bottom, db, we, be, taps, bm, ws)
+    )(edge, nb, top, bottom, d_act, we, be, ws, taps, bm)
+
+
+def feed_grads_kernel(act_ref, d_hid_ref, nb_ref, db_ref, gws_ref, gwe_ref, db_own):
+    count, rows, columns, features = nb_ref.shape
+    own = rows * columns
+
+    @pl.when(pl.program_id(0) == 0)
+    def _():
+        for l in range(count):
+            db_own[l * own : (l + 1) * own] = db_ref[l, 1 : rows + 1].reshape(own, features)
+
+    gws_ref[...] = dot_tn(act_ref[...], db_own[...]).astype(bfloat)
+    gwe_ref[0] = dot_tn(nb_ref[...].reshape(count * own, features), d_hid_ref[...]).astype(bfloat)
+
+
+def feed_grads(act, d_hid, nb, db):
+    count, rows, columns, features = nb.shape
+    tokens, hidden = act.shape
+    block = features
+    steps = hidden // block
+    whole = lambda a: pl.BlockSpec(a.shape, lambda s: (0,) * a.ndim)
+    return pl.pallas_call(
+        feed_grads_kernel,
+        grid=(steps,),
+        in_specs=[
+            pl.BlockSpec((tokens, block), lambda s: (0, s)),
+            pl.BlockSpec((tokens, block), lambda s: (0, s)),
+            whole(nb), whole(db),
+        ],
+        out_specs=[
+            pl.BlockSpec((block, features), lambda s: (s, 0)),
+            pl.BlockSpec((1, features, block), lambda s: (s, 0, 0)),
+        ],
+        out_shape=[
+            jax.ShapeDtypeStruct((hidden, features), bfloat),
+            jax.ShapeDtypeStruct((steps, features, block), bfloat),
+        ],
+        scratch_shapes=[pltpu.VMEM((tokens, features), bfloat)],
+        compiler_params=params(),
+        cost_estimate=cost(4 * features * hidden * tokens, 8 * features * hidden + 4 * tokens * hidden),
+        name="feed_grads",
+    )(act, d_hid, nb, db)
 
 
 def turn_kernel(parts, *refs):
@@ -764,21 +896,224 @@
     return jnp.concatenate([jnp.cos(phase), jnp.sin(phase)], axis=1)
 
 
-def exact(a, b):
-    return jnp.dot(a, b, precision=highest)
-
-
-def exact_nt(a, b):
-    return lax.dot_general(a, b, (((1,), (1,)), ((), ())), precision=highest)
-
-
-def exact_tn(a, b):
-    return lax.dot_general(a, b, (((0,), (0,)), ((), ())), precision=highest)
+def thirds(value):
+    high = value.astype(bfloat)
+    rest = value - high.astype(single)
+    middle = rest.astype(bfloat)
+    low = (rest - middle.astype(single)).astype(bfloat)
+    return jnp.concatenate([high, middle, low], axis=0)
+
+
+def exact(value, weight, nt=False):
+    n = value.shape[0]
+    out = (dot_nt if nt else dot)(thirds(value), weight)
+    return out[:n] + out[n : 2 * n] + out[2 * n :]
+
+
+def silu(value):
+    return value * (1.0 / (1.0 + jnp.exp(-value)))
 
 
 def silu_slope(value):
-    gate = jax.nn.sigmoid(value)
+    gate = 1.0 / (1.0 + jnp.exp(-value))
     return gate * (1.0 + value * (1.0 - gate))
+
+
+def label_rows(labels, classes):
+    return (lax.broadcasted_iota(jnp.int32, (labels.shape[0], classes), 1) == labels).astype(bfloat)
+
+
+def condition(sinus, labels, wi_ref, bi_ref, wo_ref, bo_ref, table_ref):
+    before = exact(sinus, wi_ref[...]) + bi_ref[...]
+    inner = silu(before)
+    onehot = label_rows(labels, table_ref.shape[1])
+    cond = exact(inner, wo_ref[...]) + bo_ref[...] + dot_nt(onehot, table_ref[...])
+    return before, inner, cond
+
+
+def modulate_kernel(
+    sinus_ref, label_ref, wi_ref, bi_ref, wo_ref, bo_ref, table_ref, ada_ref, ab_ref, out_ref, active
+):
+    @pl.when(pl.program_id(0) == 0)
+    def _():
+        cond = condition(
+            sinus_ref[...], label_ref[...], wi_ref, bi_ref, wo_ref, bo_ref, table_ref
+        )[2]
+        active[...] = silu(cond)
+
+    out_ref[0] = exact(active[...], ada_ref[...]) + ab_ref[...]
+
+
+def modulate(sinus, labels, weights, ada, ada_bias):
+    n = sinus.shape[0]
+    features = ada.shape[0]
+    whole = lambda a: pl.BlockSpec(a.shape, lambda s: (0,) * a.ndim)
+    return pl.pallas_call(
+        modulate_kernel,
+        grid=(6,),
+        in_specs=[whole(a) for a in (sinus, labels) + weights]
+        + [
+            pl.BlockSpec((features, features), lambda s: (0, s)),
+            pl.BlockSpec((1, features), lambda s: (0, s)),
+        ],
+        out_specs=pl.BlockSpec((1, n, features), lambda s: (s, 0, 0)),
+        out_shape=jax.ShapeDtypeStruct((6, n, features), single),
+        scratch_shapes=[pltpu.VMEM((n, features), single)],
+        compiler_params=params(),
+        cost_estimate=cost(50 * n * ada.size, 2 * ada.size),
+        name="modulate",
+    )(sinus, labels, *weights, ada, ada_bias)
+
+
+def own_rows(me_ref, value, size):
+    width = value.shape[1]
+    place = lax.broadcasted_iota(jnp.int32, (size, width), 1)
+    line = lax.broadcasted_iota(jnp.int32, (size, width), 0)
+    pick = (place == me_ref[0] * size + line).astype(single)
+    return lax.dot_general(
+        pick, value, (((1,), (1,)), ((), ())), precision=highest, preferred_element_type=single
+    )
+
+
+def exact_small(a, b):
+    return lax.dot_general(
+        a, b, (((1,), (0,)), ((), ())), precision=highest, preferred_element_type=single
+    )
+
+
+def strip_sum(ref, kinds, count, features):
+    lines = []
+    for item in range(ref.shape[0]):
+        for l in range(count):
+            at = l * kinds * features
+            lines.append(jnp.sum(ref[item, :, at : at + kinds * features], axis=0, keepdims=True))
+    return jnp.concatenate(lines, axis=0)
+
+
+def early_kernel(
+    count, me_ref, parts_ref, sinus_ref, label_ref, wi_ref, bi_ref, wo_ref, bo_ref, table_ref, ada_ref,
+    before_ref, cond_ref, d_active_ref, ada_out_ref, d_mod_ref,
+):
+    features = ada_ref.shape[0]
+    d_mod = strip_sum(parts_ref, 4, count, features)
+    before, _, cond = condition(
+        sinus_ref[...], label_ref[...], wi_ref, bi_ref, wo_ref, bo_ref, table_ref
+    )
+    before_ref[...] = before
+    cond_ref[...] = cond
+    d_active_ref[...] = exact(d_mod, ada_ref[:, 2 * features :], nt=True)
+    size = ada_out_ref.shape[0]
+    ada_out_ref[...] = exact_small(own_rows(me_ref, silu(cond), size), d_mod)
+    d_mod_ref[...] = jnp.sum(d_mod, axis=0, keepdims=True)
+
+
+def early_condition(me, parts, count, sinus, labels, weights, ada, size):
+    n = sinus.shape[0]
+    features = ada.shape[0]
+    whole = lambda a: pl.BlockSpec(a.shape, lambda s: (0,) * a.ndim)
+    shapes = [
+        jax.ShapeDtypeStruct((n, features), single),
+        jax.ShapeDtypeStruct((n, features), single),
+        jax.ShapeDtypeStruct((n, features), single),
+        jax.ShapeDtypeStruct((size, 4 * features), single),
+        jax.ShapeDtypeStruct((1, 4 * features), single),
+    ]
+    return pl.pallas_call(
+        partial(early_kernel, count),
+        grid=(1,),
+        in_specs=[pl.BlockSpec(memory_space=pltpu.SMEM)]
+        + [whole(a) for a in (parts, sinus, labels) + weights + (ada,)],
+        out_specs=[whole(a) for a in shapes],
+        out_shape=shapes,
+        compiler_params=params(),
+        cost_estimate=cost(50 * n * ada.size, 2 * ada.size),
+        name="early_condition",
+    )(me, parts, sinus, labels, *weights, ada)
+
+
+def late_kernel(
+    count, me_ref, parts_ref, before_ref, cond_ref, d_active_ref, sinus_ref, label_ref,
+    wo_ref, ada_ref,
+    ada_out_ref, d_mod_ref, table_out_ref, wo_out_ref, wi_out_ref, d_cond_ref, d_before_ref,
+):
+    features = wo_ref.shape[0]
+    before = before_ref[...]
+    cond = cond_ref[...]
+    d_mod = strip_sum(parts_ref, 2, count, features)
+    d_active = d_active_ref[...] + exact(d_mod, ada_ref[...], nt=True)
+    d_cond = d_active * silu_slope(cond)
+    d_before = exact(d_cond, wo_ref[...], nt=True) * silu_slope(before)
+    size = ada_out_ref.shape[0]
+    ada_out_ref[...] = exact_small(own_rows(me_ref, silu(cond), size), d_mod)
+    d_mod_ref[...] = jnp.sum(d_mod, axis=0, keepdims=True)
+    onehot = label_rows(label_ref[...], table_out_ref.shape[1]).astype(single)
+    table_out_ref[...] = exact_small(own_rows(me_ref, d_cond, size), onehot)
+    wo_out_ref[...] = exact_small(own_rows(me_ref, silu(before), size), d_cond)
+    wi_out_ref[...] = exact_small(
+        own_rows(me_ref, sinus_ref[...], wi_out_ref.shape[0]), d_before
+    )
+    d_cond_ref[...] = jnp.sum(d_cond, axis=0, keepdims=True)
+    d_before_ref[...] = jnp.sum(d_before, axis=0, keepdims=True)
+
+
+def late_condition(me, parts, count, before, cond, d_active, sinus, labels, wo, ada, classes, devices):
+    features = ada.shape[0]
+    size = features // devices
+    whole = lambda a: pl.BlockSpec(a.shape, lambda s: (0,) * a.ndim)
+    shapes = [
+        jax.ShapeDtypeStruct((size, 2 * features), single),
+        jax.ShapeDtypeStruct((1, 2 * features), single),
+        jax.ShapeDtypeStruct((size, classes), single),
+        jax.ShapeDtypeStruct((size, features), single),
+        jax.ShapeDtypeStruct((sinus.shape[1] // devices, features), single),
+        jax.ShapeDtypeStruct((1, features), single),
+        jax.ShapeDtypeStruct((1, features), single),
+    ]
+    return pl.pallas_call(
+        partial(late_kernel, count),
+        grid=(1,),
+        in_specs=[pl.BlockSpec(memory_space=pltpu.SMEM)]
+        + [whole(a) for a in (parts, before, cond, d_active, sinus, labels, wo)]
+        + [pl.BlockSpec((features, 2 * features), lambda s: (0, 0))],
+        out_specs=[whole(a) for a in shapes],
+        out_shape=shapes,
+        compiler_params=params(),
+        cost_estimate=cost(20 * ada.size, ada.size),
+        name="late_condition",
+    )(me, parts, before, cond, d_active, sinus, labels, wo, ada)
+
+
+def sum_cores(halves):
+    strips = lax.axis_size("strips")
+    core = lax.axis_index("strips") % 2
+    got = lax.ppermute(halves(1 - core), "strips", [(i, i ^ 1) for i in range(strips)])
+    return (halves(core).astype(single) + got.astype(single)).astype(bfloat)
+
+
+def sum_axis(part, axis, size, place, step):
+    pick = lambda k: lax.dynamic_index_in_dim(part, place ^ k, 0, keepdims=False)
+    count = lax.axis_size(axis)
+    got = [
+        lax.ppermute(pick(k), axis, [(i, i ^ (k * step)) for i in range(count)])
+        for k in range(1, size)
+    ]
+    total = pick(0).astype(single)
+    for g in got:
+        total = total + g.astype(single)
+    return total
+
+
+def sum_items(part):
+    return sum_axis(part, "items", lax.axis_size("items"), lax.axis_index("items"), 1).astype(bfloat)
+
+
+def sum_strips(part):
+    strip = lax.axis_index("strips")
+    return sum_axis(part, "strips", lax.axis_size("strips") // 2, strip // 2, 2)
+
+
+def after(value, *others):
+    return lax.optimization_barrier((value,) + others)[0]
 
 
 def tap_rows(kernel):
@@ -826,23 +1161,21 @@
     row_vector = lambda v: v.astype(single).reshape(1, -1)
     edge = jnp.stack([strip > 0, strip < strips - 1]).astype(single)
 
-    all_times = lax.all_gather(timesteps, "items", axis=0, tiled=True)
-    all_labels = lax.all_gather(labels, "items", axis=0, tiled=True)
-    time_in, time_out, table, ada = (
-        w.astype(single) for w in (time_in_weight, time_out_weight, label_table, ada_weight)
-    )
-    sinus = time_features(all_times, time_in_weight.shape[0] // 2)
-    before = exact(sinus, time_in) + time_in_bias.astype(single)
-    inner = jax.nn.silu(before)
-    onehot = (all_labels[:, None] == jnp.arange(table.shape[1], dtype=jnp.int32)[None, :]).astype(
-        single
-    )
-    cond = exact(inner, time_out) + time_out_bias.astype(single) + exact_nt(onehot, table)
-    active = jax.nn.silu(cond)
-    own_active = lax.dynamic_slice_in_dim(active, item * count, count, axis=0)
-    modulation = exact(own_active, ada) + ada_bias.astype(single)
+    lines = -(-count // 8) * 8
+    weights = (
+        time_in_weight, row_vector(time_in_bias), time_out_weight, row_vector(time_out_bias),
+        label_table,
+    )
+    waves = time_in_weight.shape[0] // 2
+    modulation = modulate(
+        time_features(jnp.pad(timesteps, (0, lines - count)), waves),
+        jnp.pad(labels, (0, lines - count))[:, None],
+        weights,
+        ada_weight,
+        row_vector(ada_bias),
+    )
     shift_a, scale_a, gate_a, shift_b, scale_b, gate_b = (
-        modulation[:, None, i * features : (i + 1) * features] for i in range(6)
+        modulation[i, :count, None, :] for i in range(6)
     )
 
     ends = jnp.concatenate([latents[:, -1:], cotangent[:, -1:]], axis=1)
@@ -875,17 +1208,19 @@
     def own_columns(array, axis):
         return array if share == 1 else lax.dynamic_slice_in_dim(array, head_at, width, axis=axis)
 
-    wq, wk, wv = (
-        own_columns(input_weight[:, i * features : (i + 1) * features], 1) for i in range(3)
-    )
-    bq = own_columns(row_vector(query_bias), 1)
-    bv = own_columns(row_vector(value_bias), 1)
+    own_weight = jnp.concatenate(
+        [own_columns(input_weight[:, i * features : (i + 1) * features], 1) for i in range(3)], axis=1
+    ) if share > 1 else input_weight
+    own_bias = jnp.concatenate(
+        [own_columns(row_vector(b), 1) for b in (query_bias, value_bias)], axis=1
+    )
     piece = width // CHUNKS
     saved = []
     mixed = []
+    d_act = feed_upstream(d_branch, shrink_weight)
+    group, d_act = lax.optimization_barrier((group, d_act))
     for c in range(CHUNKS):
-        at = slice(c * piece, (c + 1) * piece)
-        saved.append(attend(group, wq[:, at], wk[:, at], wv[:, at], bq[:, at], bv[:, at]))
+        saved.append(attend(group, own_weight, own_bias, c * piece, piece))
         mixed.append(collect(saved[c][3]))
     if share == 1:
         mixed = [m.reshape(count, 4, quarter, piece) for m in mixed]
@@ -897,12 +1232,12 @@
     attended, middle, normed_b = middle_part(
         mixed, output_weight, row_vector(output_bias), kept, gate_a, scale_b, shift_b
     )
-    branch, e, grad_shrink, grad_expand, feed_small = feed_forward(
+    branch, e, act, d_hid, feed_small = feed_forward(
         edge,
         normed_b,
         from_above(normed_b[:, -2:]),
         from_below(normed_b[:, :2]),
-        d_branch,
+        d_act,
         expand_weight,
         row_vector(expand_bias),
         tap_rows(mixer_kernel),
@@ -919,13 +1254,14 @@
 
     hidden = expand_weight.shape[1]
     steps = hidden // features
+    grad_shrink, grad_expand = feed_grads(act, d_hid, normed_b, d_branch)
+
     early = jnp.concatenate(
         [
             grad_shrink.reshape(devices, hidden // devices, features),
             grad_expand.reshape(steps, devices, features // devices, features)
             .transpose(1, 0, 2, 3)
             .reshape(devices, hidden // devices, features),
-            grad_output.reshape(devices, features // devices, features),
         ],
         axis=1,
     )
@@ -940,33 +1276,72 @@
         d_mixed = [got[:, c * piece : (c + 1) * piece] for c in range(CHUNKS)]
     grads = []
     for c in range(CHUNKS):
+        if c == 0:
+            d_mixed[c], _ = lax.optimization_barrier((d_mixed[c], early))
         q, k, v, out, logs = saved[c]
         grads.append(attend_back(q, k, v, out, d_mixed[c], logs))
-    d_query, d_key, d_value = (
-        jnp.concatenate([grads[c][i] for c in range(CHUNKS)], axis=1) for i in range(3)
-    )
-    d_projected = jnp.concatenate([d_query, d_key, d_value], axis=1)
-    own_weight = jnp.concatenate([wq, wk, wv], axis=1)
-    d_group = dot_nt(d_projected, own_weight).astype(bfloat)
+    size = features // devices
+    narrow = jnp.stack([jnp.sum(turn_sums[:, 4], axis=0), jnp.sum(grad_shrink_bias[:, 0], axis=0)])
+    to_all = jnp.concatenate(
+        [
+            turn_sums[:, 3], turn_sums[:, 1], turn_sums[:, 2], turn_sums[:, 0],
+        ],
+        axis=1,
+    ).reshape(-1)
+    to_all = jnp.concatenate([to_all, timesteps.astype(single), labels.astype(single)])
+    fill = -(to_all.shape[0] + 11 * (hidden // devices) + 2 * size) % LANES
+    early_small = jnp.concatenate(
+        [
+            jnp.broadcast_to(to_all, (devices, to_all.shape[0])),
+            feed_small[:11].reshape(11, devices, -1).transpose(1, 0, 2).reshape(devices, -1),
+            narrow.reshape(2, devices, -1).transpose(1, 0, 2).reshape(devices, -1),
+            jnp.zeros((devices, fill), single),
+        ],
+        axis=1,
+    )
+    early_small = after(early_small, grads[0][0], *d_mixed)
+    early_got = lax.all_to_all(early_small, both, 0, 0, tiled=True)
+
+    parts = [g for chunk in grads for g in chunk]
+    d_group = regroup(parts, own_weight)
     d_reduced = collect(d_group)
     if share > 1:
         d_reduced = jnp.sum(
             d_reduced.reshape(groups, share, quarter, features).astype(single), axis=1
         ).astype(bfloat)
     d_reduced = d_reduced.reshape(count, 4, quarter, features)
-    grad_input = dot_tn(group, d_projected).astype(bfloat)
-    d_query_sum = jnp.sum(d_query.astype(single), axis=0)
-    d_value_sum = jnp.sum(d_value.astype(single), axis=0)
+    late, d_sums = input_grad(after(group, d_group), grad_output, parts)
+    d_query_sum = d_sums[0, :width]
+    d_value_sum = d_sums[0, width:]
     if share > 1:
         zero = jnp.zeros((features, 3, features), bfloat)
         grad_input = lax.dynamic_update_slice(
-            zero, grad_input.reshape(features, 3, width), (0, 0, head_at)
+            zero, late[:, : 3 * width].reshape(features, 3, width), (0, 0, head_at)
         ).reshape(features, 3 * features)
+        late = jnp.concatenate([grad_input, grad_output], axis=1)
         flat = jnp.zeros((features,), single)
         d_query_sum = lax.dynamic_update_slice(flat, d_query_sum, (head_at,))
         d_value_sum = lax.dynamic_update_slice(flat, d_value_sum, (head_at,))
-    late_sum = lax.psum_scatter(grad_input, both, scatter_dimension=0, tiled=True).astype(single)
-
+    late = late.reshape(items, strips // 2, 2, size, 4 * features)
+    late_part = sum_cores(lambda core: lax.dynamic_index_in_dim(late, core, 2, keepdims=False))
+
+    per_latent = count * 4 * features
+    parts_early = early_got[:, :per_latent].reshape(items, strips, per_latent)
+    first = early_got.reshape(items, strips, -1)[:, 0, per_latent : per_latent + 2 * count]
+    all_times = first[:, :count].reshape(-1)
+    all_labels = first[:, count:].reshape(-1, 1).astype(jnp.int32)
+    sinus = time_features(all_times, waves)
+    early_sums = jnp.sum(early_got[:, per_latent + 2 * count :], axis=0)
+    cut = 11 * (hidden // devices)
+    feed_sum = early_sums[:cut].reshape(11, -1)
+    narrow_sum = early_sums[cut : cut + 2 * size].reshape(2, size)
+    index = jnp.reshape(me, (1,)).astype(jnp.int32)
+    before, cond, d_active, grad_ada_early, d_mod_early = early_condition(
+        index, parts_early, count, sinus, all_labels, weights, ada_weight, size
+    )
+
+    d_reduced, before, late_part = lax.optimization_barrier((d_reduced, before, late_part))
+    late_part = sum_items(late_part)
     grad_latents, down_small, final_sums = final(
         d_reduced,
         from_above(d_reduced[:, 2:, -2 * sub :]),
@@ -978,61 +1353,61 @@
         down_taps,
     )
 
-    d_gate_b, d_shift_b, d_scale_b, d_gate_a, output_bias_part = (
-        turn_sums[:, t] for t in range(5)
-    )
-    narrow = jnp.stack(
+    late_narrow = jnp.concatenate([d_query_sum[None], d_value_sum[None], down_small[:10]], axis=0)
+    to_all = final_sums[:, :2].reshape(-1)
+    fill = -(to_all.shape[0] + 12 * size) % LANES
+    late_small = jnp.concatenate(
         [
-            jnp.sum(output_bias_part, axis=0),
-            jnp.sum(grad_shrink_bias[:, 0], axis=0),
-            d_query_sum,
-            d_value_sum,
-        ]
-    )
-    narrow = jnp.concatenate([narrow, down_small[:10]], axis=0)
-    small = jnp.concatenate(
-        [
-            feed_small[:11].reshape(11, devices, hidden // devices).transpose(1, 0, 2).reshape(devices, -1),
-            narrow.reshape(14, devices, features // devices).transpose(1, 0, 2).reshape(devices, -1),
+            jnp.broadcast_to(to_all, (devices, to_all.shape[0])),
+            late_narrow.reshape(12, devices, size).transpose(1, 0, 2).reshape(devices, -1),
+            jnp.zeros((devices, fill), single),
         ],
         axis=1,
     )
-    small = jnp.sum(lax.all_to_all(small, both, 0, 0, tiled=True), axis=0)
-    cut = 11 * (hidden // devices)
-    feed_sum = small[:cut].reshape(11, hidden // devices)
-    narrow_sum = small[cut:].reshape(14, features // devices)
-
-    d_modulation = jnp.concatenate(
-        [final_sums[:, 0], final_sums[:, 1], d_gate_a, d_shift_b, d_scale_b, d_gate_b], axis=1
-    )
-    d_modulation = jnp.sum(lax.all_gather(d_modulation, "strips", axis=0), axis=0)
-    d_modulation = lax.all_gather(d_modulation, "items", axis=0, tiled=True)
-    d_cond = exact_nt(d_modulation, ada) * silu_slope(cond)
-    d_before = exact_nt(d_cond, time_out) * silu_slope(before)
+    late_small, late_part = lax.optimization_barrier((late_small, late_part))
+    late_sum = sum_strips(late_part)
+    late_got = lax.all_to_all(late_small, both, 0, 0, tiled=True)
+    late_sums = jnp.sum(late_got[:, to_all.shape[0] :], axis=0)[: 12 * size].reshape(12, size)
+    (
+        grad_ada_late, d_mod_late, grad_table, grad_time_out, grad_time_in, d_cond, d_before,
+    ) = late_condition(
+        index,
+        late_got[:, : to_all.shape[0]].reshape(items, strips, -1),
+        count,
+        before,
+        cond,
+        d_active,
+        sinus,
+        all_labels,
+        time_out_weight,
+        ada_weight,
+        label_table.shape[1],
+        devices,
+    )
 
     def mine(array):
-        size = array.shape[-1] // devices
-        return lax.dynamic_slice_in_dim(array, me * size, size, axis=array.ndim - 1)
+        part = array.shape[-1] // devices
+        return lax.dynamic_slice_in_dim(array[0], me * part, part, axis=0)
 
     feed_rows = hidden // devices
     return (
         result,
         grad_latents,
-        exact_tn(mine(sinus), d_before),
-        jnp.sum(mine(d_before), axis=0),
-        exact_tn(mine(inner), d_cond),
-        jnp.sum(mine(d_cond), axis=0),
-        exact_tn(mine(d_cond), onehot),
-        exact_tn(mine(active), d_modulation),
-        jnp.sum(mine(d_modulation), axis=0),
-        narrow_sum[4:13].T,
-        narrow_sum[13],
-        late_sum,
-        narrow_sum[2],
-        narrow_sum[3],
-        early_sum[2 * feed_rows :],
+        grad_time_in,
+        mine(d_before),
+        grad_time_out,
+        mine(d_cond),
+        grad_table,
+        jnp.concatenate([grad_ada_late, grad_ada_early], axis=1),
+        mine(jnp.concatenate([d_mod_late, d_mod_early], axis=1)),
+        late_sums[2:11].T,
+        late_sums[11],
+        late_sum[:, : 3 * features],
+        late_sums[0],
+        late_sums[1],
+        late_sum[:, 3 * features :],
         narrow_sum[0],
-        early_sum[feed_rows : 2 * feed_rows]
+        early_sum[feed_rows:]
         .reshape(steps, features // devices, features)
         .transpose(1, 0, 2)
         .reshape(features // devices, hidden),

time: 649 us -> 518 us (0.80)
  waiting for transfers between devices: 198 us -> 102 us
  blocking collectives: 60.4 us -> 0 us
  Pallas kernels: 219 us -> 267 us
  matrix products: 41.3 us -> 0 us
  starting transfers between devices: 41 us -> 61.5 us
    reduce_scatter x1, waiting for transfers between devices: 100 us -> 0.01 us  [per_device(): lax.psum_scatter(early, both, scatter_dimension=0, tiled=False)]
    pallas_call x0 -> x7, Pallas kernels: none -> 66.3 us  [the longest x1 14.8 us: feed_grads(): pl.pallas_call(feed_grads_kernel, grid=(steps,), in_specs=[pl.BlockSpec((...]
    dot_general x12 -> x0, matrix products: 41.3 us -> none  [the longest x3 10.8 us: exact_nt(): return lax.dot_general(a, b, (((1,), (1,)), ((), ())), precision=highest)]
    all_to_all x1 -> x0, blocking collectives: 26.3 us -> none  [spread(): got = lax.all_to_all(flat, 'strips', 0, 0, tiled=True)]
    all_gather x2 -> x0, blocking collectives: 24.8 us -> none  [the longest x1 16.2 us: per_device(): lax.all_gather(d_modulation, 'strips', axis=0)]
    all_to_all x1 -> x2, waiting for transfers between devices: 0.01 us -> 13.7 us  [the longest x1 13.7 us: per_device(): late_got = lax.all_to_all(late_small, both, 0, 0, tiled=True)]
    pallas_call x2, Pallas kernels: 45.1 us -> 33.9 us  [attend(): pl.pallas_call(attend_kernel, grid=(pairs,), in_specs=[pl.BlockSpec((toke...]
    all_to_all x2 -> x3, starting transfers between devices: 8.43 us -> 19.1 us  [spread(): got = lax.all_to_all(flat, 'strips', 0, 0, tiled=True)]
  transfers between devices with their start and end apart: 14 -> 22, of which waited for: 6 -> 9; matrix products, arithmetic and copies ran while one was open for 12% -> 10% of each run, Pallas kernels for 10% -> 28%
where the time goes in v2:
time: 518 us; the launch traced here: 510 us
  Pallas kernels  267 us (52%)
  waiting for transfers between devices  102 us (20%)
  starting transfers between devices  61.5 us (12%)
  local copies, waits for them, and re-layouts  44.5 us (9%)
  other arithmetic  19.5 us (4%)
  between operations  15 us (3%)
    pallas_call x1, Pallas kernels, feed_forward(): pl.pallas_call(feed_kernel, grid=(steps,), in_specs=[pl.BlockSpec(memory_...  73.1 us
    all_to_all x3, waiting for transfers between devices, collect(): return lax.all_to_all(flat, 'strips', 0, 0, tiled=True)  58.8 us
    pallas_call x2, Pallas kernels, attend_back(): pl.pallas_call(attend_back_kernel, grid=(pairs,), in_specs=[column] * 5 +...  36.3 us
    pallas_call x2, Pallas kernels, attend(): pl.pallas_call(attend_kernel, grid=(pairs,), in_specs=[pl.BlockSpec((toke...  33.9 us
    all_to_all x3, waiting for transfers between devices, spread(): got = lax.all_to_all(flat, 'strips', 0, 0, tiled=True)  23.9 us
    all_to_all x3, starting transfers between devices, spread(): got = lax.all_to_all(flat, 'strips', 0, 0, tiled=True)  19.1 us
    pallas_call x1, Pallas kernels, final(): pl.pallas_call(final_kernel, grid=(count,), in_specs=[pl.BlockSpec((1, 4,...  17 us
    pallas_call x1, Pallas kernels, turn(): pl.pallas_call(partial(turn_kernel, len(mixed)), grid=(count,), in_specs=...  15.3 us
  transfers between devices with their start and end apart: 22, of which 9 were waited for; matrix products, arithmetic and copies ran while one was open for 10% of the time, Pallas kernels for 28%

profile of v2, /device:TPU:0, one launch (start us, length us, event | category | flops | bytes accessed | tf_op | source)
XLA Modules:
  0.0 510.0 jit_solution(4163739150962957273)
XLA Ops:
  18.0 8.2 %modulate.1 = f32[6,8,768]{2,1,0:T(8,128)} custom-call(f32[8,256]{1,0:T(8,128)} %pad_maximum_fusion.5.sinus_ref, s32[8,1]{1,0:T(8,128)} %copy.87.label_ref, bf16[256,768]{1,0:T(8,128)(2,1)} %wi_ref.3, f32[1,768]{1,0:T(1,128)} %reshape.305.bi_ref, bf16[768,768]{1,0:T(8,128)(2,1)} %wo_ref.5, f32[1,768]{1,0:T(1,128)} %reshape.307.bo_ref, ...), custom_call_target="tpu_custom_call" | custom-call | flops 1415577600 | bytes 7077888 | tf_op jit(solution)/shard_map/modulate/pallas_call | solution.py:951
  31.6 11.6 %front.1 = (bf16[2,4,128,768]{3,2,1,0:T(8,128)(2,1)}, bf16[2,10,64,768]{3,2,1,0:T(8,128)(2,1)}, bf16[2,8,64,768]{3,2,1,0:T(8,128)(2,1)}) custom-call(f32[2]{0:T(128)} %add_convert_fusion.edge_ref, bf16[2,8,64,768]{3,2,1,0:T(8,128)(2,1)} %x_ref.1, bf16[2,1,64,768]{3,2,1,0:T(8,128)(2,1)} %get-tuple-element.171.top_ref, ...), custom_call_target="tpu_custom_call" | custom-call | flops 117964800 | bytes 6291456 | tf_op jit(solution)/shard_map/front/pallas_call | solution.py:146
  43.2 6.3 %all-to-all-start = ((bf16[8,128,768]{2,1,0:T(8,128)(2,1)}), bf16[8,128,768]{2,1,0:T(8,128)(2,1)S(1)}, u32[]{:S(2)}, u32[]{:S(2)}) async-start(bf16[8,128,768]{2,1,0:T(8,128)(2,1)} %bitcast.135), calls=%async_computation | async-start | bytes 3145728 | tf_op jit(solution)/shard_map/all_to_all | solution.py:1195
  50.2 5.6 %upstream.1 = (bf16[2,8,64,768]{3,2,1,0:T(8,128)(2,1)}, bf16[2,10,64,768]{3,2,1,0:T(8,128)(2,1)}, f32[2,1,768]{2,1,0:T(1,128)}) custom-call(bf16[2,8,64,768]{3,2,1,0:T(8,128)(2,1)} %g_ref.1, bf16[2,1,64,768]{3,2,1,0:T(8,128)(2,1)} %get-tuple-element.170.top_ref, bf16[2,1,64,768]{3,2,1,0:T(8,128)(2,1)} %get-tuple-element.168.bottom_ref, ...), custom_call_target="tpu_custom_call" | custom-call | flops 102236160 | bytes 4718592 | tf_op jit(solution)/shard_map/upstream/pallas_call | solution.py:196
  55.8 10.5 %feed_upstream.1.d_act_ref = bf16[1280,3072]{1,0:T(8,128)(2,1)} custom-call(bf16[1280,768]{1,0:T(8,128)(2,1)} %bitcast.163, bf16[3072,768]{1,0:T(8,128)(2,1)} %ws_ref.3), custom_call_target="tpu_custom_call" | custom-call | flops 6039797760 | bytes 9830400 | tf_op jit(solution)/shard_map/feed_upstream/pallas_call | solution.py:483
  66.3 21.0 %all-to-all-done = bf16[8,128,768]{2,1,0:T(8,128)(2,1)S(1)} async-done(((bf16[8,128,768]{2,1,0:T(8,128)(2,1)}), bf16[8,128,768]{2,1,0:T(8,128)(2,1)S(1)}, u32[]{:S(2)}, u32[]{:S(2)}) %all-to-all-start) | async-done | bytes 1572896 | tf_op jit(solution)/shard_map/all_to_all | solution.py:1195
  88.6 17.0 %attend.2 = (bf16[1024,384]{1,0:T(8,128)(2,1)}, bf16[1024,384]{1,0:T(8,128)(2,1)}, bf16[1024,384]{1,0:T(8,128)(2,1)}, bf16[1024,384]{1,0:T(8,128)(2,1)}, f32[3,2,1024]{2,1,0:T(2,128)}) custom-call(bf16[1024,768]{1,0:T(8,128)(2,1)} %bitcast.132, bf16[768,2304]{1,0:T(8,128)(2,1)} %refs_6_.1, bf16[768,2304]{1,0:T(8,128)(2,1)} %refs_6_.1, ...), custom_call_target="tpu_custom_call" | custom-call | flops 8254390272 | bytes 6488064 | tf_op jit(solution)/shard_map/attend/pallas_call | solution.py:252
  109.4 16.9 %attend.3 = (bf16[1024,384]{1,0:T(8,128)(2,1)}, bf16[1024,384]{1,0:T(8,128)(2,1)}, bf16[1024,384]{1,0:T(8,128)(2,1)}, bf16[1024,384]{1,0:T(8,128)(2,1)}, f32[3,2,1024]{2,1,0:T(2,128)}) custom-call(bf16[1024,768]{1,0:T(8,128)(2,1)} %bitcast.133, bf16[768,2304]{1,0:T(8,128)(2,1)} %refs_6_.1, bf16[768,2304]{1,0:T(8,128)(2,1)} %refs_6_.1, ...), custom_call_target="tpu_custom_call" | custom-call | flops 8254390272 | bytes 6488064 | tf_op jit(solution)/shard_map/attend/pallas_call | solution.py:252
  135.6 19.1 %all-to-all-done.2 = bf16[8,128,384]{2,1,0:T(8,128)(2,1)S(1)} async-done(((bf16[8,128,384]{2,1,0:T(8,128)(2,1)}), bf16[8,128,384]{2,1,0:T(8,128)(2,1)S(1)}, u32[]{:S(2)}, u32[]{:S(2)}) %all-to-all-start.2) | async-done | bytes 786464 | tf_op jit(solution)/shard_map/all_to_all | solution.py:1200
  155.7 8.0 %middle.1 = (f32[2,8,64,768]{3,2,1,0:T(8,128)}, f32[2,8,64,768]{3,2,1,0:T(8,128)}, bf16[2,8,64,768]{3,2,1,0:T(8,128)(2,1)}) custom-call(bf16[2,4,128,384]{3,2,1,0:T(8,128)(2,1)} %bitcast.126, bf16[2,4,128,384]{3,2,1,0:T(8,128)(2,1)} %bitcast.128, bf16[768,768]{1,0:T(8,128)(2,1)} %refs_9_.1, f32[1,768]{1,0:T(1,128)} %reshape.313.refs_3_, ...), custom_call_target="tpu_custom_call" | custom-call | flops 1207959552 | bytes 11010048 | tf_op jit(solution)/shard_map/middle/pallas_call | solution.py:451
  171.9 73.1 %feed_forward.1 = (f32[1024,768]{1,0:T(8,128)}, f32[1024,768]{1,0:T(8,128)}, bf16[1024,3072]{1,0:T(8,128)(2,1)}, bf16[1024,3072]{1,0:T(8,128)(2,1)}, f32[16,3072]{1,0:T(8,128)}) custom-call(f32[2]{0:T(128)} %add_convert_fusion.edge_ref, bf16[2,8,64,768]{3,2,1,0:T(8,128)(2,1)} %get-tuple-element.93.nb_ref, bf16[2,2,64,768]{3,2,1,0:T(8,128)(2,1)} %copy-done.25, ...), custom_call_target="tpu_custom_call" | custom-call | flops 16911433728 | bytes 44040192 | tf_op jit(solution)/shard_map/feed_forward/pallas_call | solution.py:590
  245.0 15.3 %turn.1 = (bf16[2,8,64,768]{3,2,1,0:T(8,128)(2,1)}, f32[2,8,64,768]{3,2,1,0:T(8,128)}, bf16[2,4,128,384]{3,2,1,0:T(8,128)(2,1)}, bf16[2,4,128,384]{3,2,1,0:T(8,1...) custom-call(f32[1024,768]{1,0:T(8,128)} %get-tuple-element.95.refs_0_, f32[1024,768]{1,0:T(8,128)} %get-tuple-element.96.refs_1_, ...), custom_call_target="tpu_custom_call" | custom-call | flops 2415919104 | bytes 20447232 | tf_op jit(solution)/shard_map/turn/pallas_call | solution.py:745
  260.3 7.6 %all-to-all-start.3 = ((bf16[8,128,384]{2,1,0:T(8,128)(2,1)}), bf16[8,128,384]{2,1,0:T(8,128)(2,1)S(1)}, u32[]{:S(2)}, u32[]{:S(2)}) async-start(bf16[8,128,384]{2,1,0:T(8,128)(2,1)} %bitcast.141), calls=%async_computation.3 | async-start | bytes 1572864 | tf_op jit(solution)/shard_map/all_to_all | solution.py:1195
  268.0 14.8 %feed_grads.1 = (bf16[3072,768]{1,0:T(8,128)(2,1)}, bf16[4,768,768]{2,1,0:T(8,128)(2,1)}) custom-call(bf16[1024,3072]{1,0:T(8,128)(2,1)} %get-tuple-element.105.act_ref, bf16[1024,3072]{1,0:T(8,128)(2,1)} %get-tuple-element.106.d_hid_ref, bf16[2,8,64,768]{3,2,1,0:T(8,128)(2,1)} %get-tuple-element.93.nb_ref, bf16[2,10,64,768]{3,2,1,0:T(8,128)(2,1)} %get-tuple-element.88.db_ref), custom_call_target="tpu_custom_call" | custom-call | flops 9663676416 | bytes 31457280 | tf_op jit(solution)/shard_map/feed_grads/pallas_call | solution.py:643
  297.2 18.1 %attend_back.2 = (bf16[1024,384]{1,0:T(8,128)(2,1)}, bf16[1024,384]{1,0:T(8,128)(2,1)}, bf16[1024,384]{1,0:T(8,128)(2,1)}) custom-call(bf16[1024,384]{1,0:T(8,128)(2,1)} %get-tuple-element.101.q_ref, bf16[1024,384]{1,0:T(8,128)(2,1)} %get-tuple-element.102.k_ref, bf16[1024,384]{1,0:T(8,128)(2,1)} %get-tuple-element.103.v_ref, ...), custom_call_target="tpu_custom_call" | custom-call | flops 16106127360 | bytes 6291456 | tf_op jit(solution)/shard_map/attend_back/pallas_call | solution.py:313
  323.3 18.2 %attend_back.3 = (bf16[1024,384]{1,0:T(8,128)(2,1)}, bf16[1024,384]{1,0:T(8,128)(2,1)}, bf16[1024,384]{1,0:T(8,128)(2,1)}) custom-call(bf16[1024,384]{1,0:T(8,128)(2,1)} %get-tuple-element.114.q_ref, bf16[1024,384]{1,0:T(8,128)(2,1)} %get-tuple-element.115.k_ref, bf16[1024,384]{1,0:T(8,128)(2,1)} %get-tuple-element.116.v_ref, ...), custom_call_target="tpu_custom_call" | custom-call | flops 16106127360 | bytes 6291456 | tf_op jit(solution)/shard_map/attend_back/pallas_call | solution.py:313
  341.5 9.1 %regroup.1 = bf16[1024,768]{1,0:T(8,128)(2,1)} custom-call(bf16[1024,384]{1,0:T(8,128)(2,1)} %get-tuple-element.111.refs_0_.refs_2_, bf16[1024,384]{1,0:T(8,128)(2,1)} %get-tuple-element.112.refs_1_.refs_3_, bf16[1024,384]{1,0:T(8,128)(2,1)} %get-tuple-element.113.refs_2_.refs_4_, bf16[1024,384]{1,0:T(8,128)(2,1)} %get-tuple-element.119.refs_3_.refs_5_, ...), custom_call_target="tpu_custom_call" | custom-call | flops 3623878656 | bytes 6291456 | tf_op jit(solution)/shard_map/regroup/pallas_call | solution.py:346
  350.6 10.1 %input_grad.1 = (bf16[768,3072]{1,0:T(8,128)(2,1)}, f32[8,1536]{1,0:T(8,128)}) custom-call(bf16[1024,768]{1,0:T(8,128)(2,1)} %bitcast.134, bf16[768,768]{1,0:T(8,128)(2,1)} %get-tuple-element.128.refs_1_, bf16[1024,384]{1,0:T(8,128)(2,1)} %get-tuple-element.111.refs_0_.refs_2_, bf16[1024,384]{1,0:T(8,128)(2,1)} %get-tuple-element.112.refs_1_.refs_3_, ...), custom_call_target="tpu_custom_call" | custom-call | flops 3623878656 | bytes 7864320 | tf_op jit(solution)/shard_map/input_grad/pallas_call | solution.py:387
  373.1 8.1 %early_condition.1 = (f32[8,768]{1,0:T(8,128)}, f32[8,768]{1,0:T(8,128)}, f32[8,768]{1,0:T(8,128)}, f32[24,3072]{1,0:T(8,128)}, f32[1,3072]{1,0:T(1,128)}) custom-call(s32[1]{0:T(128)} %bitcast.30.me_ref, f32[4,8,6144]{2,1,0:T(8,128)} %slice_bitcast_fusion.parts_ref, f32[8,256]{1,0:T(8,128)} %pad_maximum_fusion.6.sinus_ref, ...), custom_call_target="tpu_custom_call" | custom-call | flops 1415577600 | bytes 7077888 | tf_op jit(solution)/shard_map/early_condition/pallas_call | solution.py:1021
  384.6 35.8 %all-to-all-done.5 = bf16[8,128,768]{2,1,0:T(8,128)(2,1)} async-done(((bf16[8,128,768]{2,1,0:T(8,128)(2,1)}), bf16[8,128,768]{2,1,0:T(8,128)(2,1)}, u32[]{:S(2)}, u32[]{:S(2)}) %all-to-all-start.5) | async-done | bytes 1572896 | tf_op jit(solution)/shard_map/all_to_all | solution.py:1200
  431.5 17.0 %final.1 = (bf16[2,8,64,768]{3,2,1,0:T(8,128)(2,1)}, f32[16,768]{1,0:T(8,128)}, f32[2,8,768]{2,1,0:T(8,128)}) custom-call(bf16[2,4,128,768]{3,2,1,0:T(8,128)(2,1)} %bitcast.29.d_ref, bf16[2,2,32,768]{3,2,1,0:T(8,128)(2,1)} %copy-done.8, bf16[2,2,32,768]{3,2,1,0:T(8,128)(2,1)} %copy-done.9, bf16[2,10,64,768]{3,2,1,0:T(8,128)(2,1)} %get-tuple-element.131.normed_ref, ...), custom_call_target="tpu_custom_call" | custom-call | flops 141557760 | bytes 9437184 | tf_op jit(solution)/shard_map/final/pallas_call | solution.py:858
  461.4 6.6 %all-to-all-start.7 = ((f32[32,1,3456]{2,1,0:T(1,128)}), f32[32,1,3456]{2,1,0:T(1,128)S(1)}, u32[]{:S(2)}, u32[]{:S(2)}) async-start(f32[32,1,3456]{2,1,0:T(1,128)} %all_to_all.43), calls=%async_computation.7 | async-start | bytes 884736 | tf_op jit(solution)/shard_map/all_to_all | solution.py:1369
  472.7 13.7 %all-to-all-done.7 = f32[32,1,3456]{2,1,0:T(1,128)S(1)} async-done(((f32[32,1,3456]{2,1,0:T(1,128)}), f32[32,1,3456]{2,1,0:T(1,128)S(1)}, u32[]{:S(2)}, u32[]{:S(2)}) %all-to-all-start.7) | async-done | bytes 442400 | tf_op jit(solution)/shard_map/all_to_all | solution.py:1369
  488.0 5.5 %late_condition.1 = (f32[24,1536]{1,0:T(8,128)}, f32[1,1536]{1,0:T(1,128)}, f32[24,1001]{1,0:T(8,128)}, f32[24,768]{1,0:T(8,128)}, f32[8,768]{1,0:T(8,128)}, /*index=5*/f32[1,768]{1,0:T(1,128)}, f32[1,768]{1,0:T(1,128)}) custom-call(s32[1]{0:T(128)} %bitcast.30.me_ref, f32[4,8,3072]{2,1,0:T(8,128)} %slice_bitcast_fusion.1.parts_ref, ...), custom_call_target="tpu_custom_call" | custom-call | flops 70778880 | bytes 3538944 | tf_op jit(solution)/shard_map/late_condition/pallas_call | solution.py:1072
  (204 shorter events, 117.7 us)
Async XLA Ops:
  8.7 21.4 %collective-permute-start.1 = (bf16[2,2,64,768]{3,2,1,0:T(8,128)(2,1)S(1)}, bf16[2,2,64,768]{3,2,1,0:T(8,128)(2,1)S(1)}, u32[]{:S(2)}, u32[]{:S(2)}) collective-permute-start(bf16[2,2,64,768]{3,2,1,0:T(8,128)(2,1)S(1)} %pad_maximum_fusion.3), channel_id=1, source_target_pairs={{1,0},{2,1},{3,2},{4,3},{5,4},{6,5},{7,6},{9,8},{10,9},{11,10},{12... | collective-permute-start | bytes 1179656 | tf_op jit(solution)/shard_map/ppermute | solution.py:890
  10.0 20.8 %collective-permute-start = (bf16[2,2,64,768]{3,2,1,0:T(8,128)(2,1)S(1)}, bf16[2,2,64,768]{3,2,1,0:T(8,128)(2,1)S(1)}, u32[]{:S(2)}, u32[]{:S(2)}) collective-permute-start(bf16[2,2,64,768]{3,2,1,0:T(8,128)(2,1)S(1)} %pad_maximum_fusion.2), channel_id=1, source_target_pairs={{0,1},{1,2},{2,3},{3,4},{4,5},{5,6},{6,7},{8,9},{9,10},{10,11},{11... | collective-permute-start | bytes 1179656 | tf_op jit(solution)/shard_map/ppermute | solution.py:885
  43.2 44.2 %all-to-all-start = ((bf16[8,128,768]{2,1,0:T(8,128)(2,1)}), bf16[8,128,768]{2,1,0:T(8,128)(2,1)S(1)}, u32[]{:S(2)}, u32[]{:S(2)}) async-start(bf16[8,128,768]{2,1,0:T(8,128)(2,1)} %bitcast.135), calls=%async_computation | async-start | bytes 3145728 | tf_op jit(solution)/shard_map/all_to_all | solution.py:1195
  105.5 24.7 %all-to-all-start.1 = ((bf16[8,128,384]{2,1,0:T(8,128)(2,1)}), bf16[8,128,384]{2,1,0:T(8,128)(2,1)S(1)}, u32[]{:S(2)}, u32[]{:S(2)}) async-start(bf16[8,128,384]{2,1,0:T(8,128)(2,1)} %bitcast.139), calls=%async_computation.1 | async-start | bytes 1572864 | tf_op jit(solution)/shard_map/all_to_all | solution.py:1200
  109.4 25.1 %copy-start.23 = (bf16[768]{0:T(1024)(128)(2,1)S(1)}, bf16[768]{0:T(1024)(128)(2,1)}, u32[]{:S(2)}) copy-start(bf16[768]{0:T(1024)(128)(2,1)} %param.40) | copy-start | bytes 4612
  130.3 24.5 %copy-start = (bf16[8,128,384]{2,1,0:T(8,128)(2,1)}, bf16[8,128,384]{2,1,0:T(8,128)(2,1)S(1)}, u32[]{:S(2)}) copy-start(bf16[8,128,384]{2,1,0:T(8,128)(2,1)S(1)} %all-to-all-done.1) | copy-start | bytes 2359300
  130.3 24.5 %all-to-all-start.2 = ((bf16[8,128,384]{2,1,0:T(8,128)(2,1)}), bf16[8,128,384]{2,1,0:T(8,128)(2,1)S(1)}, u32[]{:S(2)}, u32[]{:S(2)}) async-start(bf16[8,128,384]{2,1,0:T(8,128)(2,1)} %bitcast.138), calls=%async_computation.2 | async-start | bytes 1572864 | tf_op jit(solution)/shard_map/all_to_all | solution.py:1200
  164.9 6.1 %collective-permute-start.2 = (bf16[2,2,64,768]{3,2,1,0:T(8,128)(2,1)S(1)}, bf16[2,2,64,768]{3,2,1,0:T(8,128)(2,1)S(1)}, u32[]{:S(2)}, u32[]{:S(2)}) collective-permute-start(bf16[2,2,64,768]{3,2,1,0:T(8,128)(2,1)S(1)} %get-tuple-element.158), channel_id=1, source_target_pairs={{0,1},{1,2},{2,3},{3,4},{4,5},{5,6},{6,7},{8,9},{9,10},{10,11},{11... | collective-permute-start | bytes 1179656 | tf_op jit(solution)/shard_map/ppermute | solution.py:885
  166.5 4.6 collective-permute-start.3
  260.3 31.6 %all-to-all-start.3 = ((bf16[8,128,384]{2,1,0:T(8,128)(2,1)}), bf16[8,128,384]{2,1,0:T(8,128)(2,1)S(1)}, u32[]{:S(2)}, u32[]{:S(2)}) async-start(bf16[8,128,384]{2,1,0:T(8,128)(2,1)} %bitcast.141), calls=%async_computation.3 | async-start | bytes 1572864 | tf_op jit(solution)/shard_map/all_to_all | solution.py:1195
  267.9 231.6 %reduce-scatter.2.cloned.1.call-start = ((), (), s32[]{:S(2)}) async-start(), calls=%async_computation.9 | async-start | bytes 9732096 | tf_op jit(solution)/shard_map/reduce_scatter | solution.py:1268
  292.0 26.2 %all-to-all-start.4 = ((bf16[8,128,384]{2,1,0:T(8,128)(2,1)}), bf16[8,128,384]{2,1,0:T(8,128)(2,1)S(1)}, u32[]{:S(2)}, u32[]{:S(2)}) async-start(bf16[8,128,384]{2,1,0:T(8,128)(2,1)} %bitcast.26), calls=%async_computation.4 | async-start | bytes 1572864 | tf_op jit(solution)/shard_map/all_to_all | solution.py:1195
  319.8 45.1 %all-to-all-start.6 = ((f32[32,1,7296]{2,1,0:T(1,128)}), f32[32,1,7296]{2,1,0:T(1,128)S(1)}, u32[]{:S(2)}, u32[]{:S(2)}) async-start(f32[32,1,7296]{2,1,0:T(1,128)} %all_to_all.40), calls=%async_computation.6 | async-start | bytes 1867776 | tf_op jit(solution)/shard_map/all_to_all | solution.py:1303
  364.0 17.3 %collective-permute-start.4 = (bf16[4,4,24,3072]{3,2,1,0:T(8,128)(2,1)}, bf16[4,4,24,3072]{3,2,1,0:T(8,128)(2,1)}, u32[]{:S(2)}, u32[]{:S(2)}) collective-permute-start(bf16[4,4,24,3072]{3,2,1,0:T(8,128)(2,1)} %dynamic-slice_bitcast_fusion), channel_id=1, source_target_pairs={{0,1},{1,0},{2,3},{3,2},{4,5},{5,4},{6,7},{7,6},{8,9},{9,8},{10,11... | collective-permute-start | bytes 7077896 | tf_op jit(solution)/shard_map/ppermute | solution.py:1089
  364.9 55.5 %all-to-all-start.5 = ((bf16[8,128,768]{2,1,0:T(8,128)(2,1)}), bf16[8,128,768]{2,1,0:T(8,128)(2,1)}, u32[]{:S(2)}, u32[]{:S(2)}) async-start(bf16[8,128,768]{2,1,0:T(8,128)(2,1)} %bitcast.28), calls=%async_computation.5 | async-start | bytes 3145728 | tf_op jit(solution)/shard_map/all_to_all | solution.py:1200
  421.6 29.1 %collective-permute-start.7 = (bf16[4,24,3072]{2,1,0:T(8,128)(2,1)}, bf16[4,24,3072]{2,1,0:T(8,128)(2,1)}, u32[]{:S(2)}, u32[]{:S(2)}) collective-permute-start(bf16[4,24,3072]{2,1,0:T(8,128)(2,1)} %get-tuple-element.152), channel_id=1, source_target_pairs={{0,8},{8,0},{16,24},{24,16},{1,9},{9,1},{17,25},{25,17},{2,10},{10... | collective-permute-start | bytes 1769480 | tf_op jit(solution)/shard_map/ppermute | solution.py:1097
  423.1 29.6 %collective-permute-start.8 = (bf16[4,24,3072]{2,1,0:T(8,128)(2,1)}, bf16[4,24,3072]{2,1,0:T(8,128)(2,1)}, u32[]{:S(2)}, u32[]{:S(2)}) collective-permute-start(bf16[4,24,3072]{2,1,0:T(8,128)(2,1)} %get-tuple-element.154), channel_id=1, source_target_pairs={{0,16},{8,24},{16,0},{24,8},{1,17},{9,25},{17,1},{25,9},{2,18},{10... | collective-permute-start | bytes 1769480 | tf_op jit(solution)/shard_map/ppermute | solution.py:1097
  424.6 28.1 %collective-permute-start.9 = (bf16[4,24,3072]{2,1,0:T(8,128)(2,1)}, bf16[4,24,3072]{2,1,0:T(8,128)(2,1)}, u32[]{:S(2)}, u32[]{:S(2)}) collective-permute-start(bf16[4,24,3072]{2,1,0:T(8,128)(2,1)} %get-tuple-element.153), channel_id=1, source_target_pairs={{0,24},{8,16},{16,8},{24,0},{1,25},{9,17},{17,9},{25,1},{2,26},{10... | collective-permute-start | bytes 1769480 | tf_op jit(solution)/shard_map/ppermute | solution.py:1097
  426.2 3.4 collective-permute-start.5
  427.5 3.3 collective-permute-start.6
  454.6 14.0 %collective-permute-start.10 = (bf16[24,3072]{1,0:T(8,128)(2,1)S(1)}, bf16[24,3072]{1,0:T(8,128)(2,1)S(1)}, u32[]{:S(2)}, u32[]{:S(2)}) collective-permute-start(bf16[24,3072]{1,0:T(8,128)(2,1)S(1)} %get-tuple-element.165), channel_id=1, source_target_pairs={{0,2},{1,3},{2,0},{3,1},{4,6},{5,7},{6,4},{7,5},{8,10},{9,11},{10,... | collective-permute-start | bytes 442376 | tf_op jit(solution)/shard_map/ppermute | solution.py:1097
  456.4 14.9 %collective-permute-start.11 = (bf16[24,3072]{1,0:T(8,128)(2,1)S(1)}, bf16[24,3072]{1,0:T(8,128)(2,1)S(1)}, u32[]{:S(2)}, u32[]{:S(2)}) collective-permute-start(bf16[24,3072]{1,0:T(8,128)(2,1)S(1)} %get-tuple-element.167), channel_id=1, source_target_pairs={{0,4},{1,5},{2,6},{3,7},{4,0},{5,1},{6,2},{7,3},{8,12},{9,13},{10,... | collective-permute-start | bytes 442376 | tf_op jit(solution)/shard_map/ppermute | solution.py:1097
  460.3 11.0 %collective-permute-start.12 = (bf16[24,3072]{1,0:T(8,128)(2,1)S(1)}, bf16[24,3072]{1,0:T(8,128)(2,1)S(1)}, u32[]{:S(2)}, u32[]{:S(2)}) collective-permute-start(bf16[24,3072]{1,0:T(8,128)(2,1)S(1)} %get-tuple-element.166), channel_id=1, source_target_pairs={{0,6},{1,7},{2,4},{3,5},{4,2},{5,3},{6,0},{7,1},{8,14},{9,15},{10,... | collective-permute-start | bytes 442376 | tf_op jit(solution)/shard_map/ppermute | solution.py:1097
  461.4 25.0 %all-to-all-start.7 = ((f32[32,1,3456]{2,1,0:T(1,128)}), f32[32,1,3456]{2,1,0:T(1,128)S(1)}, u32[]{:S(2)}, u32[]{:S(2)}) async-start(f32[32,1,3456]{2,1,0:T(1,128)} %all_to_all.43), calls=%async_computation.7 | async-start | bytes 884736 | tf_op jit(solution)/shard_map/all_to_all | solution.py:1369
  (29 other events, 213.4 us)
Sparse Core Ops, SparseCore 0:
  290.6 151.5 reduce-scatter.1

commit v3 on v2

--- a/solution.py
+++ b/solution.py
@@ -13,7 +13,6 @@
 LANES = 128
 COLUMN_PARTS = 4
 CHUNKS = 2
-VMEM_BYTES = 60 * 1024 * 1024
 
 highest = lax.Precision.HIGHEST
 epsilon = 1e-06
@@ -22,8 +21,8 @@
 both = ("items", "strips")
 
 
-def params():
-    return pltpu.CompilerParams(vmem_limit_bytes=VMEM_BYTES)
+def params(mebibytes):
+    return pltpu.CompilerParams(vmem_limit_bytes=mebibytes * 1024 * 1024)
 
 
 def cost(flops, moved, exps=0):
@@ -67,27 +66,42 @@
 def put_wide(ref, row, cells):
     sub = cells.shape[1]
     place = lax.broadcasted_iota(jnp.int32, cells.shape[1:], 0)
+    last = cells[COLUMN_PARTS - 1].astype(single)
+    first = cells[0].astype(single)
     ref[row, 1 : COLUMN_PARTS + 1] = cells
-    ref[row, 0] = jnp.where(place == 0, 0.0, pltpu.roll(cells[COLUMN_PARTS - 1], 1, 0))
+    ref[row, 0] = jnp.where(place == 0, 0.0, pltpu.roll(last, 1, 0)).astype(ref.dtype)
     ref[row, COLUMN_PARTS + 1] = jnp.where(
-        place == sub - 1, 0.0, pltpu.roll(cells[0], sub - 1, 0)
-    )
-
-
-def conv_row(ref, row, taps, start):
-    total = start
+        place == sub - 1, 0.0, pltpu.roll(first, sub - 1, 0)
+    ).astype(ref.dtype)
+
+
+def put_part(ref, row, j, cells):
+    sub = cells.shape[0]
+    place = lax.broadcasted_iota(jnp.int32, cells.shape, 0)
+    ref[row, j + 1] = cells
+    if j == COLUMN_PARTS - 1:
+        ref[row, 0] = jnp.where(place == 0, 0.0, pltpu.roll(cells, 1, 0))
+    if j == 0:
+        ref[row, COLUMN_PARTS + 1] = jnp.where(place == sub - 1, 0.0, pltpu.roll(cells, sub - 1, 0))
+
+
+def conv_low(ref, row, taps):
+    total = None
     for i in range(3):
-        for j in range(3):
-            total = total + taps[3 * i + j] * ref[row + i, j : j + COLUMN_PARTS]
+        line = [taps[3 * i + j] * ref[row + i, j : j + COLUMN_PARTS] for j in range(3)]
+        line = (line[0] + line[1]) + line[2]
+        total = line if total is None else total + line
     return total
 
 
 def conv_back_row(ref, row, taps):
     total = None
     for i in range(3):
-        for j in range(3):
-            term = taps[3 * i + j] * ref[row + 2 - i, 2 - j : 2 - j + COLUMN_PARTS]
-            total = term if total is None else total + term
+        line = [
+            taps[3 * i + j] * ref[row + 2 - i, 2 - j : 2 - j + COLUMN_PARTS] for j in range(3)
+        ]
+        line = (line[0] + line[1]) + line[2]
+        total = line if total is None else total + line
     return total
 
 
@@ -101,20 +115,22 @@
     scale = 1.0 + scale_ref[0]
     shift = shift_ref[0]
 
-    def fill(row, raw, keep):
+    def fill(row, raw, keep, kept_row=None):
         cells = dot(order, raw)
-        normed = (norm_parts(cells)[0] * scale + shift) * keep
-        low = normed.astype(bfloat)
-        normed_ref[0, row] = low
-        put_wide(wide, row, low.astype(single).reshape(COLUMN_PARTS, sub, features))
-        return cells
+        if kept_row is not None:
+            kept_ref[0, kept_row] = cells.astype(bfloat)
+        for j in range(COLUMN_PARTS):
+            line = slice(j * sub, (j + 1) * sub)
+            normed = norm_parts(cells[line])[0] * scale + shift
+            low = (normed if keep is None else normed * keep).astype(bfloat)
+            normed_ref[0, row, line] = low
+            put_part(wide, row, j, low.astype(single))
 
     fill(0, top_ref[0, 0], edge_ref[0])
     fill(rows + 1, bottom_ref[0, 0], edge_ref[1])
 
-    @pl.loop(0, rows)
-    def _(row):
-        kept_ref[0, row] = fill(row + 1, x_ref[0, row], 1.0).astype(bfloat)
+    for row in range(rows):
+        fill(row + 1, x_ref[0, row], None, row)
 
     taps = [taps_ref[t : t + 1] for t in range(9)]
     bias = bias_ref[...]
@@ -162,7 +178,7 @@
             jax.ShapeDtypeStruct((count, rows, columns, features), bfloat),
         ],
         scratch_shapes=[pltpu.VMEM((rows + 2, COLUMN_PARTS + 2, sub, features), single)],
-        compiler_params=params(),
+        compiler_params=params(18),
         cost_estimate=cost(count * rows * columns * features * 150, count * rows * columns * features * 8),
         name="front",
     )(edge, latents, top, bottom, scale, shift, taps, bias)
@@ -186,7 +202,10 @@
         branch_ref[0, row + 1] = grad
         return total + jnp.sum(grad.astype(single), axis=0, keepdims=True)
 
-    bias_ref[0] = lax.fori_loop(0, rows, step, jnp.zeros((1, features), single))
+    total = jnp.zeros((1, features), single)
+    for row in range(rows):
+        total = step(row, total)
+    bias_ref[0] = total
 
 
 def upstream_parts(cotangent, top, bottom, gate):
@@ -203,13 +222,13 @@
             jax.ShapeDtypeStruct((count, rows + 2, columns, features), bfloat),
             jax.ShapeDtypeStruct((count, 1, features), single),
         ],
-        compiler_params=params(),
+        compiler_params=params(14),
         cost_estimate=cost(count * rows * columns * features * 130, count * rows * columns * features * 6),
         name="upstream",
     )(cotangent, top, bottom, gate)
 
 
-QUERY_STEP = 512
+QUERY_STEP = 1024
 QUERY_STEP_BACK = 256
 
 
@@ -256,7 +275,7 @@
         + [weight(0), weight(1), weight(2), bias(0), bias(1)],
         out_specs=[column] * 4 + [pl.BlockSpec((1, 2, tokens), lambda h: (h, 0, 0))],
         out_shape=[lows] * 4 + [jax.ShapeDtypeStruct((pairs, 2, tokens), single)],
-        compiler_params=params(),
+        compiler_params=params(60),
         cost_estimate=cost(
             6 * tokens * features * width + 16 * tokens * tokens * width,
             2 * tokens * features + 8 * tokens * width + 6 * features * width,
@@ -317,7 +336,7 @@
         out_specs=[column] * 3,
         out_shape=[lows] * 3,
         scratch_shapes=[pltpu.VMEM((tokens, LANES), single)] * 2,
-        compiler_params=params(),
+        compiler_params=params(60),
         cost_estimate=cost(
             40 * tokens * tokens * width, 16 * tokens * width, 2 * pairs * tokens * tokens
         ),
@@ -350,7 +369,7 @@
         + [pl.BlockSpec(weight.shape, lambda t: (0, 0))],
         out_specs=pl.BlockSpec((step, features), lambda t: (t, 0)),
         out_shape=jax.ShapeDtypeStruct((tokens, features), bfloat),
-        compiler_params=params(),
+        compiler_params=params(60),
         cost_estimate=cost(2 * tokens * features * weight.shape[1], 2 * tokens * features * 4),
         name="regroup",
     )(*parts, weight)
@@ -400,7 +419,7 @@
             jax.ShapeDtypeStruct((features, 3 * third + other.shape[1]), bfloat),
             jax.ShapeDtypeStruct((8, 2 * third), single),
         ],
-        compiler_params=params(),
+        compiler_params=params(60),
         cost_estimate=cost(6 * tokens * features * third, 2 * tokens * features * 5),
         name="input_grad",
     )(x, other, *parts)
@@ -411,7 +430,7 @@
 ):
     mixed_refs = refs[:parts]
     weight_ref, bias_ref, x_ref, gate_ref, scale_ref, shift_ref = refs[parts : parts + 6]
-    attended_ref, middle_ref, normed_ref, grouped = refs[parts + 6 :]
+    attended_ref, middle_ref, normed_ref, first_ref, last_ref, grouped = refs[parts + 6 :]
     rows, columns, features = x_ref.shape[1:]
     sub = columns // COLUMN_PARTS
     quarter = rows * columns // 4
@@ -426,21 +445,23 @@
     scale = 1.0 + scale_ref[0]
     shift = shift_ref[0]
 
-    @pl.loop(0, rows // 2)
-    def _(pair):
+    for pair in range(rows // 2):
         for a in range(2):
             row = pair * 2 + a
-            cells = jnp.concatenate(
-                [
-                    grouped[2 * a + j % 2, pl.ds(pl.multiple_of((pair * 2 + j // 2) * sub, sub), sub)]
-                    for j in range(COLUMN_PARTS)
-                ],
-                axis=0,
-            )
-            attended_ref[0, row] = cells
-            middle = x_ref[0, row].astype(single) + gate * cells
-            middle_ref[0, row] = middle
-            normed_ref[0, row] = (norm_parts(middle)[0] * scale + shift).astype(bfloat)
+            for j in range(COLUMN_PARTS):
+                line = slice(j * sub, (j + 1) * sub)
+                cells = grouped[
+                    2 * a + j % 2, pl.ds((pair * 2 + j // 2) * sub, sub)
+                ]
+                attended_ref[0, row, line] = cells
+                middle = x_ref[0, row, line].astype(single) + gate * cells
+                middle_ref[0, row, line] = middle
+                low = (norm_parts(middle)[0] * scale + shift).astype(bfloat)
+                normed_ref[0, row, line] = low
+                if row < 2:
+                    first_ref[0, row, line] = low
+                if row >= rows - 2:
+                    last_ref[0, row - rows + 2, line] = low
 
 
 def middle_part(mixed, weight, bias, kept, gate, scale, shift):
@@ -459,14 +480,16 @@
             pl.BlockSpec((1, features), lambda l: (0, 0)),
             image, vector, vector, vector,
         ],
-        out_specs=[image] * 3,
+        out_specs=[image] * 3
+        + [pl.BlockSpec((1, 2, columns, features), lambda l: (l, 0, 0, 0))] * 2,
         out_shape=[
             jax.ShapeDtypeStruct(kept.shape, single),
             jax.ShapeDtypeStruct(kept.shape, single),
             jax.ShapeDtypeStruct(kept.shape, bfloat),
-        ],
+        ]
+        + [jax.ShapeDtypeStruct((count, 2, columns, features), bfloat)] * 2,
         scratch_shapes=[pltpu.VMEM((4, quarter, features), single)],
-        compiler_params=params(),
+        compiler_params=params(60),
         cost_estimate=cost(2 * kept.size * features, 14 * kept.size),
         name="middle",
     )(*mixed, weight, bias, kept, gate, scale, shift)
@@ -489,15 +512,15 @@
         ],
         out_specs=pl.BlockSpec((lines, features), lambda s: (0, s)),
         out_shape=jax.ShapeDtypeStruct((lines, hidden), bfloat),
-        compiler_params=params(),
+        compiler_params=params(60),
         cost_estimate=cost(2 * lines * features * hidden, 2 * lines * (features + hidden)),
         name="feed_upstream",
     )(db.reshape(lines, features), ws)
 
 
 def feed_kernel(
-    edge_ref, nb_ref, top_ref, bottom_ref, d_act_ref, we_ref, be_ref, ws_ref, taps_ref, bm_ref,
-    branch_ref, e_ref, act_ref, d_hid_ref, small_ref,
+    edge_ref, nb_ref, top_ref, bottom_ref, d_act_ref, we_ref, be_ref, taps_ref, bm_ref,
+    act_ref, d_hid_ref, small_ref,
     nb_wide, hidden, wide, d_wide,
 ):
     count, rows, columns, features = nb_ref.shape
@@ -517,8 +540,6 @@
             nb_wide[(l + 1) * tall - 2 * columns : (l + 1) * tall] = bottom_ref[l].reshape(
                 2 * columns, features
             )
-        branch_ref[...] = jnp.zeros_like(branch_ref)
-        e_ref[...] = jnp.zeros_like(e_ref)
 
     hidden[...] = (dot(nb_wide[...], we_ref[...]) + be_ref[...]).astype(bfloat)
     small_ref[...] = jnp.zeros_like(small_ref)
@@ -534,15 +555,14 @@
         bias = bm_ref[:, at]
         for row in range(rows + 4):
             cells = hidden[pl.ds(pl.multiple_of(l * tall + row * columns, columns), columns), at]
-            cells = cells.astype(single)
             if row < 2:
-                cells = cells * edge_ref[0]
+                cells = cells * edge_ref[0].astype(bfloat)
             if row >= rows + 2:
-                cells = cells * edge_ref[1]
+                cells = cells * edge_ref[1].astype(bfloat)
             put_wide(wide, row, cells.reshape(COLUMN_PARTS, sub, LANES))
-        start = jnp.zeros((COLUMN_PARTS, sub, LANES), single) + bias
+        taps = [(t + jnp.zeros((sub, LANES), single)).astype(bfloat) for t in taps]
         for row in range(rows + 2):
-            v = conv_row(wide, row, taps, start)
+            v = conv_low(wide, row, taps).astype(single) + bias
             cube = (v * v) * c1
             half = 0.5 * jnp.tanh(v * (cube + c0)) + 0.5
             gelu = v * half
@@ -553,7 +573,7 @@
                 ] = gelu.reshape(columns, LANES).astype(bfloat)
             grad = d_act_ref[pl.ds(pl.multiple_of(l * mid + row * columns, columns), columns), at]
             grad = grad.astype(single).reshape(COLUMN_PARTS, sub, LANES) * slope
-            put_wide(d_wide, row, grad.astype(bfloat).astype(single))
+            put_wide(d_wide, row, grad.astype(bfloat))
         sums = [jnp.zeros((sub, LANES), single) for _ in range(11)]
         for row in range(rows):
             d_in = conv_back_row(d_wide, row, taps).astype(bfloat)
@@ -563,19 +583,16 @@
             center = d_wide[row + 1, 1 : COLUMN_PARTS + 1]
             for i in range(3):
                 for j in range(3):
-                    sums[3 * i + j] += jnp.sum(
-                        center * wide[row + 1 + i, j : j + COLUMN_PARTS], axis=0
-                    )
-            sums[9] += jnp.sum(center, axis=0)
+                    term = center * wide[row + 1 + i, j : j + COLUMN_PARTS]
+                    term = (term[0] + term[1]) + (term[2] + term[3])
+                    sums[3 * i + j] += term.astype(single)
+            sums[9] += jnp.sum(center.astype(single), axis=0)
             sums[10] += jnp.sum(d_in.astype(single), axis=0)
         for t in range(11):
             small_ref[t : t + 1, at] += jnp.sum(sums[t], axis=0, keepdims=True)
 
-    branch_ref[...] += dot(act_ref[...], ws_ref[...])
-    e_ref[...] += dot_nt(d_hid_ref[...], we_ref[...])
-
-
-def feed_forward(edge, nb, top, bottom, d_act, we, be, taps, bm, ws):
+
+def feed_forward(edge, nb, top, bottom, d_act, we, be, taps, bm):
     count, rows, columns, features = nb.shape
     hidden = we.shape[1]
     block = features
@@ -586,21 +603,16 @@
     sub = columns // COLUMN_PARTS
     whole = lambda a: pl.BlockSpec(a.shape, lambda s: (0,) * a.ndim)
     column = lambda n: pl.BlockSpec((n, block), lambda s: (0, s))
-    flat = pl.BlockSpec((tokens, features), lambda s: (0, 0))
     return pl.pallas_call(
         feed_kernel,
         grid=(steps,),
         in_specs=[
             pl.BlockSpec(memory_space=pltpu.SMEM),
             whole(nb), whole(top), whole(bottom),
-            column(mid), column(features), column(1),
-            pl.BlockSpec((block, features), lambda s: (s, 0)),
-            column(16), column(1),
-        ],
-        out_specs=[flat, flat, column(tokens), column(tokens), column(16)],
+            column(mid), column(features), column(1), column(16), column(1),
+        ],
+        out_specs=[column(tokens), column(tokens), column(16)],
         out_shape=[
-            jax.ShapeDtypeStruct((tokens, features), single),
-            jax.ShapeDtypeStruct((tokens, features), single),
             jax.ShapeDtypeStruct((tokens, hidden), bfloat),
             jax.ShapeDtypeStruct((tokens, hidden), bfloat),
             jax.ShapeDtypeStruct((16, hidden), single),
@@ -608,37 +620,76 @@
         scratch_shapes=[
             pltpu.VMEM((tall, features), bfloat),
             pltpu.VMEM((tall, block), bfloat),
-            pltpu.VMEM((rows + 4, COLUMN_PARTS + 2, sub, LANES), single),
-            pltpu.VMEM((rows + 2, COLUMN_PARTS + 2, sub, LANES), single),
-        ],
-        compiler_params=params(),
+            pltpu.VMEM((rows + 4, COLUMN_PARTS + 2, sub, LANES), bfloat),
+            pltpu.VMEM((rows + 2, COLUMN_PARTS + 2, sub, LANES), bfloat),
+        ],
+        compiler_params=params(60),
         cost_estimate=cost(
-            2 * features * hidden * (tall + 2 * tokens),
-            8 * tokens * features + 8 * features * hidden + 6 * tokens * hidden,
+            2 * features * hidden * tall,
+            8 * tokens * features + 4 * features * hidden + 6 * tokens * hidden,
             mid * hidden,
         ),
         name="feed_forward",
-    )(edge, nb, top, bottom, d_act, we, be, ws, taps, bm)
-
-
-def feed_grads_kernel(act_ref, d_hid_ref, nb_ref, db_ref, gws_ref, gwe_ref, db_own):
+    )(edge, nb, top, bottom, d_act, we, be, taps, bm)
+
+
+def feed_grads_kernel(
+    act_ref, d_hid_ref, nb_ref, db_ref, out_ref, db_own, shrink_s, expand_s, shrink_sem, expand_sem
+):
     count, rows, columns, features = nb_ref.shape
     own = rows * columns
-
-    @pl.when(pl.program_id(0) == 0)
+    step = pl.program_id(0)
+    steps = pl.num_programs(0)
+    some, slots, unit = shrink_s.shape[:3]
+
+    @pl.when(step == 0)
     def _():
         for l in range(count):
             db_own[l * own : (l + 1) * own] = db_ref[l, 1 : rows + 1].reshape(own, features)
 
-    gws_ref[...] = dot_tn(act_ref[...], db_own[...]).astype(bfloat)
-    gwe_ref[0] = dot_tn(nb_ref[...].reshape(count * own, features), d_hid_ref[...]).astype(bfloat)
-
-
-def feed_grads(act, d_hid, nb, db):
+    def copies(s):
+        return (
+            pltpu.make_async_copy(
+                shrink_s, out_ref.at[pl.ds(s * some, some), pl.ds(0, slots)], shrink_sem
+            ),
+            pltpu.make_async_copy(expand_s, out_ref.at[:, slots + s], expand_sem),
+        )
+
+    shrink = dot_tn(act_ref[...], db_own[...])
+    expand = dot_tn(nb_ref[...].reshape(count * own, features), d_hid_ref[...])
+
+    @pl.when(step > 0)
+    def _():
+        for c in copies(step - 1):
+            c.wait()
+
+    shrink_s[...] = shrink.reshape(shrink_s.shape).astype(bfloat)
+    expand_s[...] = expand.reshape(expand_s.shape).astype(bfloat)
+    for c in copies(step):
+        c.start()
+
+    @pl.when(step == steps - 1)
+    def _():
+        for c in copies(step):
+            c.wait()
+
+
+def feed_grads(act, d_hid, nb, db, devices):
     count, rows, columns, features = nb.shape
     tokens, hidden = act.shape
     block = features
     steps = hidden // block
+    unit = features // devices
+    if unit % 8:
+        shrink = dot_tn(act, db[:, 1:-1].reshape(tokens, features))
+        expand = dot_tn(nb.reshape(tokens, features), d_hid)
+        return jnp.concatenate(
+            [
+                shrink.reshape(devices, steps, unit, features),
+                expand.reshape(devices, unit, steps, features).transpose(0, 2, 1, 3),
+            ],
+            axis=1,
+        ).astype(bfloat)
     whole = lambda a: pl.BlockSpec(a.shape, lambda s: (0,) * a.ndim)
     return pl.pallas_call(
         feed_grads_kernel,
@@ -648,30 +699,33 @@
             pl.BlockSpec((tokens, block), lambda s: (0, s)),
             whole(nb), whole(db),
         ],
-        out_specs=[
-            pl.BlockSpec((block, features), lambda s: (s, 0)),
-            pl.BlockSpec((1, features, block), lambda s: (s, 0, 0)),
-        ],
-        out_shape=[
-            jax.ShapeDtypeStruct((hidden, features), bfloat),
-            jax.ShapeDtypeStruct((steps, features, block), bfloat),
-        ],
-        scratch_shapes=[pltpu.VMEM((tokens, features), bfloat)],
-        compiler_params=params(),
+        out_specs=pl.BlockSpec(memory_space=pl.ANY),
+        out_shape=jax.ShapeDtypeStruct((devices, 2 * steps, unit, features), bfloat),
+        scratch_shapes=[
+            pltpu.VMEM((tokens, features), bfloat),
+            pltpu.VMEM((devices // steps, steps, unit, features), bfloat),
+            pltpu.VMEM((devices, unit, features), bfloat),
+            pltpu.SemaphoreType.DMA,
+            pltpu.SemaphoreType.DMA,
+        ],
+        compiler_params=params(60),
         cost_estimate=cost(4 * features * hidden * tokens, 8 * features * hidden + 4 * tokens * hidden),
         name="feed_grads",
     )(act, d_hid, nb, db)
 
 
+TURN_ROWS = 4
+
+
 def turn_kernel(parts, *refs):
     (
-        branch_ref, e_ref, middle_ref, attended_ref, g_ref,
-        gate_b_ref, scale_ref, gate_a_ref, bias_ref, weight_ref,
-    ) = refs[:10]
-    mixed_refs = refs[10 : 10 + parts]
-    result_ref, d_middle_ref = refs[10 + parts : 12 + parts]
-    d_mixed_refs = refs[12 + parts : 12 + 2 * parts]
-    gw_ref, sums_ref, gw_sum, grouped = refs[12 + 2 * parts :]
+        act_ref, d_hid_ref, middle_ref, attended_ref, g_ref,
+        gate_b_ref, scale_ref, gate_a_ref, bias_ref, weight_ref, ws_ref, we_ref,
+    ) = refs[:12]
+    mixed_refs = refs[12 : 12 + parts]
+    result_ref, d_middle_ref = refs[12 + parts : 14 + parts]
+    d_mixed_refs = refs[14 + parts : 14 + 2 * parts]
+    gw_ref, sums_ref, gw_sum, grouped, branch_s, e_s, sums = refs[14 + 2 * parts :]
     rows, columns, features = g_ref.shape[1:]
     sub = columns // COLUMN_PARTS
     quarter = rows * columns // 4
@@ -679,34 +733,44 @@
     gate_b = gate_b_ref[0]
     scale = 1.0 + scale_ref[0]
     gate_a = gate_a_ref[0]
-
-    def step(pair, sums):
+    first = (pl.program_id(0) == 0) & (pl.program_id(1) == 0)
+    last = (pl.program_id(0) == pl.num_programs(0) - 1) & (
+        pl.program_id(1) == pl.num_programs(1) - 1
+    )
+
+    branch_s[...] = dot(act_ref[...], ws_ref[...]) + bias_ref[...]
+    e_s[...] = dot_nt(d_hid_ref[...], we_ref[...])
+
+    @pl.when(pl.program_id(1) == 0)
+    def _():
+        sums[...] = jnp.zeros_like(sums)
+
+    for pair in range(rows // 2):
         for a in range(2):
             row = pair * 2 + a
-            at = pl.ds(pl.multiple_of(row * columns, columns), columns)
-            branch = branch_ref[at] + bias_ref[...]
-            middle = middle_ref[0, row]
-            g = g_ref[0, row].astype(single)
-            result = (middle + gate_b * branch).astype(bfloat)
-            result_ref[0, row] = dot(back, result).astype(bfloat)
-            normed, inverse = norm_parts(middle)
-            e = e_ref[at]
-            d_middle = g + norm_back(normed, inverse, e * scale)
-            d_middle_ref[0, row] = d_middle
-            low = (d_middle * gate_a).astype(bfloat)
+            lows = []
             for j in range(COLUMN_PARTS):
+                line = slice(j * sub, (j + 1) * sub)
+                at = pl.ds(row * columns + j * sub, sub)
+                branch = branch_s[at]
+                middle = middle_ref[0, row, line]
+                g = g_ref[0, row, line].astype(single)
+                lows.append((middle + gate_b * branch).astype(bfloat))
+                normed, inverse = norm_parts(middle)
+                e = e_s[at]
+                d_middle = g + norm_back(normed, inverse, e * scale)
+                d_middle_ref[0, row, line] = d_middle
+                low = (d_middle * gate_a).astype(bfloat)
                 grouped[
-                    2 * a + j % 2, pl.ds(pl.multiple_of((pair * 2 + j // 2) * sub, sub), sub)
-                ] = low[j * sub : (j + 1) * sub]
-            terms = (g * branch, e, e * normed, d_middle * attended_ref[0, row], low.astype(single))
-            sums = tuple(
-                s + jnp.sum(t.reshape(columns // 8, 8, features), axis=0) for s, t in zip(sums, terms)
-            )
-        return sums
-
-    sums = lax.fori_loop(
-        0, rows // 2, step, tuple(jnp.zeros((8, features), single) for _ in range(5))
-    )
+                    2 * a + j % 2, pl.ds((pair * 2 + j // 2) * sub, sub)
+                ] = low
+                terms = (
+                    g * branch, e, e * normed, d_middle * attended_ref[0, row, line], low.astype(single)
+                )
+                for t, term in enumerate(terms):
+                    sums[t] += jnp.sum(term.reshape(sub // 8, 8, features), axis=0)
+            result_ref[0, row] = dot(back, jnp.concatenate(lows, axis=0)).astype(bfloat)
+
     for t in range(5):
         sums_ref[0, t : t + 1] = jnp.sum(sums[t], axis=0, keepdims=True)
     sums_ref[0, 5:8] = jnp.zeros((3, features), single)
@@ -718,37 +782,46 @@
         d_ref[0] = dot_nt(grad, weight_ref[piece]).astype(bfloat).reshape(4, quarter, width)
         part = dot_tn(mixed_ref[0].reshape(4 * quarter, width), grad)
 
-        @pl.when(pl.program_id(0) == 0)
+        @pl.when(first)
         def _():
             gw_sum[piece] = part
 
-        @pl.when(pl.program_id(0) > 0)
+        @pl.when(jnp.logical_not(first))
         def _():
             gw_sum[piece] += part
 
         at += width
 
-    @pl.when(pl.program_id(0) == pl.num_programs(0) - 1)
+    @pl.when(last)
     def _():
         gw_ref[...] = gw_sum[...].astype(bfloat)
 
 
-def turn(branch, e, middle, attended, g, gate_b, scale, gate_a, bias, weight, mixed):
+def turn(
+    act, d_hid, middle, attended, g, gate_b, scale, gate_a, bias, weight, shrink, expand, mixed
+):
     count, rows, columns, features = g.shape
-    quarter = rows * columns // 4
-    own = rows * columns
-    image = pl.BlockSpec((1, rows, columns, features), lambda l: (l, 0, 0, 0))
-    flat = pl.BlockSpec((own, features), lambda l: (l, 0))
-    vector = pl.BlockSpec((1, 1, features), lambda l: (l, 0, 0))
-    groups = [pl.BlockSpec((1, 4, quarter, m.shape[-1]), lambda l: (l, 0, 0, 0)) for m in mixed]
-    square = pl.BlockSpec((features, features), lambda l: (0, 0))
+    hidden = act.shape[1]
+    step = min(TURN_ROWS, rows)
+    steps = rows // step
+    quarter = step * columns // 4
+    image = pl.BlockSpec((1, step, columns, features), lambda l, r: (l, r, 0, 0))
+    flat = pl.BlockSpec((step * columns, hidden), lambda l, r: (l * steps + r, 0))
+    vector = pl.BlockSpec((1, 1, features), lambda l, r: (l, 0, 0))
+    groups = [
+        pl.BlockSpec((1, 4, quarter, m.shape[-1]), lambda l, r: (l, 0, r, 0)) for m in mixed
+    ]
+    whole = lambda a: pl.BlockSpec(a.shape, lambda l, r: (0,) * a.ndim)
+    square = pl.BlockSpec((features, features), lambda l, r: (0, 0))
     return pl.pallas_call(
         partial(turn_kernel, len(mixed)),
-        grid=(count,),
+        grid=(count, steps),
         in_specs=[flat, flat, image, image, image, vector, vector, vector]
-        + [pl.BlockSpec((1, features), lambda l: (0, 0)), square]
+        + [whole(bias), square, whole(shrink), whole(expand)]
         + groups,
-        out_specs=[image, image] + groups + [square, pl.BlockSpec((1, 8, features), lambda l: (l, 0, 0))],
+        out_specs=[image, image]
+        + groups
+        + [square, pl.BlockSpec((1, 8, features), lambda l, r: (l, 0, 0))],
         out_shape=[
             jax.ShapeDtypeStruct(g.shape, bfloat),
             jax.ShapeDtypeStruct(g.shape, single),
@@ -761,11 +834,14 @@
         scratch_shapes=[
             pltpu.VMEM((features, features), single),
             pltpu.VMEM((4, quarter, features), bfloat),
-        ],
-        compiler_params=params(),
-        cost_estimate=cost(4 * g.size * features, 26 * g.size),
+            pltpu.VMEM((step * columns, features), single),
+            pltpu.VMEM((step * columns, features), single),
+            pltpu.VMEM((5, 8, features), single),
+        ],
+        compiler_params=params(60),
+        cost_estimate=cost(4 * g.size * (features + hidden), 20 * g.size + 4 * act.size),
         name="turn",
-    )(branch, e, middle, attended, g, gate_b, scale, gate_a, bias, weight, *mixed)
+    )(act, d_hid, middle, attended, g, gate_b, scale, gate_a, bias, weight, shrink, expand, *mixed)
 
 
 def final_kernel(
@@ -800,7 +876,8 @@
 
     @pl.loop(0, rows + 2)
     def _(row):
-        put_wide(wide, row, normed_ref[0, row].astype(single).reshape(COLUMN_PARTS, sub, features))
+        for j in range(COLUMN_PARTS):
+            put_part(wide, row, j, normed_ref[0, row, j * sub : (j + 1) * sub].astype(single))
 
     @pl.when(pl.program_id(0) == 0)
     def _():
@@ -833,16 +910,23 @@
             taps_out_ref[t : t + 1, at] += jnp.sum(sums[t], axis=0, keepdims=True)
 
     def last(row, sums):
-        cells = d_normed[row, 1 : COLUMN_PARTS + 1].reshape(columns, features)
-        normed, inverse = norm_parts(x_ref[0, row].astype(single))
-        grad = d_middle_ref[0, row] + norm_back(normed, inverse, cells * scale)
-        out_ref[0, row] = dot(back, grad.astype(bfloat)).astype(bfloat)
-        return tuple(
-            s + jnp.sum(t.reshape(columns // 8, 8, features), axis=0)
-            for s, t in zip(sums, (cells, cells * normed))
-        )
-
-    sums = lax.fori_loop(0, rows, last, tuple(jnp.zeros((8, features), single) for _ in range(2)))
+        lows = []
+        for j in range(COLUMN_PARTS):
+            line = slice(j * sub, (j + 1) * sub)
+            cells = d_normed[row, j + 1]
+            normed, inverse = norm_parts(x_ref[0, row, line].astype(single))
+            grad = d_middle_ref[0, row, line] + norm_back(normed, inverse, cells * scale)
+            lows.append(grad.astype(bfloat))
+            sums = tuple(
+                s + jnp.sum(t.reshape(sub // 8, 8, features), axis=0)
+                for s, t in zip(sums, (cells, cells * normed))
+            )
+        out_ref[0, row] = dot(back, jnp.concatenate(lows, axis=0)).astype(bfloat)
+        return sums
+
+    sums = tuple(jnp.zeros((8, features), single) for _ in range(2))
+    for row in range(rows):
+        sums = last(row, sums)
     for t in range(2):
         sums_ref[0, t : t + 1] = jnp.sum(sums[t], axis=0, keepdims=True)
     sums_ref[0, 2:8] = jnp.zeros((6, features), single)
@@ -874,7 +958,7 @@
             jax.ShapeDtypeStruct((count, 8, features), single),
         ],
         scratch_shapes=[pltpu.VMEM((rows + 2, COLUMN_PARTS + 2, sub, features), single)] * 2,
-        compiler_params=params(),
+        compiler_params=params(60),
         cost_estimate=cost(kept.size * 180, kept.size * 12),
         name="final",
     )(d_reduced, top, bottom, normed, kept, d_middle, scale, taps)
@@ -959,7 +1043,7 @@
         out_specs=pl.BlockSpec((1, n, features), lambda s: (s, 0, 0)),
         out_shape=jax.ShapeDtypeStruct((6, n, features), single),
         scratch_shapes=[pltpu.VMEM((n, features), single)],
-        compiler_params=params(),
+        compiler_params=params(16),
         cost_estimate=cost(50 * n * ada.size, 2 * ada.size),
         name="modulate",
     )(sinus, labels, *weights, ada, ada_bias)
@@ -986,7 +1070,9 @@
     for item in range(ref.shape[0]):
         for l in range(count):
             at = l * kinds * features
-            lines.append(jnp.sum(ref[item, :, at : at + kinds * features], axis=0, keepdims=True))
+            lines.append(jnp.sum(
+                    ref[item, :, at : at + kinds * features].astype(single), axis=0, keepdims=True
+                ))
     return jnp.concatenate(lines, axis=0)
 
 
@@ -1025,15 +1111,15 @@
         + [whole(a) for a in (parts, sinus, labels) + weights + (ada,)],
         out_specs=[whole(a) for a in shapes],
         out_shape=shapes,
-        compiler_params=params(),
+        compiler_params=params(28),
         cost_estimate=cost(50 * n * ada.size, 2 * ada.size),
         name="early_condition",
     )(me, parts, sinus, labels, *weights, ada)
 
 
 def late_kernel(
-    count, me_ref, parts_ref, before_ref, cond_ref, d_active_ref, sinus_ref, label_ref,
-    wo_ref, ada_ref,
+    count, me_ref, parts_ref, before_ref, cond_ref, d_active_ref, ada_early_ref, d_mod_early_ref,
+    sinus_ref, label_ref, wo_ref, ada_ref,
     ada_out_ref, d_mod_ref, table_out_ref, wo_out_ref, wi_out_ref, d_cond_ref, d_before_ref,
 ):
     features = wo_ref.shape[0]
@@ -1044,8 +1130,10 @@
     d_cond = d_active * silu_slope(cond)
     d_before = exact(d_cond, wo_ref[...], nt=True) * silu_slope(before)
     size = ada_out_ref.shape[0]
-    ada_out_ref[...] = exact_small(own_rows(me_ref, silu(cond), size), d_mod)
-    d_mod_ref[...] = jnp.sum(d_mod, axis=0, keepdims=True)
+    ada_out_ref[:, : 2 * features] = exact_small(own_rows(me_ref, silu(cond), size), d_mod)
+    ada_out_ref[:, 2 * features :] = ada_early_ref[...]
+    d_mod_ref[:, : 2 * features] = jnp.sum(d_mod, axis=0, keepdims=True)
+    d_mod_ref[:, 2 * features :] = d_mod_early_ref[...]
     onehot = label_rows(label_ref[...], table_out_ref.shape[1]).astype(single)
     table_out_ref[...] = exact_small(own_rows(me_ref, d_cond, size), onehot)
     wo_out_ref[...] = exact_small(own_rows(me_ref, silu(before), size), d_cond)
@@ -1056,13 +1144,16 @@
     d_before_ref[...] = jnp.sum(d_before, axis=0, keepdims=True)
 
 
-def late_condition(me, parts, count, before, cond, d_active, sinus, labels, wo, ada, classes, devices):
+def late_condition(
+    me, parts, count, before, cond, d_active, ada_early, d_mod_early, sinus, labels, wo, ada, classes,
+    devices,
+):
     features = ada.shape[0]
     size = features // devices
     whole = lambda a: pl.BlockSpec(a.shape, lambda s: (0,) * a.ndim)
     shapes = [
-        jax.ShapeDtypeStruct((size, 2 * features), single),
-        jax.ShapeDtypeStruct((1, 2 * features), single),
+        jax.ShapeDtypeStruct((size, 6 * features), single),
+        jax.ShapeDtypeStruct((1, 6 * features), single),
         jax.ShapeDtypeStruct((size, classes), single),
         jax.ShapeDtypeStruct((size, features), single),
         jax.ShapeDtypeStruct((sinus.shape[1] // devices, features), single),
@@ -1073,21 +1164,23 @@
         partial(late_kernel, count),
         grid=(1,),
         in_specs=[pl.BlockSpec(memory_space=pltpu.SMEM)]
-        + [whole(a) for a in (parts, before, cond, d_active, sinus, labels, wo)]
+        + [
+            whole(a)
+            for a in (parts, before, cond, d_active, ada_early, d_mod_early, sinus, labels, wo)
+        ]
         + [pl.BlockSpec((features, 2 * features), lambda s: (0, 0))],
         out_specs=[whole(a) for a in shapes],
         out_shape=shapes,
-        compiler_params=params(),
+        compiler_params=params(16),
         cost_estimate=cost(20 * ada.size, ada.size),
         name="late_condition",
-    )(me, parts, before, cond, d_active, sinus, labels, wo, ada)
-
-
-def sum_cores(halves):
+    )(me, parts, before, cond, d_active, ada_early, d_mod_early, sinus, labels, wo, ada)
+
+
+def sum_cores(keep, give):
     strips = lax.axis_size("strips")
-    core = lax.axis_index("strips") % 2
-    got = lax.ppermute(halves(1 - core), "strips", [(i, i ^ 1) for i in range(strips)])
-    return (halves(core).astype(single) + got.astype(single)).astype(bfloat)
+    got = lax.ppermute(give, "strips", [(i, i ^ 1) for i in range(strips)])
+    return (keep.astype(single) + got.astype(single)).astype(bfloat)
 
 
 def sum_axis(part, axis, size, place, step):
@@ -1218,7 +1311,19 @@
     saved = []
     mixed = []
     d_act = feed_upstream(d_branch, shrink_weight)
-    group, d_act = lax.optimization_barrier((group, d_act))
+    group, d_act, expand_line, mixer_taps, mixer_line, output_line, shrink_line = (
+        lax.optimization_barrier(
+            (
+                group,
+                d_act,
+                row_vector(expand_bias),
+                tap_rows(mixer_kernel),
+                row_vector(mixer_bias),
+                row_vector(output_bias),
+                row_vector(shrink_bias),
+            )
+        )
+    )
     for c in range(CHUNKS):
         saved.append(attend(group, own_weight, own_bias, c * piece, piece))
         mixed.append(collect(saved[c][3]))
@@ -1229,24 +1334,23 @@
         joined = joined.transpose(0, 2, 1, 3).reshape(count, 4, quarter, features)
         mixed = [joined]
 
-    attended, middle, normed_b = middle_part(
-        mixed, output_weight, row_vector(output_bias), kept, gate_a, scale_b, shift_b
-    )
-    branch, e, act, d_hid, feed_small = feed_forward(
+    attended, middle, normed_b, first_rows, last_rows = middle_part(
+        mixed, output_weight, output_line, kept, gate_a, scale_b, shift_b
+    )
+    act, d_hid, feed_small = feed_forward(
         edge,
         normed_b,
-        from_above(normed_b[:, -2:]),
-        from_below(normed_b[:, :2]),
+        from_above(last_rows),
+        from_below(first_rows),
         d_act,
         expand_weight,
-        row_vector(expand_bias),
-        tap_rows(mixer_kernel),
-        row_vector(mixer_bias),
-        shrink_weight,
+        expand_line,
+        mixer_taps,
+        mixer_line,
     )
     turned = turn(
-        branch, e, middle, attended, g_kept, gate_b, scale_b, gate_a, row_vector(shrink_bias),
-        output_weight, mixed,
+        act, d_hid, middle, attended, g_kept, gate_b, scale_b, gate_a, shrink_line,
+        output_weight, shrink_weight, expand_weight, mixed,
     )
     result, d_middle = turned[:2]
     d_mixed = turned[2:-2]
@@ -1254,17 +1358,7 @@
 
     hidden = expand_weight.shape[1]
     steps = hidden // features
-    grad_shrink, grad_expand = feed_grads(act, d_hid, normed_b, d_branch)
-
-    early = jnp.concatenate(
-        [
-            grad_shrink.reshape(devices, hidden // devices, features),
-            grad_expand.reshape(steps, devices, features // devices, features)
-            .transpose(1, 0, 2, 3)
-            .reshape(devices, hidden // devices, features),
-        ],
-        axis=1,
-    )
+    early = feed_grads(act, d_hid, normed_b, d_branch, devices)
     early_sum = lax.psum_scatter(early, both, scatter_dimension=0, tiled=False).astype(single)
 
     if share == 1:
@@ -1288,7 +1382,8 @@
         ],
         axis=1,
     ).reshape(-1)
-    to_all = jnp.concatenate([to_all, timesteps.astype(single), labels.astype(single)])
+    whole_numbers = jnp.concatenate([timesteps // 32, timesteps % 32, labels // 32, labels % 32])
+    to_all = jnp.concatenate([to_all, whole_numbers.astype(single)])
     fill = -(to_all.shape[0] + 11 * (hidden // devices) + 2 * size) % LANES
     early_small = jnp.concatenate(
         [
@@ -1298,7 +1393,7 @@
             jnp.zeros((devices, fill), single),
         ],
         axis=1,
-    )
+    ).astype(bfloat)
     early_small = after(early_small, grads[0][0], *d_mixed)
     early_got = lax.all_to_all(early_small, both, 0, 0, tiled=True)
 
@@ -1323,15 +1418,18 @@
         d_query_sum = lax.dynamic_update_slice(flat, d_query_sum, (head_at,))
         d_value_sum = lax.dynamic_update_slice(flat, d_value_sum, (head_at,))
     late = late.reshape(items, strips // 2, 2, size, 4 * features)
-    late_part = sum_cores(lambda core: lax.dynamic_index_in_dim(late, core, 2, keepdims=False))
+    core = strip % 2
+    keep = lax.dynamic_index_in_dim(late, core, 2, keepdims=False)
+    give = lax.dynamic_index_in_dim(late, 1 - core, 2, keepdims=False)
 
     per_latent = count * 4 * features
     parts_early = early_got[:, :per_latent].reshape(items, strips, per_latent)
-    first = early_got.reshape(items, strips, -1)[:, 0, per_latent : per_latent + 2 * count]
-    all_times = first[:, :count].reshape(-1)
-    all_labels = first[:, count:].reshape(-1, 1).astype(jnp.int32)
+    first = early_got.reshape(items, strips, -1)[:, 0, per_latent : per_latent + 4 * count]
+    first = first.astype(single).reshape(items, 4, count)
+    all_times = (first[:, 0] * 32.0 + first[:, 1]).reshape(-1)
+    all_labels = (first[:, 2] * 32.0 + first[:, 3]).reshape(-1, 1).astype(jnp.int32)
     sinus = time_features(all_times, waves)
-    early_sums = jnp.sum(early_got[:, per_latent + 2 * count :], axis=0)
+    early_sums = jnp.sum(early_got[:, per_latent + 4 * count :].astype(single), axis=0)
     cut = 11 * (hidden // devices)
     feed_sum = early_sums[:cut].reshape(11, -1)
     narrow_sum = early_sums[cut : cut + 2 * size].reshape(2, size)
@@ -1340,8 +1438,8 @@
         index, parts_early, count, sinus, all_labels, weights, ada_weight, size
     )
 
-    d_reduced, before, late_part = lax.optimization_barrier((d_reduced, before, late_part))
-    late_part = sum_items(late_part)
+    d_reduced, before, keep, give = lax.optimization_barrier((d_reduced, before, keep, give))
+    late_part = sum_items(sum_cores(keep, give))
     grad_latents, down_small, final_sums = final(
         d_reduced,
         from_above(d_reduced[:, 2:, -2 * sub :]),
@@ -1363,13 +1461,13 @@
             jnp.zeros((devices, fill), single),
         ],
         axis=1,
-    )
-    late_small, late_part = lax.optimization_barrier((late_small, late_part))
+    ).astype(bfloat)
+    late_got = lax.all_to_all(late_small, both, 0, 0, tiled=True)
+    late_got, late_part = lax.optimization_barrier((late_got, late_part))
     late_sum = sum_strips(late_part)
-    late_got = lax.all_to_all(late_small, both, 0, 0, tiled=True)
-    late_sums = jnp.sum(late_got[:, to_all.shape[0] :], axis=0)[: 12 * size].reshape(12, size)
+    late_sums = jnp.sum(late_got[:, to_all.shape[0] :].astype(single), axis=0)[: 12 * size].reshape(12, size)
     (
-        grad_ada_late, d_mod_late, grad_table, grad_time_out, grad_time_in, d_cond, d_before,
+        grad_ada, d_mod, grad_table, grad_time_out, grad_time_in, d_cond, d_before,
     ) = late_condition(
         index,
         late_got[:, : to_all.shape[0]].reshape(items, strips, -1),
@@ -1377,6 +1475,8 @@
         before,
         cond,
         d_active,
+        grad_ada_early,
+        d_mod_early,
         sinus,
         all_labels,
         time_out_weight,
@@ -1389,7 +1489,6 @@
         part = array.shape[-1] // devices
         return lax.dynamic_slice_in_dim(array[0], me * part, part, axis=0)
 
-    feed_rows = hidden // devices
     return (
         result,
         grad_latents,
@@ -1398,8 +1497,8 @@
         grad_time_out,
         mine(d_cond),
         grad_table,
-        jnp.concatenate([grad_ada_late, grad_ada_early], axis=1),
-        mine(jnp.concatenate([d_mod_late, d_mod_early], axis=1)),
+        grad_ada,
+        mine(d_mod),
         late_sums[2:11].T,
         late_sums[11],
         late_sum[:, : 3 * features],
@@ -1407,14 +1506,11 @@
         late_sums[1],
         late_sum[:, 3 * features :],
         narrow_sum[0],
-        early_sum[feed_rows:]
-        .reshape(steps, features // devices, features)
-        .transpose(1, 0, 2)
-        .reshape(features // devices, hidden),
+        early_sum[steps:].transpose(1, 0, 2).reshape(size, hidden),
         feed_sum[10],
         feed_sum[:9].T,
         feed_sum[9],
-        early_sum[:feed_rows],
+        early_sum[:steps].reshape(hidden // devices, features),
         narrow_sum[1],
     )
 

time: 518 us -> 478 us (0.923)
  Pallas kernels: 267 us -> 223 us
  waiting for transfers between devices: 102 us -> 73.6 us
  local copies, waits for them, and re-layouts: 44.5 us -> 68.2 us
  starting transfers between devices: 61.5 us -> 73.9 us
    pallas_call x1, Pallas kernels: 73.1 us -> 48 us  [feed_forward(): pl.pallas_call(feed_kernel, grid=(steps,), in_specs=[pl.BlockSpec(memory_...]
    unnamed x69 -> x88, local copies, waits for them, and re-layouts: 7.82 us -> 31.7 us
    all_to_all x3, starting transfers between devices: 12.2 us -> 24.5 us  [collect(): return lax.all_to_all(flat, 'strips', 0, 0, tiled=True)]
    all_to_all x3, waiting for transfers between devices: 58.8 us -> 46.6 us  [collect(): return lax.all_to_all(flat, 'strips', 0, 0, tiled=True)]
    pallas_call x1, Pallas kernels: 15.3 us -> 26.9 us  [turn(): pl.pallas_call(partial(turn_kernel, len(mixed)), grid=(count, steps), in_...]
    all_to_all x3, waiting for transfers between devices: 23.9 us -> 15.4 us  [spread(): got = lax.all_to_all(flat, 'strips', 0, 0, tiled=True)]
    pallas_call x1, Pallas kernels: 11.6 us -> 5 us  [front(): pl.pallas_call(front_kernel, grid=(count,), in_specs=[pl.BlockSpec(memory...]
    all_to_all x1, waiting for transfers between devices: 13.7 us -> 8.3 us  [per_device(): late_got = lax.all_to_all(late_small, both, 0, 0, tiled=True)]
  transfers between devices with their start and end apart: 22 -> 22, of which waited for: 9 -> 8; matrix products, arithmetic and copies ran while one was open for 10% -> 13% of each run, Pallas kernels for 28% -> 26%
where the time goes in v3:
time: 478 us; the launch traced here: 474 us
  Pallas kernels  223 us (47%)
  starting transfers between devices  73.9 us (15%)
  waiting for transfers between devices  73.6 us (15%)
  local copies, waits for them, and re-layouts  68.2 us (14%)
  other arithmetic  20.5 us (4%)
  between operations  15.1 us (3%)
    pallas_call x1, Pallas kernels, feed_forward(): pl.pallas_call(feed_kernel, grid=(steps,), in_specs=[pl.BlockSpec(memory_...  48 us
    all_to_all x3, waiting for transfers between devices, collect(): return lax.all_to_all(flat, 'strips', 0, 0, tiled=True)  46.6 us
    pallas_call x2, Pallas kernels, attend_back(): pl.pallas_call(attend_back_kernel, grid=(pairs,), in_specs=[column] * 5 +...  36.3 us
    unnamed x88, local copies, waits for them, and re-layouts  31.7 us
    pallas_call x2, Pallas kernels, attend(): pl.pallas_call(attend_kernel, grid=(pairs,), in_specs=[pl.BlockSpec((toke...  30.9 us
    pallas_call x1, Pallas kernels, turn(): pl.pallas_call(partial(turn_kernel, len(mixed)), grid=(count, steps), in_...  26.9 us
    all_to_all x3, starting transfers between devices, collect(): return lax.all_to_all(flat, 'strips', 0, 0, tiled=True)  24.5 us
    all_to_all x3, starting transfers between devices, spread(): got = lax.all_to_all(flat, 'strips', 0, 0, tiled=True)  19.6 us
  transfers between devices with their start and end apart: 22, of which 8 were waited for; matrix products, arithmetic and copies ran while one was open for 13% of the time, Pallas kernels for 26%

profile of v3, /device:TPU:0, one launch (start us, length us, event | category | flops | bytes accessed | tf_op | source)
XLA Modules:
  0.0 474.5 jit_solution(15133092071634611334)
XLA Ops:
  36.0 6.3 %all-to-all-start = ((bf16[8,128,768]{2,1,0:T(8,128)(2,1)}), bf16[8,128,768]{2,1,0:T(8,128)(2,1)}, u32[]{:S(2)}, u32[]{:S(2)}) async-start(bf16[8,128,768]{2,1,0:T(8,128)(2,1)} %bitcast.111), calls=%async_computation | async-start | bytes 3145728 | tf_op jit(solution)/shard_map/all_to_all | solution.py:1288
  57.0 10.6 %feed_upstream.1.d_act_ref = bf16[1280,3072]{1,0:T(8,128)(2,1)} custom-call(bf16[1280,768]{1,0:T(8,128)(2,1)} %bitcast.114, bf16[3072,768]{1,0:T(8,128)(2,1)} %refs_10_.1), custom_call_target="tpu_custom_call" | custom-call | flops 6039797760 | bytes 9830400 | tf_op jit(solution)/shard_map/feed_upstream/pallas_call | solution.py:506
  67.6 12.5 %all-to-all-done = bf16[8,128,768]{2,1,0:T(8,128)(2,1)} async-done(((bf16[8,128,768]{2,1,0:T(8,128)(2,1)}), bf16[8,128,768]{2,1,0:T(8,128)(2,1)}, u32[]{:S(2)}, u32[]{:S(2)}) %all-to-all-start) | async-done | bytes 1572896 | tf_op jit(solution)/shard_map/all_to_all | solution.py:1288
  80.2 15.5 %attend.2 = (bf16[1024,384]{1,0:T(8,128)(2,1)}, bf16[1024,384]{1,0:T(8,128)(2,1)}, bf16[1024,384]{1,0:T(8,128)(2,1)}, bf16[1024,384]{1,0:T(8,128)(2,1)}, f32[3,2,1024]{2,1,0:T(2,128)}) custom-call(bf16[1024,768]{1,0:T(8,128)(2,1)} %bitcast.7.x_ref.refs_0_, bf16[768,2304]{1,0:T(8,128)(2,1)} %refs_6_.1, bf16[768,2304]{1,0:T(8,128)(2,1)} %refs_6_.1, ...), custom_call_target="tpu_custom_call" | custom-call | flops 8254390272 | bytes 6488064 | tf_op jit(solution)/shard_map/attend/pallas_call | solution.py:271
  95.6 15.3 %all-to-all-start.1 = ((bf16[8,128,384]{2,1,0:T(8,128)(2,1)}), bf16[8,128,384]{2,1,0:T(8,128)(2,1)}, u32[]{:S(2)}, u32[]{:S(2)}) async-start(bf16[8,128,384]{2,1,0:T(8,128)(2,1)} %bitcast.124), calls=%async_computation.1 | async-start | bytes 1572864 | tf_op jit(solution)/shard_map/all_to_all | solution.py:1293
  111.0 15.4 %attend.3 = (bf16[1024,384]{1,0:T(8,128)(2,1)}, bf16[1024,384]{1,0:T(8,128)(2,1)}, bf16[1024,384]{1,0:T(8,128)(2,1)}, bf16[1024,384]{1,0:T(8,128)(2,1)}, f32[3,2,1024]{2,1,0:T(2,128)}) custom-call(bf16[1024,768]{1,0:T(8,128)(2,1)} %bitcast.7.x_ref.refs_0_, bf16[768,2304]{1,0:T(8,128)(2,1)} %refs_6_.1, bf16[768,2304]{1,0:T(8,128)(2,1)} %refs_6_.1, ...), custom_call_target="tpu_custom_call" | custom-call | flops 8254390272 | bytes 6488064 | tf_op jit(solution)/shard_map/attend/pallas_call | solution.py:271
  126.4 5.2 %all-to-all-done.1 = bf16[8,128,384]{2,1,0:T(8,128)(2,1)} async-done(((bf16[8,128,384]{2,1,0:T(8,128)(2,1)}), bf16[8,128,384]{2,1,0:T(8,128)(2,1)}, u32[]{:S(2)}, u32[]{:S(2)}) %all-to-all-start.1) | async-done | bytes 786464 | tf_op jit(solution)/shard_map/all_to_all | solution.py:1293
  137.0 19.8 %all-to-all-done.2 = bf16[8,128,384]{2,1,0:T(8,128)(2,1)} async-done(((bf16[8,128,384]{2,1,0:T(8,128)(2,1)}), bf16[8,128,384]{2,1,0:T(8,128)(2,1)}, u32[]{:S(2)}, u32[]{:S(2)}) %all-to-all-start.2) | async-done | bytes 786464 | tf_op jit(solution)/shard_map/all_to_all | solution.py:1293
  156.8 6.5 %middle.1 = (f32[2,8,64,768]{3,2,1,0:T(8,128)}, f32[2,8,64,768]{3,2,1,0:T(8,128)}, bf16[2,8,64,768]{3,2,1,0:T(8,128)(2,1)}, bf16[2,2,64,768]{3,2,1,0:T(8,128)(2,1)}, bf16[2,2,64,768]{3,2,1,0:T(8,128)(2,1)}) custom-call(bf16[2,4,128,384]{3,2,1,0:T(8,128)(2,1)} %bitcast.14.refs_0_.refs_12_, bf16[2,4,128,384]{3,2,1,0:T(8,128)(2,1)} %bitcast.16.refs_1_.refs_13_, ...), custom_call_target="tpu_custom_call" | custom-call | flops 1207959552 | bytes 11010048 | tf_op jit(solution)/shard_map/middle/pallas_call | solution.py:472
  169.6 48.0 %feed_forward.1 = (bf16[1024,3072]{1,0:T(8,128)(2,1)}, bf16[1024,3072]{1,0:T(8,128)(2,1)}, f32[16,3072]{1,0:T(8,128)}) custom-call(f32[2]{0:T(128)} %copy-done.15, bf16[2,8,64,768]{3,2,1,0:T(8,128)(2,1)} %get-tuple-element.98.nb_ref, bf16[2,2,64,768]{3,2,1,0:T(8,128)(2,1)} %collective-permute-done.2.top_ref, ...), custom_call_target="tpu_custom_call" | custom-call | flops 7247757312 | bytes 34603008 | tf_op jit(solution)/shard_map/feed_forward/pallas_call | solution.py:606
  217.7 26.9 %turn.1 = (bf16[2,8,64,768]{3,2,1,0:T(8,128)(2,1)}, f32[2,8,64,768]{3,2,1,0:T(8,128)}, bf16[2,4,128,384]{3,2,1,0:T(8,128)(2,1)}, bf16[2,4,128,384]{3,2,1,0:T(8,1...) custom-call(bf16[1024,3072]{1,0:T(8,128)(2,1)} %get-tuple-element.105.refs_0_.act_ref, ...), custom_call_target="tpu_custom_call" | custom-call | flops 12079595520 | bytes 28311552 | tf_op jit(solution)/shard_map/turn/pallas_call | solution.py:816
  244.6 7.8 %all-to-all-start.3 = ((bf16[8,128,384]{2,1,0:T(8,128)(2,1)}), bf16[8,128,384]{2,1,0:T(8,128)(2,1)}, u32[]{:S(2)}, u32[]{:S(2)}) async-start(bf16[8,128,384]{2,1,0:T(8,128)(2,1)} %bitcast.126), calls=%async_computation.3 | async-start | bytes 1572864 | tf_op jit(solution)/shard_map/all_to_all | solution.py:1288
  256.9 15.9 %feed_grads.1 = bf16[32,8,24,768]{3,2,1,0:T(8,128)(2,1)} custom-call(bf16[1024,3072]{1,0:T(8,128)(2,1)} %get-tuple-element.105.refs_0_.act_ref, bf16[1024,3072]{1,0:T(8,128)(2,1)} %get-tuple-element.106.refs_1_.d_hid_ref, bf16[2,8,64,768]{3,2,1,0:T(8,128)(2,1)} %get-tuple-element.98.nb_ref, bf16[2,10,64,768]{3,2,1,0:T(8,128)(2,1)} %copy-done.16), custom_call_target="tpu_custom_call" | custom-call | flops 9663676416 | bytes 31457280 | tf_op jit(solution)/shard_map/feed_grads/pallas_call | solution.py:694
  275.3 5.5 %all-to-all-start.4 = ((bf16[8,128,384]{2,1,0:T(8,128)(2,1)}), bf16[8,128,384]{2,1,0:T(8,128)(2,1)}, u32[]{:S(2)}, u32[]{:S(2)}) async-start(bf16[8,128,384]{2,1,0:T(8,128)(2,1)} %bitcast.125), calls=%async_computation.4 | async-start | bytes 1572864 | tf_op jit(solution)/shard_map/all_to_all | solution.py:1288
  280.8 18.2 %attend_back.2 = (bf16[1024,384]{1,0:T(8,128)(2,1)}, bf16[1024,384]{1,0:T(8,128)(2,1)}, bf16[1024,384]{1,0:T(8,128)(2,1)}) custom-call(bf16[1024,384]{1,0:T(8,128)(2,1)} %get-tuple-element.112.q_ref, bf16[1024,384]{1,0:T(8,128)(2,1)} %get-tuple-element.113.k_ref, bf16[1024,384]{1,0:T(8,128)(2,1)} %get-tuple-element.114.v_ref, ...), custom_call_target="tpu_custom_call" | custom-call | flops 16106127360 | bytes 6291456 | tf_op jit(solution)/shard_map/attend_back/pallas_call | solution.py:332
  311.0 18.2 %attend_back.3 = (bf16[1024,384]{1,0:T(8,128)(2,1)}, bf16[1024,384]{1,0:T(8,128)(2,1)}, bf16[1024,384]{1,0:T(8,128)(2,1)}) custom-call(bf16[1024,384]{1,0:T(8,128)(2,1)} %get-tuple-element.121.q_ref, bf16[1024,384]{1,0:T(8,128)(2,1)} %get-tuple-element.122.k_ref, bf16[1024,384]{1,0:T(8,128)(2,1)} %get-tuple-element.123.v_ref, ...), custom_call_target="tpu_custom_call" | custom-call | flops 16106127360 | bytes 6291456 | tf_op jit(solution)/shard_map/attend_back/pallas_call | solution.py:332
  329.1 9.1 %regroup.1 = bf16[1024,768]{1,0:T(8,128)(2,1)} custom-call(bf16[1024,384]{1,0:T(8,128)(2,1)} %get-tuple-element.118.refs_0_.refs_2_, bf16[1024,384]{1,0:T(8,128)(2,1)} %get-tuple-element.119.refs_1_.refs_3_, bf16[1024,384]{1,0:T(8,128)(2,1)} %get-tuple-element.120.refs_2_.refs_4_, bf16[1024,384]{1,0:T(8,128)(2,1)} %get-tuple-element.126.refs_3_.refs_5_, ...), custom_call_target="tpu_custom_call" | custom-call | flops 3623878656 | bytes 6291456 | tf_op jit(solution)/shard_map/regroup/pallas_call | solution.py:365
  338.2 5.0 %all-to-all-start.5 = ((bf16[8,128,768]{2,1,0:T(8,128)(2,1)}), bf16[8,128,768]{2,1,0:T(8,128)(2,1)}, u32[]{:S(2)}, u32[]{:S(2)}) async-start(bf16[8,128,768]{2,1,0:T(8,128)(2,1)} %bitcast.120), calls=%async_computation.5 | async-start | bytes 3145728 | tf_op jit(solution)/shard_map/all_to_all | solution.py:1293
  343.3 10.0 %input_grad.1 = (bf16[768,3072]{1,0:T(8,128)(2,1)}, f32[8,1536]{1,0:T(8,128)}) custom-call(bf16[1024,768]{1,0:T(8,128)(2,1)} %bitcast.7.x_ref.refs_0_, bf16[768,768]{1,0:T(8,128)(2,1)} %get-tuple-element.135.refs_1_, bf16[1024,384]{1,0:T(8,128)(2,1)} %get-tuple-element.118.refs_0_.refs_2_, bf16[1024,384]{1,0:T(8,128)(2,1)} %get-tuple-element.119.refs_1_.refs_3_, ...), custom_call_target="tpu_custom_call" | custom-call | flops 3623878656 | bytes 7864320 | tf_op jit(solution)/shard_map/input_grad/pallas_call | solution.py:406
  353.3 5.3 %dynamic-slice_bitcast_fusion = (bf16[4,4,24,3072]{3,2,1,0:T(8,128)(2,1)}, bf16[4,4,24,3072]{3,2,1,0:T(8,128)(2,1)}) fusion(bf16[4,4,2,24,3072]{4,3,2,1,0:T(8,128)(2,1)} %bitcast.115, s32[]{:T(128)S(6)} %select_n.75, s32[]{:T(128)S(6)} %select_n.74), kind=kLoop, calls=%fused_computation.1 | loop fusion | bytes 9437192 | tf_op jit(solution)/shard_map/jit(dynamic_index_in_dim)/squeeze | solution.py:1423
  372.0 21.7 %all-to-all-done.5 = bf16[8,128,768]{2,1,0:T(8,128)(2,1)} async-done(((bf16[8,128,768]{2,1,0:T(8,128)(2,1)}), bf16[8,128,768]{2,1,0:T(8,128)(2,1)}, u32[]{:S(2)}, u32[]{:S(2)}) %all-to-all-start.5) | async-done | bytes 1572896 | tf_op jit(solution)/shard_map/all_to_all | solution.py:1293
  411.1 13.1 %final.1 = (bf16[2,8,64,768]{3,2,1,0:T(8,128)(2,1)}, f32[16,768]{1,0:T(8,128)}, f32[2,8,768]{2,1,0:T(8,128)}) custom-call(bf16[2,4,128,768]{3,2,1,0:T(8,128)(2,1)} %bitcast.25.d_ref, bf16[2,2,32,768]{3,2,1,0:T(8,128)(2,1)} %copy-done.21, bf16[2,2,32,768]{3,2,1,0:T(8,128)(2,1)} %copy-done.22, bf16[2,10,64,768]{3,2,1,0:T(8,128)(2,1)} %copy-done.6, ...), custom_call_target="tpu_custom_call" | custom-call | flops 141557760 | bytes 9437184 | tf_op jit(solution)/shard_map/final/pallas_call | solution.py:942
  430.4 5.6 %all-to-all-start.7 = ((bf16[32,2,1728]{2,1,0:T(2,128)(2,1)}), bf16[32,2,1728]{2,1,0:T(2,128)(2,1)S(1)}, u32[]{:S(2)}, u32[]{:S(2)}) async-start(bf16[32,2,1728]{2,1,0:T(2,128)(2,1)} %reshape.402), calls=%async_computation.7 | async-start | bytes 458752 | tf_op jit(solution)/shard_map/all_to_all | solution.py:1465
  437.3 8.3 %all-to-all-done.7 = bf16[32,2,1728]{2,1,0:T(2,128)(2,1)S(1)} async-done(((bf16[32,2,1728]{2,1,0:T(2,128)(2,1)}), bf16[32,2,1728]{2,1,0:T(2,128)(2,1)S(1)}, u32[]{:S(2)}, u32[]{:S(2)}) %all-to-all-start.7) | async-done | bytes 221216 | tf_op jit(solution)/shard_map/all_to_all | solution.py:1465
  (226 shorter events, 133.6 us)
Async XLA Ops:
  9.3 15.9 %collective-permute-start.1 = (bf16[2,2,64,768]{3,2,1,0:T(8,128)(2,1)}, bf16[2,2,64,768]{3,2,1,0:T(8,128)(2,1)}, u32[]{:S(2)}, u32[]{:S(2)}) collective-permute-start(bf16[2,2,64,768]{3,2,1,0:T(8,128)(2,1)} %pad_maximum_fusion.1), channel_id=1, source_target_pairs={{1,0},{2,1},{3,2},{4,3},{5,4},{6,5},{7,6},{9,8},{10,9},{11,10},{12... | collective-permute-start | bytes 1179656 | tf_op jit(solution)/shard_map/ppermute | solution.py:974
  11.5 14.8 %collective-permute-start = (bf16[2,2,64,768]{3,2,1,0:T(8,128)(2,1)}, bf16[2,2,64,768]{3,2,1,0:T(8,128)(2,1)}, u32[]{:S(2)}, u32[]{:S(2)}) collective-permute-start(bf16[2,2,64,768]{3,2,1,0:T(8,128)(2,1)} %pad_maximum_fusion), channel_id=1, source_target_pairs={{0,1},{1,2},{2,3},{3,4},{4,5},{5,6},{6,7},{8,9},{9,10},{10,11},{11... | collective-permute-start | bytes 1179656 | tf_op jit(solution)/shard_map/ppermute | solution.py:969
  36.0 44.2 %all-to-all-start = ((bf16[8,128,768]{2,1,0:T(8,128)(2,1)}), bf16[8,128,768]{2,1,0:T(8,128)(2,1)}, u32[]{:S(2)}, u32[]{:S(2)}) async-start(bf16[8,128,768]{2,1,0:T(8,128)(2,1)} %bitcast.111), calls=%async_computation | async-start | bytes 3145728 | tf_op jit(solution)/shard_map/all_to_all | solution.py:1288
  95.6 36.0 %all-to-all-start.1 = ((bf16[8,128,384]{2,1,0:T(8,128)(2,1)}), bf16[8,128,384]{2,1,0:T(8,128)(2,1)}, u32[]{:S(2)}, u32[]{:S(2)}) async-start(bf16[8,128,384]{2,1,0:T(8,128)(2,1)} %bitcast.124), calls=%async_computation.1 | async-start | bytes 1572864 | tf_op jit(solution)/shard_map/all_to_all | solution.py:1293
  110.9 25.5 %copy-start.24 = (f32[1,2,768]{2,1,0:T(2,128)S(1)}, f32[1,2,768]{2,1,0:T(2,128)}, u32[]{:S(2)}) copy-start(f32[1,2,768]{2,1,0:T(2,128)} %get-tuple-element.180) | copy-start | bytes 18436
  131.6 25.2 %all-to-all-start.2 = ((bf16[8,128,384]{2,1,0:T(8,128)(2,1)}), bf16[8,128,384]{2,1,0:T(8,128)(2,1)}, u32[]{:S(2)}, u32[]{:S(2)}) async-start(bf16[8,128,384]{2,1,0:T(8,128)(2,1)} %bitcast.123), calls=%async_computation.2 | async-start | bytes 1572864 | tf_op jit(solution)/shard_map/all_to_all | solution.py:1293
  163.3 3.9 collective-permute-start.2
  165.7 3.9 collective-permute-start.3
  217.7 38.2 %copy-start.23 = (f32[16,3072]{1,0:T(8,128)S(1)}, f32[16,3072]{1,0:T(8,128)}, u32[]{:S(2)}) copy-start(f32[16,3072]{1,0:T(8,128)} %get-tuple-element.130) | copy-start | bytes 589828
  244.6 30.7 %all-to-all-start.3 = ((bf16[8,128,384]{2,1,0:T(8,128)(2,1)}), bf16[8,128,384]{2,1,0:T(8,128)(2,1)}, u32[]{:S(2)}, u32[]{:S(2)}) async-start(bf16[8,128,384]{2,1,0:T(8,128)(2,1)} %bitcast.126), calls=%async_computation.3 | async-start | bytes 1572864 | tf_op jit(solution)/shard_map/all_to_all | solution.py:1288
  252.4 212.4 %reduce-scatter.2.cloned.1.call-start = ((), (), s32[]{:S(2)}) async-start(), calls=%async_computation.9 | async-start | bytes 9732096 | tf_op jit(solution)/shard_map/reduce_scatter | solution.py:1362
  275.3 26.5 %all-to-all-start.4 = ((bf16[8,128,384]{2,1,0:T(8,128)(2,1)}), bf16[8,128,384]{2,1,0:T(8,128)(2,1)}, u32[]{:S(2)}, u32[]{:S(2)}) async-start(bf16[8,128,384]{2,1,0:T(8,128)(2,1)} %bitcast.125), calls=%async_computation.4 | async-start | bytes 1572864 | tf_op jit(solution)/shard_map/all_to_all | solution.py:1288
  307.3 30.9 %all-to-all-start.6 = ((bf16[32,2,3648]{2,1,0:T(2,128)(2,1)}), bf16[32,2,3648]{2,1,0:T(2,128)(2,1)}, u32[]{:S(2)}, u32[]{:S(2)}) async-start(bf16[32,2,3648]{2,1,0:T(2,128)(2,1)} %reshape.400), calls=%async_computation.6 | async-start | bytes 950272 | tf_op jit(solution)/shard_map/all_to_all | solution.py:1398
  338.2 55.4 %all-to-all-start.5 = ((bf16[8,128,768]{2,1,0:T(8,128)(2,1)}), bf16[8,128,768]{2,1,0:T(8,128)(2,1)}, u32[]{:S(2)}, u32[]{:S(2)}) async-start(bf16[8,128,768]{2,1,0:T(8,128)(2,1)} %bitcast.120), calls=%async_computation.5 | async-start | bytes 3145728 | tf_op jit(solution)/shard_map/all_to_all | solution.py:1293
  393.7 5.6 %collective-permute-start.6 = (bf16[4,4,24,3072]{3,2,1,0:T(8,128)(2,1)}, bf16[4,4,24,3072]{3,2,1,0:T(8,128)(2,1)}, u32[]{:S(2)}, u32[]{:S(2)}) collective-permute-start(bf16[4,4,24,3072]{3,2,1,0:T(8,128)(2,1)} %get-tuple-element.145), channel_id=1, source_target_pairs={{0,1},{1,0},{2,3},{3,2},{4,5},{5,4},{6,7},{7,6},{8,9},{9,8},{10,11... | collective-permute-start | bytes 7077896 | tf_op jit(solution)/shard_map/ppermute | solution.py:1182
  395.6 14.7 %collective-permute-start.4 = (bf16[2,2,32,768]{3,2,1,0:T(8,128)(2,1)S(1)}, bf16[2,2,32,768]{3,2,1,0:T(8,128)(2,1)S(1)}, u32[]{:S(2)}, u32[]{:S(2)}) collective-permute-start(bf16[2,2,32,768]{3,2,1,0:T(8,128)(2,1)S(1)} %get-tuple-element.166), channel_id=1, source_target_pairs={{0,1},{1,2},{2,3},{3,4},{4,5},{5,6},{6,7},{8,9},{9,10},{10,11},{11... | collective-permute-start | bytes 589832 | tf_op jit(solution)/shard_map/ppermute | solution.py:969
  398.0 12.4 %collective-permute-start.5 = (bf16[2,2,32,768]{3,2,1,0:T(8,128)(2,1)S(1)}, bf16[2,2,32,768]{3,2,1,0:T(8,128)(2,1)S(1)}, u32[]{:S(2)}, u32[]{:S(2)}) collective-permute-start(bf16[2,2,32,768]{3,2,1,0:T(8,128)(2,1)S(1)} %get-tuple-element.165), channel_id=1, source_target_pairs={{1,0},{2,1},{3,2},{4,3},{5,4},{6,5},{7,6},{9,8},{10,9},{11,10},{12... | collective-permute-start | bytes 589832 | tf_op jit(solution)/shard_map/ppermute | solution.py:974
  405.2 40.7 %collective-permute-start.7 = (bf16[4,24,3072]{2,1,0:T(8,128)(2,1)}, bf16[4,24,3072]{2,1,0:T(8,128)(2,1)}, u32[]{:S(2)}, u32[]{:S(2)}) collective-permute-start(bf16[4,24,3072]{2,1,0:T(8,128)(2,1)} %get-tuple-element.162), channel_id=1, source_target_pairs={{0,8},{8,0},{16,24},{24,16},{1,9},{9,1},{17,25},{25,17},{2,10},{10... | collective-permute-start | bytes 1769480 | tf_op jit(solution)/shard_map/ppermute | solution.py:1190
  406.7 39.2 %collective-permute-start.8 = (bf16[4,24,3072]{2,1,0:T(8,128)(2,1)}, bf16[4,24,3072]{2,1,0:T(8,128)(2,1)}, u32[]{:S(2)}, u32[]{:S(2)}) collective-permute-start(bf16[4,24,3072]{2,1,0:T(8,128)(2,1)} %get-tuple-element.164), channel_id=1, source_target_pairs={{0,16},{8,24},{16,0},{24,8},{1,17},{9,25},{17,1},{25,9},{2,18},{10... | collective-permute-start | bytes 1769480 | tf_op jit(solution)/shard_map/ppermute | solution.py:1190
  408.6 37.3 %collective-permute-start.9 = (bf16[4,24,3072]{2,1,0:T(8,128)(2,1)S(1)}, bf16[4,24,3072]{2,1,0:T(8,128)(2,1)}, u32[]{:S(2)}, u32[]{:S(2)}) collective-permute-start(bf16[4,24,3072]{2,1,0:T(8,128)(2,1)S(1)} %get-tuple-element.163), channel_id=1, source_target_pairs={{0,24},{8,16},{16,8},{24,0},{1,25},{9,17},{17,9},{25,1},{2,26},{10... | collective-permute-start | bytes 1769480 | tf_op jit(solution)/shard_map/ppermute | solution.py:1190
  430.4 15.1 %all-to-all-start.7 = ((bf16[32,2,1728]{2,1,0:T(2,128)(2,1)}), bf16[32,2,1728]{2,1,0:T(2,128)(2,1)S(1)}, u32[]{:S(2)}, u32[]{:S(2)}) async-start(bf16[32,2,1728]{2,1,0:T(2,128)(2,1)} %reshape.402), calls=%async_computation.7 | async-start | bytes 458752 | tf_op jit(solution)/shard_map/all_to_all | solution.py:1465
  448.6 13.9 %collective-permute-start.10 = (bf16[24,3072]{1,0:T(8,128)(2,1)}, bf16[24,3072]{1,0:T(8,128)(2,1)S(1)}, u32[]{:S(2)}, u32[]{:S(2)}) collective-permute-start(bf16[24,3072]{1,0:T(8,128)(2,1)} %get-tuple-element.173), channel_id=1, source_target_pairs={{0,2},{1,3},{2,0},{3,1},{4,6},{5,7},{6,4},{7,5},{8,10},{9,11},{10,... | collective-permute-start | bytes 442376 | tf_op jit(solution)/shard_map/ppermute | solution.py:1190
  449.4 14.0 %collective-permute-start.11 = (bf16[24,3072]{1,0:T(8,128)(2,1)S(1)}, bf16[24,3072]{1,0:T(8,128)(2,1)S(1)}, u32[]{:S(2)}, u32[]{:S(2)}) collective-permute-start(bf16[24,3072]{1,0:T(8,128)(2,1)S(1)} %get-tuple-element.175), channel_id=1, source_target_pairs={{0,4},{1,5},{2,6},{3,7},{4,0},{5,1},{6,2},{7,3},{8,12},{9,13},{10,... | collective-permute-start | bytes 442376 | tf_op jit(solution)/shard_map/ppermute | solution.py:1190
  449.9 13.5 %collective-permute-start.12 = (bf16[24,3072]{1,0:T(8,128)(2,1)S(1)}, bf16[24,3072]{1,0:T(8,128)(2,1)S(1)}, u32[]{:S(2)}, u32[]{:S(2)}) collective-permute-start(bf16[24,3072]{1,0:T(8,128)(2,1)S(1)} %get-tuple-element.174), channel_id=1, source_target_pairs={{0,6},{1,7},{2,4},{3,5},{4,2},{5,3},{6,0},{7,1},{8,14},{9,15},{10,... | collective-permute-start | bytes 442376 | tf_op jit(solution)/shard_map/ppermute | solution.py:1190
  (36 other events, 205.3 us)
Sparse Core Ops, SparseCore 0:
  272.9 150.8 reduce-scatter.1

commit v4 on v3

--- a/solution.py
+++ b/solution.py
@@ -518,20 +518,46 @@
     )(db.reshape(lines, features), ws)
 
 
-def feed_kernel(
-    edge_ref, nb_ref, top_ref, bottom_ref, d_act_ref, we_ref, be_ref, taps_ref, bm_ref,
-    act_ref, d_hid_ref, small_ref,
-    nb_wide, hidden, wide, d_wide,
-):
-    count, rows, columns, features = nb_ref.shape
+TURN_ROWS = 4
+
+
+def feed_turn_kernel(parts, feeds, turns, *refs):
+    (
+        edge_ref, nb_ref, top_ref, bottom_ref, d_act_ref, we_ref, be_ref, taps_ref, bm_ref,
+        middle_ref, attended_ref, g_ref, gate_b_ref, scale_ref, gate_a_ref, shrink_ref,
+        ws_hbm, we_hbm, wo_hbm,
+    ) = refs[:19]
+    mixed_refs = refs[19 : 19 + parts]
+    small_ref, act_hbm, d_hid_hbm, result_ref, d_middle_ref = refs[19 + parts : 24 + parts]
+    d_mixed_refs = refs[24 + parts : 24 + 2 * parts]
+    (
+        gw_ref, sums_ref,
+        nb_wide, hidden, wide, d_wide, act_s, d_hid_s, ws, we, wo, gw_sum, grouped, branch_s, e_s, sums,
+        weight_sem, act_sem, d_hid_sem,
+    ) = refs[24 + 2 * parts :]
+    step = pl.program_id(0)
+    columns, features = nb_ref.shape[2:]
     sub = columns // COLUMN_PARTS
-    block = we_ref.shape[1]
-    own = rows * columns
-    tall = (rows + 4) * columns
-    mid = (rows + 2) * columns
-
-    @pl.when(pl.program_id(0) == 0)
+    weights = (
+        pltpu.make_async_copy(ws_hbm, ws, weight_sem.at[0]),
+        pltpu.make_async_copy(we_hbm, we, weight_sem.at[1]),
+        pltpu.make_async_copy(wo_hbm, wo, weight_sem.at[2]),
+    )
+
+    def out_copies(n):
+        at = pl.ds(pl.multiple_of(n * features, features), features)
+        return (
+            pltpu.make_async_copy(act_s.at[:, at], act_hbm.at[:, at], act_sem.at[n]),
+            pltpu.make_async_copy(d_hid_s.at[:, at], d_hid_hbm.at[:, at], d_hid_sem.at[n]),
+        )
+
+    @pl.when(step == 0)
     def _():
+        count, rows = nb_ref.shape[:2]
+        own = rows * columns
+        tall = (rows + 4) * columns
+        for c in weights:
+            c.start()
         for l in range(count):
             nb_wide[l * tall : l * tall + 2 * columns] = top_ref[l].reshape(2 * columns, features)
             nb_wide[l * tall + 2 * columns : (l + 1) * tall - 2 * columns] = nb_ref[l].reshape(
@@ -541,6 +567,45 @@
                 2 * columns, features
             )
 
+    @pl.when(step < feeds)
+    def _():
+        feed_step(
+            step, edge_ref, d_act_ref, we_ref, be_ref, taps_ref, bm_ref, small_ref,
+            nb_wide, hidden, wide, d_wide, act_s, d_hid_s, nb_ref.shape,
+        )
+        for c in out_copies(step):
+            c.start()
+
+    @pl.when(step == feeds)
+    def _():
+        for c in weights:
+            c.wait()
+
+    @pl.when(step >= feeds)
+    def _():
+        turn_step(
+            step, feeds, turns, middle_ref, attended_ref, g_ref, gate_b_ref, scale_ref, gate_a_ref,
+            shrink_ref, mixed_refs, result_ref, d_middle_ref, d_mixed_refs, gw_ref, sums_ref,
+            act_s, d_hid_s, ws, we, wo, gw_sum, grouped, branch_s, e_s, sums,
+        )
+
+    @pl.when(step == pl.num_programs(0) - 1)
+    def _():
+        for n in range(feeds):
+            for c in out_copies(n):
+                c.wait()
+
+
+def feed_step(
+    step, edge_ref, d_act_ref, we_ref, be_ref, taps_ref, bm_ref, small_ref,
+    nb_wide, hidden, wide, d_wide, act_s, d_hid_s, shape,
+):
+    count, rows, columns, features = shape
+    sub = columns // COLUMN_PARTS
+    block = we_ref.shape[1]
+    own = rows * columns
+    tall = (rows + 4) * columns
+    mid = (rows + 2) * columns
     hidden[...] = (dot(nb_wide[...], we_ref[...]) + be_ref[...]).astype(bfloat)
     small_ref[...] = jnp.zeros_like(small_ref)
 
@@ -551,6 +616,9 @@
     def _(index):
         l = index // (block // LANES)
         at = pl.ds(pl.multiple_of((index % (block // LANES)) * LANES, LANES), LANES)
+        out = pl.ds(
+            pl.multiple_of(step * block + index % (block // LANES) * LANES, LANES), LANES
+        )
         taps = [taps_ref[t : t + 1, at] for t in range(9)]
         bias = bm_ref[:, at]
         for row in range(rows + 4):
@@ -568,8 +636,8 @@
             gelu = v * half
             slope = half + gelu * (1.0 - half) * (6.0 * cube + 2.0 * c0)
             if 1 <= row <= rows:
-                act_ref[
-                    pl.ds(pl.multiple_of(l * own + (row - 1) * columns, columns), columns), at
+                act_s[
+                    pl.ds(pl.multiple_of(l * own + (row - 1) * columns, columns), columns), out
                 ] = gelu.reshape(columns, LANES).astype(bfloat)
             grad = d_act_ref[pl.ds(pl.multiple_of(l * mid + row * columns, columns), columns), at]
             grad = grad.astype(single).reshape(COLUMN_PARTS, sub, LANES) * slope
@@ -577,7 +645,7 @@
         sums = [jnp.zeros((sub, LANES), single) for _ in range(11)]
         for row in range(rows):
             d_in = conv_back_row(d_wide, row, taps).astype(bfloat)
-            d_hid_ref[pl.ds(pl.multiple_of(l * own + row * columns, columns), columns), at] = (
+            d_hid_s[pl.ds(pl.multiple_of(l * own + row * columns, columns), columns), out] = (
                 d_in.reshape(columns, LANES)
             )
             center = d_wide[row + 1, 1 : COLUMN_PARTS + 1]
@@ -592,156 +660,26 @@
             small_ref[t : t + 1, at] += jnp.sum(sums[t], axis=0, keepdims=True)
 
 
-def feed_forward(edge, nb, top, bottom, d_act, we, be, taps, bm):
-    count, rows, columns, features = nb.shape
-    hidden = we.shape[1]
-    block = features
-    steps = hidden // block
-    tokens = count * rows * columns
-    tall = count * (rows + 4) * columns
-    mid = count * (rows + 2) * columns
+def turn_step(
+    step, feeds, turns, middle_ref, attended_ref, g_ref, gate_b_ref, scale_ref, gate_a_ref,
+    shrink_ref, mixed_refs, result_ref, d_middle_ref, d_mixed_refs, gw_ref, sums_ref,
+    act_s, d_hid_s, ws, we, wo, gw_sum, grouped, branch_s, e_s, sums,
+):
+    columns, features = g_ref.shape[2:]
     sub = columns // COLUMN_PARTS
-    whole = lambda a: pl.BlockSpec(a.shape, lambda s: (0,) * a.ndim)
-    column = lambda n: pl.BlockSpec((n, block), lambda s: (0, s))
-    return pl.pallas_call(
-        feed_kernel,
-        grid=(steps,),
-        in_specs=[
-            pl.BlockSpec(memory_space=pltpu.SMEM),
-            whole(nb), whole(top), whole(bottom),
-            column(mid), column(features), column(1), column(16), column(1),
-        ],
-        out_specs=[column(tokens), column(tokens), column(16)],
-        out_shape=[
-            jax.ShapeDtypeStruct((tokens, hidden), bfloat),
-            jax.ShapeDtypeStruct((tokens, hidden), bfloat),
-            jax.ShapeDtypeStruct((16, hidden), single),
-        ],
-        scratch_shapes=[
-            pltpu.VMEM((tall, features), bfloat),
-            pltpu.VMEM((tall, block), bfloat),
-            pltpu.VMEM((rows + 4, COLUMN_PARTS + 2, sub, LANES), bfloat),
-            pltpu.VMEM((rows + 2, COLUMN_PARTS + 2, sub, LANES), bfloat),
-        ],
-        compiler_params=params(60),
-        cost_estimate=cost(
-            2 * features * hidden * tall,
-            8 * tokens * features + 4 * features * hidden + 6 * tokens * hidden,
-            mid * hidden,
-        ),
-        name="feed_forward",
-    )(edge, nb, top, bottom, d_act, we, be, taps, bm)
-
-
-def feed_grads_kernel(
-    act_ref, d_hid_ref, nb_ref, db_ref, out_ref, db_own, shrink_s, expand_s, shrink_sem, expand_sem
-):
-    count, rows, columns, features = nb_ref.shape
-    own = rows * columns
-    step = pl.program_id(0)
-    steps = pl.num_programs(0)
-    some, slots, unit = shrink_s.shape[:3]
-
-    @pl.when(step == 0)
-    def _():
-        for l in range(count):
-            db_own[l * own : (l + 1) * own] = db_ref[l, 1 : rows + 1].reshape(own, features)
-
-    def copies(s):
-        return (
-            pltpu.make_async_copy(
-                shrink_s, out_ref.at[pl.ds(s * some, some), pl.ds(0, slots)], shrink_sem
-            ),
-            pltpu.make_async_copy(expand_s, out_ref.at[:, slots + s], expand_sem),
-        )
-
-    shrink = dot_tn(act_ref[...], db_own[...])
-    expand = dot_tn(nb_ref[...].reshape(count * own, features), d_hid_ref[...])
-
-    @pl.when(step > 0)
-    def _():
-        for c in copies(step - 1):
-            c.wait()
-
-    shrink_s[...] = shrink.reshape(shrink_s.shape).astype(bfloat)
-    expand_s[...] = expand.reshape(expand_s.shape).astype(bfloat)
-    for c in copies(step):
-        c.start()
-
-    @pl.when(step == steps - 1)
-    def _():
-        for c in copies(step):
-            c.wait()
-
-
-def feed_grads(act, d_hid, nb, db, devices):
-    count, rows, columns, features = nb.shape
-    tokens, hidden = act.shape
-    block = features
-    steps = hidden // block
-    unit = features // devices
-    if unit % 8:
-        shrink = dot_tn(act, db[:, 1:-1].reshape(tokens, features))
-        expand = dot_tn(nb.reshape(tokens, features), d_hid)
-        return jnp.concatenate(
-            [
-                shrink.reshape(devices, steps, unit, features),
-                expand.reshape(devices, unit, steps, features).transpose(0, 2, 1, 3),
-            ],
-            axis=1,
-        ).astype(bfloat)
-    whole = lambda a: pl.BlockSpec(a.shape, lambda s: (0,) * a.ndim)
-    return pl.pallas_call(
-        feed_grads_kernel,
-        grid=(steps,),
-        in_specs=[
-            pl.BlockSpec((tokens, block), lambda s: (0, s)),
-            pl.BlockSpec((tokens, block), lambda s: (0, s)),
-            whole(nb), whole(db),
-        ],
-        out_specs=pl.BlockSpec(memory_space=pl.ANY),
-        out_shape=jax.ShapeDtypeStruct((devices, 2 * steps, unit, features), bfloat),
-        scratch_shapes=[
-            pltpu.VMEM((tokens, features), bfloat),
-            pltpu.VMEM((devices // steps, steps, unit, features), bfloat),
-            pltpu.VMEM((devices, unit, features), bfloat),
-            pltpu.SemaphoreType.DMA,
-            pltpu.SemaphoreType.DMA,
-        ],
-        compiler_params=params(60),
-        cost_estimate=cost(4 * features * hidden * tokens, 8 * features * hidden + 4 * tokens * hidden),
-        name="feed_grads",
-    )(act, d_hid, nb, db)
-
-
-TURN_ROWS = 4
-
-
-def turn_kernel(parts, *refs):
-    (
-        act_ref, d_hid_ref, middle_ref, attended_ref, g_ref,
-        gate_b_ref, scale_ref, gate_a_ref, bias_ref, weight_ref, ws_ref, we_ref,
-    ) = refs[:12]
-    mixed_refs = refs[12 : 12 + parts]
-    result_ref, d_middle_ref = refs[12 + parts : 14 + parts]
-    d_mixed_refs = refs[14 + parts : 14 + 2 * parts]
-    gw_ref, sums_ref, gw_sum, grouped, branch_s, e_s, sums = refs[14 + 2 * parts :]
-    rows, columns, features = g_ref.shape[1:]
-    sub = columns // COLUMN_PARTS
+    rows = g_ref.shape[1]
     quarter = rows * columns // 4
     back = column_order(columns, True)
     gate_b = gate_b_ref[0]
     scale = 1.0 + scale_ref[0]
     gate_a = gate_a_ref[0]
-    first = (pl.program_id(0) == 0) & (pl.program_id(1) == 0)
-    last = (pl.program_id(0) == pl.num_programs(0) - 1) & (
-        pl.program_id(1) == pl.num_programs(1) - 1
-    )
-
-    branch_s[...] = dot(act_ref[...], ws_ref[...]) + bias_ref[...]
-    e_s[...] = dot_nt(d_hid_ref[...], we_ref[...])
-
-    @pl.when(pl.program_id(1) == 0)
+    piece_of = step - feeds
+    lines = pl.ds(pl.multiple_of(piece_of * rows * columns, rows * columns), rows * columns)
+
+    branch_s[...] = dot(act_s[lines], ws[...]) + shrink_ref[...]
+    e_s[...] = dot_nt(d_hid_s[lines], we[...])
+
+    @pl.when(piece_of % turns == 0)
     def _():
         sums[...] = jnp.zeros_like(sums)
 
@@ -779,50 +717,74 @@
     for mixed_ref, d_ref in zip(mixed_refs, d_mixed_refs):
         width = mixed_ref.shape[-1]
         piece = slice(at, at + width)
-        d_ref[0] = dot_nt(grad, weight_ref[piece]).astype(bfloat).reshape(4, quarter, width)
+        d_ref[0] = dot_nt(grad, wo[piece]).astype(bfloat).reshape(4, quarter, width)
         part = dot_tn(mixed_ref[0].reshape(4 * quarter, width), grad)
 
-        @pl.when(first)
+        @pl.when(piece_of == 0)
         def _():
             gw_sum[piece] = part
 
-        @pl.when(jnp.logical_not(first))
+        @pl.when(piece_of > 0)
         def _():
             gw_sum[piece] += part
 
         at += width
 
-    @pl.when(last)
+    @pl.when(step == pl.num_programs(0) - 1)
     def _():
         gw_ref[...] = gw_sum[...].astype(bfloat)
 
 
-def turn(
-    act, d_hid, middle, attended, g, gate_b, scale, gate_a, bias, weight, shrink, expand, mixed
+def feed_turn(
+    edge, nb, top, bottom, d_act, we, be, taps, bm, ws, middle, attended, g, gate_b, scale, gate_a,
+    shrink_bias, wo, mixed,
 ):
-    count, rows, columns, features = g.shape
-    hidden = act.shape[1]
-    step = min(TURN_ROWS, rows)
-    steps = rows // step
-    quarter = step * columns // 4
-    image = pl.BlockSpec((1, step, columns, features), lambda l, r: (l, r, 0, 0))
-    flat = pl.BlockSpec((step * columns, hidden), lambda l, r: (l * steps + r, 0))
-    vector = pl.BlockSpec((1, 1, features), lambda l, r: (l, 0, 0))
+    count, rows, columns, features = nb.shape
+    hidden = we.shape[1]
+    block = features
+    feeds = hidden // block
+    tokens = count * rows * columns
+    tall = count * (rows + 4) * columns
+    mid = count * (rows + 2) * columns
+    sub = columns // COLUMN_PARTS
+    some = min(TURN_ROWS, rows)
+    turns = rows // some
+    quarter = some * columns // 4
+    whole = lambda a: pl.BlockSpec(a.shape, lambda s: (0,) * a.ndim)
+    feed = lambda s: jnp.minimum(s, feeds - 1)
+    place = lambda s: jnp.maximum(s - feeds, 0)
+    column = lambda n: pl.BlockSpec((n, block), lambda s: (0, feed(s)))
+    image = pl.BlockSpec(
+        (1, some, columns, features), lambda s: (place(s) // turns, place(s) % turns, 0, 0)
+    )
+    vector = pl.BlockSpec((1, 1, features), lambda s: (place(s) // turns, 0, 0))
     groups = [
-        pl.BlockSpec((1, 4, quarter, m.shape[-1]), lambda l, r: (l, 0, r, 0)) for m in mixed
+        pl.BlockSpec(
+            (1, 4, quarter, m.shape[-1]), lambda s: (place(s) // turns, 0, place(s) % turns, 0)
+        )
+        for m in mixed
     ]
-    whole = lambda a: pl.BlockSpec(a.shape, lambda l, r: (0,) * a.ndim)
-    square = pl.BlockSpec((features, features), lambda l, r: (0, 0))
+    hbm = pl.BlockSpec(memory_space=pl.ANY)
     return pl.pallas_call(
-        partial(turn_kernel, len(mixed)),
-        grid=(count, steps),
-        in_specs=[flat, flat, image, image, image, vector, vector, vector]
-        + [whole(bias), square, whole(shrink), whole(expand)]
+        partial(feed_turn_kernel, len(mixed), feeds, turns),
+        grid=(feeds + count * turns,),
+        in_specs=[
+            pl.BlockSpec(memory_space=pltpu.SMEM),
+            whole(nb), whole(top), whole(bottom),
+            column(mid), column(features), column(1), column(16), column(1),
+            image, image, image, vector, vector, vector, whole(shrink_bias), hbm, hbm, hbm,
+        ]
         + groups,
-        out_specs=[image, image]
+        out_specs=[column(16), hbm, hbm, image, image]
         + groups
-        + [square, pl.BlockSpec((1, 8, features), lambda l, r: (l, 0, 0))],
+        + [
+            pl.BlockSpec((features, features), lambda s: (0, 0)),
+            pl.BlockSpec((1, 8, features), lambda s: (place(s) // turns, 0, 0)),
+        ],
         out_shape=[
+            jax.ShapeDtypeStruct((16, hidden), single),
+            jax.ShapeDtypeStruct((tokens, hidden), bfloat),
+            jax.ShapeDtypeStruct((tokens, hidden), bfloat),
             jax.ShapeDtypeStruct(g.shape, bfloat),
             jax.ShapeDtypeStruct(g.shape, single),
         ]
@@ -832,16 +794,116 @@
             jax.ShapeDtypeStruct((count, 8, features), single),
         ],
         scratch_shapes=[
+            pltpu.VMEM((tall, features), bfloat),
+            pltpu.VMEM((tall, block), bfloat),
+            pltpu.VMEM((rows + 4, COLUMN_PARTS + 2, sub, LANES), bfloat),
+            pltpu.VMEM((rows + 2, COLUMN_PARTS + 2, sub, LANES), bfloat),
+            pltpu.VMEM((tokens, hidden), bfloat),
+            pltpu.VMEM((tokens, hidden), bfloat),
+            pltpu.VMEM((hidden, features), bfloat),
+            pltpu.VMEM((features, hidden), bfloat),
+            pltpu.VMEM((features, features), bfloat),
             pltpu.VMEM((features, features), single),
             pltpu.VMEM((4, quarter, features), bfloat),
-            pltpu.VMEM((step * columns, features), single),
-            pltpu.VMEM((step * columns, features), single),
+            pltpu.VMEM((some * columns, features), single),
+            pltpu.VMEM((some * columns, features), single),
             pltpu.VMEM((5, 8, features), single),
+            pltpu.SemaphoreType.DMA((3,)),
+            pltpu.SemaphoreType.DMA((feeds,)),
+            pltpu.SemaphoreType.DMA((feeds,)),
+        ],
+        compiler_params=params(62),
+        cost_estimate=cost(
+            2 * features * hidden * (tall + 2 * tokens) + 4 * g.size * features,
+            30 * g.size + 8 * features * hidden + 6 * tokens * hidden,
+            mid * hidden,
+        ),
+        name="feed_turn",
+    )(
+        edge, nb, top, bottom, d_act, we, be, taps, bm, middle, attended, g, gate_b, scale, gate_a,
+        shrink_bias, ws, we, wo, *mixed,
+    )
+
+
+def feed_grads_kernel(
+    act_ref, d_hid_ref, nb_ref, db_ref, out_ref, db_own, shrink_s, expand_s, shrink_sem, expand_sem
+):
+    count, rows, columns, features = nb_ref.shape
+    own = rows * columns
+    step = pl.program_id(0)
+    steps = pl.num_programs(0)
+    some, slots, unit = shrink_s.shape[:3]
+
+    @pl.when(step == 0)
+    def _():
+        for l in range(count):
+            db_own[l * own : (l + 1) * own] = db_ref[l, 1 : rows + 1].reshape(own, features)
+
+    def copies(s):
+        return (
+            pltpu.make_async_copy(
+                shrink_s, out_ref.at[pl.ds(s * some, some), pl.ds(0, slots)], shrink_sem
+            ),
+            pltpu.make_async_copy(expand_s, out_ref.at[:, slots + s], expand_sem),
+        )
+
+    shrink = dot_tn(act_ref[...], db_own[...])
+    expand = dot_tn(nb_ref[...].reshape(count * own, features), d_hid_ref[...])
+
+    @pl.when(step > 0)
+    def _():
+        for c in copies(step - 1):
+            c.wait()
+
+    shrink_s[...] = shrink.reshape(shrink_s.shape).astype(bfloat)
+    expand_s[...] = expand.reshape(expand_s.shape).astype(bfloat)
+    for c in copies(step):
+        c.start()
+
+    @pl.when(step == steps - 1)
+    def _():
+        for c in copies(step):
+            c.wait()
+
+
+def feed_grads(act, d_hid, nb, db, devices):
+    count, rows, columns, features = nb.shape
+    tokens, hidden = act.shape
+    block = features
+    steps = hidden // block
+    unit = features // devices
+    if unit % 8:
+        shrink = dot_tn(act, db[:, 1:-1].reshape(tokens, features))
+        expand = dot_tn(nb.reshape(tokens, features), d_hid)
+        return jnp.concatenate(
+            [
+                shrink.reshape(devices, steps, unit, features),
+                expand.reshape(devices, unit, steps, features).transpose(0, 2, 1, 3),
+            ],
+            axis=1,
+        ).astype(bfloat)
+    whole = lambda a: pl.BlockSpec(a.shape, lambda s: (0,) * a.ndim)
+    return pl.pallas_call(
+        feed_grads_kernel,
+        grid=(steps,),
+        in_specs=[
+            pl.BlockSpec((tokens, block), lambda s: (0, s)),
+            pl.BlockSpec((tokens, block), lambda s: (0, s)),
+            whole(nb), whole(db),
+        ],
+        out_specs=pl.BlockSpec(memory_space=pl.ANY),
+        out_shape=jax.ShapeDtypeStruct((devices, 2 * steps, unit, features), bfloat),
+        scratch_shapes=[
+            pltpu.VMEM((tokens, features), bfloat),
+            pltpu.VMEM((devices // steps, steps, unit, features), bfloat),
+            pltpu.VMEM((devices, unit, features), bfloat),
+            pltpu.SemaphoreType.DMA,
+            pltpu.SemaphoreType.DMA,
         ],
         compiler_params=params(60),
-        cost_estimate=cost(4 * g.size * (features + hidden), 20 * g.size + 4 * act.size),
-        name="turn",
-    )(act, d_hid, middle, attended, g, gate_b, scale, gate_a, bias, weight, shrink, expand, *mixed)
+        cost_estimate=cost(4 * features * hidden * tokens, 8 * features * hidden + 4 * tokens * hidden),
+        name="feed_grads",
+    )(act, d_hid, nb, db)
 
 
 def final_kernel(
@@ -1337,7 +1399,7 @@
     attended, middle, normed_b, first_rows, last_rows = middle_part(
         mixed, output_weight, output_line, kept, gate_a, scale_b, shift_b
     )
-    act, d_hid, feed_small = feed_forward(
+    feed_small, act, d_hid, *turned = feed_turn(
         edge,
         normed_b,
         from_above(last_rows),
@@ -1347,10 +1409,16 @@
         expand_line,
         mixer_taps,
         mixer_line,
-    )
-    turned = turn(
-        act, d_hid, middle, attended, g_kept, gate_b, scale_b, gate_a, shrink_line,
-        output_weight, shrink_weight, expand_weight, mixed,
+        shrink_weight,
+        middle,
+        attended,
+        g_kept,
+        gate_b,
+        scale_b,
+        gate_a,
+        shrink_line,
+        output_weight,
+        mixed,
     )
     result, d_middle = turned[:2]
     d_mixed = turned[2:-2]

time: 478 us -> 468 us (0.979)
  waiting for transfers between devices: 73.6 us -> 79.9 us
  local copies, waits for them, and re-layouts: 68.2 us -> 62.2 us
  Pallas kernels: 223 us -> 218 us
    all_to_all x3, waiting for transfers between devices: 15.4 us -> 22.3 us  [spread(): got = lax.all_to_all(flat, 'strips', 0, 0, tiled=True)]
    pallas_call x2 -> x1, Pallas kernels: 74.9 us -> 69.1 us  [feed_turn(): pl.pallas_call(partial(feed_turn_kernel, len(mixed), feeds, turns), grid=...]
    unnamed x88 -> x92, local copies, waits for them, and re-layouts: 31.7 us -> 31.2 us
  transfers between devices with their start and end apart: 22 -> 22, of which waited for: 8 -> 9; matrix products, arithmetic and copies ran while one was open for 13% -> 11% of each run, Pallas kernels for 26% -> 26%
where the time goes in v4:
time: 468 us; the launch traced here: 465 us
  Pallas kernels  218 us (47%)
  waiting for transfers between devices  79.9 us (17%)
  starting transfers between devices  72.1 us (15%)
  local copies, waits for them, and re-layouts  62.2 us (13%)
  other arithmetic  17.1 us (4%)
  between operations  15.1 us (3%)
    pallas_call x1, Pallas kernels, feed_turn(): pl.pallas_call(partial(feed_turn_kernel, len(mixed), feeds, turns), grid=...  69.1 us
    all_to_all x3, waiting for transfers between devices, collect(): return lax.all_to_all(flat, 'strips', 0, 0, tiled=True)  45.4 us
    pallas_call x2, Pallas kernels, attend_back(): pl.pallas_call(attend_back_kernel, grid=(pairs,), in_specs=[column] * 5 +...  36.3 us
    unnamed x92, local copies, waits for them, and re-layouts  31.2 us
    pallas_call x2, Pallas kernels, attend(): pl.pallas_call(attend_kernel, grid=(pairs,), in_specs=[pl.BlockSpec((toke...  30.8 us
    all_to_all x3, starting transfers between devices, collect(): return lax.all_to_all(flat, 'strips', 0, 0, tiled=True)  23.4 us
    all_to_all x3, waiting for transfers between devices, spread(): got = lax.all_to_all(flat, 'strips', 0, 0, tiled=True)  22.3 us
    all_to_all x3, starting transfers between devices, spread(): got = lax.all_to_all(flat, 'strips', 0, 0, tiled=True)  19.1 us
  transfers between devices with their start and end apart: 22, of which 9 were waited for; matrix products, arithmetic and copies ran while one was open for 11% of the time, Pallas kernels for 26%

profile of v4, /device:TPU:0, one launch (start us, length us, event | category | flops | bytes accessed | tf_op | source)
XLA Modules:
  0.0 464.9 jit_solution(2144238019394488272)
XLA Ops:
  28.2 5.8 %front.1 = (bf16[2,4,128,768]{3,2,1,0:T(8,128)(2,1)}, bf16[2,10,64,768]{3,2,1,0:T(8,128)(2,1)S(1)}, bf16[2,8,64,768]{3,2,1,0:T(8,128)(2,1)S(1)}) custom-call(f32[2]{0:T(128)S(1)} %add_convert_fusion.1.edge_ref.refs_0_, bf16[2,8,64,768]{3,2,1,0:T(8,128)(2,1)S(1)} %copy-done.5, bf16[2,1,64,768]{3,2,1,0:T(8,128)(2,1)S(1)} %get-tuple-element.179.top_ref, ...), custom_call_target="tpu_custom_call" | custom-call | flops 117964800 | bytes 6291456 | tf_op jit(solution)/shard_map/front/pallas_call | solution.py:162
  36.6 6.4 %all-to-all-start = ((bf16[8,128,768]{2,1,0:T(8,128)(2,1)}), bf16[8,128,768]{2,1,0:T(8,128)(2,1)}, u32[]{:S(2)}, u32[]{:S(2)}) async-start(bf16[8,128,768]{2,1,0:T(8,128)(2,1)} %bitcast.6), calls=%async_computation | async-start | bytes 3145728 | tf_op jit(solution)/shard_map/all_to_all | solution.py:1350
  51.6 10.7 %feed_upstream.1.refs_4_ = bf16[1280,3072]{1,0:T(8,128)(2,1)} custom-call(bf16[1280,768]{1,0:T(8,128)(2,1)} %bitcast.113, bf16[3072,768]{1,0:T(8,128)(2,1)} %refs_16_.1), custom_call_target="tpu_custom_call" | custom-call | flops 6039797760 | bytes 9830400 | tf_op jit(solution)/shard_map/feed_upstream/pallas_call | solution.py:506
  62.3 18.7 %all-to-all-done = bf16[8,128,768]{2,1,0:T(8,128)(2,1)} async-done(((bf16[8,128,768]{2,1,0:T(8,128)(2,1)}), bf16[8,128,768]{2,1,0:T(8,128)(2,1)}, u32[]{:S(2)}, u32[]{:S(2)}) %all-to-all-start) | async-done | bytes 1572896 | tf_op jit(solution)/shard_map/all_to_all | solution.py:1350
  80.9 15.4 %attend.2 = (bf16[1024,384]{1,0:T(8,128)(2,1)}, bf16[1024,384]{1,0:T(8,128)(2,1)}, bf16[1024,384]{1,0:T(8,128)(2,1)}, bf16[1024,384]{1,0:T(8,128)(2,1)}, f32[3,2,1024]{2,1,0:T(2,128)}) custom-call(bf16[1024,768]{1,0:T(8,128)(2,1)} %bitcast.7.x_ref.refs_0_, bf16[768,2304]{1,0:T(8,128)(2,1)} %refs_6_.1, bf16[768,2304]{1,0:T(8,128)(2,1)} %refs_6_.1, ...), custom_call_target="tpu_custom_call" | custom-call | flops 8254390272 | bytes 6488064 | tf_op jit(solution)/shard_map/attend/pallas_call | solution.py:271
  96.3 14.7 %all-to-all-start.1 = ((bf16[8,128,384]{2,1,0:T(8,128)(2,1)}), bf16[8,128,384]{2,1,0:T(8,128)(2,1)S(1)}, u32[]{:S(2)}, u32[]{:S(2)}) async-start(bf16[8,128,384]{2,1,0:T(8,128)(2,1)} %bitcast.123), calls=%async_computation.1 | async-start | bytes 1572864 | tf_op jit(solution)/shard_map/all_to_all | solution.py:1355
  111.1 15.4 %attend.3 = (bf16[1024,384]{1,0:T(8,128)(2,1)}, bf16[1024,384]{1,0:T(8,128)(2,1)}, bf16[1024,384]{1,0:T(8,128)(2,1)}, bf16[1024,384]{1,0:T(8,128)(2,1)}, f32[3,2,1024]{2,1,0:T(2,128)}) custom-call(bf16[1024,768]{1,0:T(8,128)(2,1)} %bitcast.7.x_ref.refs_0_, bf16[768,2304]{1,0:T(8,128)(2,1)} %refs_6_.1, bf16[768,2304]{1,0:T(8,128)(2,1)} %refs_6_.1, ...), custom_call_target="tpu_custom_call" | custom-call | flops 8254390272 | bytes 6488064 | tf_op jit(solution)/shard_map/attend/pallas_call | solution.py:271
  126.5 5.2 %all-to-all-done.1 = bf16[8,128,384]{2,1,0:T(8,128)(2,1)S(1)} async-done(((bf16[8,128,384]{2,1,0:T(8,128)(2,1)}), bf16[8,128,384]{2,1,0:T(8,128)(2,1)S(1)}, u32[]{:S(2)}, u32[]{:S(2)}) %all-to-all-start.1) | async-done | bytes 786464 | tf_op jit(solution)/shard_map/all_to_all | solution.py:1355
  137.8 18.3 %all-to-all-done.2 = bf16[8,128,384]{2,1,0:T(8,128)(2,1)S(1)} async-done(((bf16[8,128,384]{2,1,0:T(8,128)(2,1)}), bf16[8,128,384]{2,1,0:T(8,128)(2,1)S(1)}, u32[]{:S(2)}, u32[]{:S(2)}) %all-to-all-start.2) | async-done | bytes 786464 | tf_op jit(solution)/shard_map/all_to_all | solution.py:1355
  157.0 6.5 %middle.1 = (f32[2,8,64,768]{3,2,1,0:T(8,128)}, f32[2,8,64,768]{3,2,1,0:T(8,128)}, bf16[2,8,64,768]{3,2,1,0:T(8,128)(2,1)}, bf16[2,2,64,768]{3,2,1,0:T(8,128)(2,1)}, bf16[2,2,64,768]{3,2,1,0:T(8,128)(2,1)}) custom-call(bf16[2,4,128,384]{3,2,1,0:T(8,128)(2,1)} %bitcast.124, bf16[2,4,128,384]{3,2,1,0:T(8,128)(2,1)} %bitcast.126, bf16[768,768]{1,0:T(8,128)(2,1)} %refs_18_.1, ...), custom_call_target="tpu_custom_call" | custom-call | flops 1207959552 | bytes 11010048 | tf_op jit(solution)/shard_map/middle/pallas_call | solution.py:472
  169.8 69.1 %feed_turn.1 = (f32[16,3072]{1,0:T(8,128)}, bf16[1024,3072]{1,0:T(8,128)(2,1)}, bf16[1024,3072]{1,0:T(8,128)(2,1)}, bf16[2,8,64,768]{3,2,1,0:T(8,128)(2,1)}, f32...) custom-call(f32[2]{0:T(128)} %copy-done.13, ...), custom_call_target="tpu_custom_call" | custom-call | flops 19327352832 | bytes 61341696 | tf_op jit(solution)/shard_map/feed_turn/pallas_call | solution.py:768
  238.9 7.9 %all-to-all-start.3 = ((bf16[8,128,384]{2,1,0:T(8,128)(2,1)}), bf16[8,128,384]{2,1,0:T(8,128)(2,1)}, u32[]{:S(2)}, u32[]{:S(2)}) async-start(bf16[8,128,384]{2,1,0:T(8,128)(2,1)} %bitcast.129), calls=%async_computation.3 | async-start | bytes 1572864 | tf_op jit(solution)/shard_map/all_to_all | solution.py:1350
  250.9 16.1 %feed_grads.1 = bf16[32,8,24,768]{3,2,1,0:T(8,128)(2,1)} custom-call(bf16[1024,3072]{1,0:T(8,128)(2,1)} %get-tuple-element.114.act_ref, bf16[1024,3072]{1,0:T(8,128)(2,1)} %get-tuple-element.115.d_hid_ref, bf16[2,8,64,768]{3,2,1,0:T(8,128)(2,1)} %get-tuple-element.98.refs_1_.nb_ref, bf16[2,10,64,768]{3,2,1,0:T(8,128)(2,1)} %copy-done.14), custom_call_target="tpu_custom_call" | custom-call | flops 9663676416 | bytes 31457280 | tf_op jit(solution)/shard_map/feed_grads/pallas_call | solution.py:886
  268.0 4.7 %all-to-all-start.4 = ((bf16[8,128,384]{2,1,0:T(8,128)(2,1)}), bf16[8,128,384]{2,1,0:T(8,128)(2,1)}, u32[]{:S(2)}, u32[]{:S(2)}) async-start(bf16[8,128,384]{2,1,0:T(8,128)(2,1)} %bitcast.128), calls=%async_computation.4 | async-start | bytes 1572864 | tf_op jit(solution)/shard_map/all_to_all | solution.py:1350
  272.7 18.2 %attend_back.2 = (bf16[1024,384]{1,0:T(8,128)(2,1)}, bf16[1024,384]{1,0:T(8,128)(2,1)}, bf16[1024,384]{1,0:T(8,128)(2,1)}) custom-call(bf16[1024,384]{1,0:T(8,128)(2,1)} %get-tuple-element.110.q_ref, bf16[1024,384]{1,0:T(8,128)(2,1)} %get-tuple-element.111.k_ref, bf16[1024,384]{1,0:T(8,128)(2,1)} %get-tuple-element.112.v_ref, ...), custom_call_target="tpu_custom_call" | custom-call | flops 16106127360 | bytes 6291456 | tf_op jit(solution)/shard_map/attend_back/pallas_call | solution.py:332
  300.0 18.1 %attend_back.3 = (bf16[1024,384]{1,0:T(8,128)(2,1)}, bf16[1024,384]{1,0:T(8,128)(2,1)}, bf16[1024,384]{1,0:T(8,128)(2,1)}) custom-call(bf16[1024,384]{1,0:T(8,128)(2,1)} %get-tuple-element.121.q_ref, bf16[1024,384]{1,0:T(8,128)(2,1)} %get-tuple-element.122.k_ref, bf16[1024,384]{1,0:T(8,128)(2,1)} %get-tuple-element.123.v_ref, ...), custom_call_target="tpu_custom_call" | custom-call | flops 16106127360 | bytes 6291456 | tf_op jit(solution)/shard_map/attend_back/pallas_call | solution.py:332
  318.1 9.2 %regroup.1 = bf16[1024,768]{1,0:T(8,128)(2,1)} custom-call(bf16[1024,384]{1,0:T(8,128)(2,1)} %get-tuple-element.118.refs_0_.refs_2_, bf16[1024,384]{1,0:T(8,128)(2,1)} %get-tuple-element.119.refs_1_.refs_3_, bf16[1024,384]{1,0:T(8,128)(2,1)} %get-tuple-element.120.refs_2_.refs_4_, bf16[1024,384]{1,0:T(8,128)(2,1)} %get-tuple-element.126.refs_3_.refs_5_, ...), custom_call_target="tpu_custom_call" | custom-call | flops 3623878656 | bytes 6291456 | tf_op jit(solution)/shard_map/regroup/pallas_call | solution.py:365
  327.3 5.1 %all-to-all-start.5 = ((bf16[8,128,768]{2,1,0:T(8,128)(2,1)}), bf16[8,128,768]{2,1,0:T(8,128)(2,1)}, u32[]{:S(2)}, u32[]{:S(2)}) async-start(bf16[8,128,768]{2,1,0:T(8,128)(2,1)} %bitcast.119), calls=%async_computation.5 | async-start | bytes 3145728 | tf_op jit(solution)/shard_map/all_to_all | solution.py:1355
  332.4 10.0 %input_grad.1 = (bf16[768,3072]{1,0:T(8,128)(2,1)}, f32[8,1536]{1,0:T(8,128)}) custom-call(bf16[1024,768]{1,0:T(8,128)(2,1)} %bitcast.7.x_ref.refs_0_, bf16[768,768]{1,0:T(8,128)(2,1)} %get-tuple-element.135.refs_1_, bf16[1024,384]{1,0:T(8,128)(2,1)} %get-tuple-element.118.refs_0_.refs_2_, bf16[1024,384]{1,0:T(8,128)(2,1)} %get-tuple-element.119.refs_1_.refs_3_, ...), custom_call_target="tpu_custom_call" | custom-call | flops 3623878656 | bytes 7864320 | tf_op jit(solution)/shard_map/input_grad/pallas_call | solution.py:406
  342.4 4.9 %dynamic-slice_bitcast_fusion = (bf16[4,4,24,3072]{3,2,1,0:T(8,128)(2,1)}, bf16[4,4,24,3072]{3,2,1,0:T(8,128)(2,1)}) fusion(bf16[4,4,2,24,3072]{4,3,2,1,0:T(8,128)(2,1)} %bitcast.114, s32[]{:T(128)S(6)} %select_n.75, s32[]{:T(128)S(6)} %select_n.74), kind=kLoop, calls=%fused_computation.1 | loop fusion | bytes 9437192 | tf_op jit(solution)/shard_map/jit(dynamic_index_in_dim)/squeeze | solution.py:1491
  360.7 21.9 %all-to-all-done.5 = bf16[8,128,768]{2,1,0:T(8,128)(2,1)} async-done(((bf16[8,128,768]{2,1,0:T(8,128)(2,1)}), bf16[8,128,768]{2,1,0:T(8,128)(2,1)}, u32[]{:S(2)}, u32[]{:S(2)}) %all-to-all-start.5) | async-done | bytes 1572896 | tf_op jit(solution)/shard_map/all_to_all | solution.py:1355
  400.1 13.2 %final.1 = (bf16[2,8,64,768]{3,2,1,0:T(8,128)(2,1)}, f32[16,768]{1,0:T(8,128)}, f32[2,8,768]{2,1,0:T(8,128)}) custom-call(bf16[2,4,128,768]{3,2,1,0:T(8,128)(2,1)} %bitcast.25.d_ref, bf16[2,2,32,768]{3,2,1,0:T(8,128)(2,1)} %copy-done.22, bf16[2,2,32,768]{3,2,1,0:T(8,128)(2,1)} %copy-done.23, bf16[2,10,64,768]{3,2,1,0:T(8,128)(2,1)} %copy-done.7, ...), custom_call_target="tpu_custom_call" | custom-call | flops 141557760 | bytes 9437184 | tf_op jit(solution)/shard_map/final/pallas_call | solution.py:1004
  419.5 5.8 %all-to-all-start.7 = ((bf16[32,2,1728]{2,1,0:T(2,128)(2,1)}), bf16[32,2,1728]{2,1,0:T(2,128)(2,1)S(1)}, u32[]{:S(2)}, u32[]{:S(2)}) async-start(bf16[32,2,1728]{2,1,0:T(2,128)(2,1)} %reshape.402), calls=%async_computation.7 | async-start | bytes 458752 | tf_op jit(solution)/shard_map/all_to_all | solution.py:1533
  426.5 10.2 %all-to-all-done.7 = bf16[32,2,1728]{2,1,0:T(2,128)(2,1)S(1)} async-done(((bf16[32,2,1728]{2,1,0:T(2,128)(2,1)}), bf16[32,2,1728]{2,1,0:T(2,128)(2,1)S(1)}, u32[]{:S(2)}, u32[]{:S(2)}) %all-to-all-start.7) | async-done | bytes 221216 | tf_op jit(solution)/shard_map/all_to_all | solution.py:1533
  (229 shorter events, 118.2 us)
Async XLA Ops:
  9.3 15.4 %collective-permute-start.1 = (bf16[2,2,64,768]{3,2,1,0:T(8,128)(2,1)}, bf16[2,2,64,768]{3,2,1,0:T(8,128)(2,1)}, u32[]{:S(2)}, u32[]{:S(2)}) collective-permute-start(bf16[2,2,64,768]{3,2,1,0:T(8,128)(2,1)} %pad_maximum_fusion.1), channel_id=1, source_target_pairs={{1,0},{2,1},{3,2},{4,3},{5,4},{6,5},{7,6},{9,8},{10,9},{11,10},{12... | collective-permute-start | bytes 1179656 | tf_op jit(solution)/shard_map/ppermute | solution.py:1036
  11.5 14.2 %collective-permute-start = (bf16[2,2,64,768]{3,2,1,0:T(8,128)(2,1)}, bf16[2,2,64,768]{3,2,1,0:T(8,128)(2,1)}, u32[]{:S(2)}, u32[]{:S(2)}) collective-permute-start(bf16[2,2,64,768]{3,2,1,0:T(8,128)(2,1)} %pad_maximum_fusion), channel_id=1, source_target_pairs={{0,1},{1,2},{2,3},{3,4},{4,5},{5,6},{6,7},{8,9},{9,10},{10,11},{11... | collective-permute-start | bytes 1179656 | tf_op jit(solution)/shard_map/ppermute | solution.py:1031
  24.5 22.2 %copy-start.12 = (f32[2,1,768]{2,1,0:T(1,128)}, f32[2,1,768]{2,1,0:T(1,128)S(1)}, u32[]{:S(2)}) copy-start(f32[2,1,768]{2,1,0:T(1,128)S(1)} %get-tuple-element.214.gate_ref.refs_12_) | copy-start | bytes 18436
  36.6 44.4 %all-to-all-start = ((bf16[8,128,768]{2,1,0:T(8,128)(2,1)}), bf16[8,128,768]{2,1,0:T(8,128)(2,1)}, u32[]{:S(2)}, u32[]{:S(2)}) async-start(bf16[8,128,768]{2,1,0:T(8,128)(2,1)} %bitcast.6), calls=%async_computation | async-start | bytes 3145728 | tf_op jit(solution)/shard_map/all_to_all | solution.py:1350
  96.3 35.3 %all-to-all-start.1 = ((bf16[8,128,384]{2,1,0:T(8,128)(2,1)}), bf16[8,128,384]{2,1,0:T(8,128)(2,1)S(1)}, u32[]{:S(2)}, u32[]{:S(2)}) async-start(bf16[8,128,384]{2,1,0:T(8,128)(2,1)} %bitcast.123), calls=%async_computation.1 | async-start | bytes 1572864 | tf_op jit(solution)/shard_map/all_to_all | solution.py:1355
  131.7 24.5 %copy-start.20 = (bf16[8,128,384]{2,1,0:T(8,128)(2,1)}, bf16[8,128,384]{2,1,0:T(8,128)(2,1)S(1)}, u32[]{:S(2)}) copy-start(bf16[8,128,384]{2,1,0:T(8,128)(2,1)S(1)} %all-to-all-done.1) | copy-start | bytes 2359300
  131.7 24.5 %all-to-all-start.2 = ((bf16[8,128,384]{2,1,0:T(8,128)(2,1)}), bf16[8,128,384]{2,1,0:T(8,128)(2,1)S(1)}, u32[]{:S(2)}, u32[]{:S(2)}) async-start(bf16[8,128,384]{2,1,0:T(8,128)(2,1)} %bitcast.122), calls=%async_computation.2 | async-start | bytes 1572864 | tf_op jit(solution)/shard_map/all_to_all | solution.py:1355
  163.5 4.5 collective-permute-start.2
  165.8 3.9 collective-permute-start.3
  238.9 29.2 %all-to-all-start.3 = ((bf16[8,128,384]{2,1,0:T(8,128)(2,1)}), bf16[8,128,384]{2,1,0:T(8,128)(2,1)}, u32[]{:S(2)}, u32[]{:S(2)}) async-start(bf16[8,128,384]{2,1,0:T(8,128)(2,1)} %bitcast.129), calls=%async_computation.3 | async-start | bytes 1572864 | tf_op jit(solution)/shard_map/all_to_all | solution.py:1350
  246.8 208.5 %reduce-scatter.2.cloned.1.call-start = ((), (), s32[]{:S(2)}) async-start(), calls=%async_computation.9 | async-start | bytes 9732096 | tf_op jit(solution)/shard_map/reduce_scatter | solution.py:1430
  268.0 25.8 %all-to-all-start.4 = ((bf16[8,128,384]{2,1,0:T(8,128)(2,1)}), bf16[8,128,384]{2,1,0:T(8,128)(2,1)}, u32[]{:S(2)}, u32[]{:S(2)}) async-start(bf16[8,128,384]{2,1,0:T(8,128)(2,1)} %bitcast.128), calls=%async_computation.4 | async-start | bytes 1572864 | tf_op jit(solution)/shard_map/all_to_all | solution.py:1350
  296.5 30.8 %all-to-all-start.6 = ((bf16[32,2,3648]{2,1,0:T(2,128)(2,1)}), bf16[32,2,3648]{2,1,0:T(2,128)(2,1)S(1)}, u32[]{:S(2)}, u32[]{:S(2)}) async-start(bf16[32,2,3648]{2,1,0:T(2,128)(2,1)} %reshape.400), calls=%async_computation.6 | async-start | bytes 950272 | tf_op jit(solution)/shard_map/all_to_all | solution.py:1466
  327.3 55.3 %all-to-all-start.5 = ((bf16[8,128,768]{2,1,0:T(8,128)(2,1)}), bf16[8,128,768]{2,1,0:T(8,128)(2,1)}, u32[]{:S(2)}, u32[]{:S(2)}) async-start(bf16[8,128,768]{2,1,0:T(8,128)(2,1)} %bitcast.119), calls=%async_computation.5 | async-start | bytes 3145728 | tf_op jit(solution)/shard_map/all_to_all | solution.py:1355
  382.6 5.6 %collective-permute-start.6 = (bf16[4,4,24,3072]{3,2,1,0:T(8,128)(2,1)}, bf16[4,4,24,3072]{3,2,1,0:T(8,128)(2,1)}, u32[]{:S(2)}, u32[]{:S(2)}) collective-permute-start(bf16[4,4,24,3072]{3,2,1,0:T(8,128)(2,1)} %get-tuple-element.145), channel_id=1, source_target_pairs={{0,1},{1,0},{2,3},{3,2},{4,5},{5,4},{6,7},{7,6},{8,9},{9,8},{10,11... | collective-permute-start | bytes 7077896 | tf_op jit(solution)/shard_map/ppermute | solution.py:1244
  384.5 14.9 %collective-permute-start.4 = (bf16[2,2,32,768]{3,2,1,0:T(8,128)(2,1)S(1)}, bf16[2,2,32,768]{3,2,1,0:T(8,128)(2,1)S(1)}, u32[]{:S(2)}, u32[]{:S(2)}) collective-permute-start(bf16[2,2,32,768]{3,2,1,0:T(8,128)(2,1)S(1)} %get-tuple-element.166), channel_id=1, source_target_pairs={{0,1},{1,2},{2,3},{3,4},{4,5},{5,6},{6,7},{8,9},{9,10},{10,11},{11... | collective-permute-start | bytes 589832 | tf_op jit(solution)/shard_map/ppermute | solution.py:1031
  386.9 12.4 %collective-permute-start.5 = (bf16[2,2,32,768]{3,2,1,0:T(8,128)(2,1)S(1)}, bf16[2,2,32,768]{3,2,1,0:T(8,128)(2,1)S(1)}, u32[]{:S(2)}, u32[]{:S(2)}) collective-permute-start(bf16[2,2,32,768]{3,2,1,0:T(8,128)(2,1)S(1)} %get-tuple-element.165), channel_id=1, source_target_pairs={{1,0},{2,1},{3,2},{4,3},{5,4},{6,5},{7,6},{9,8},{10,9},{11,10},{12... | collective-permute-start | bytes 589832 | tf_op jit(solution)/shard_map/ppermute | solution.py:1036
  394.2 42.8 %collective-permute-start.7 = (bf16[4,24,3072]{2,1,0:T(8,128)(2,1)}, bf16[4,24,3072]{2,1,0:T(8,128)(2,1)}, u32[]{:S(2)}, u32[]{:S(2)}) collective-permute-start(bf16[4,24,3072]{2,1,0:T(8,128)(2,1)} %get-tuple-element.162), channel_id=1, source_target_pairs={{0,8},{8,0},{16,24},{24,16},{1,9},{9,1},{17,25},{25,17},{2,10},{10... | collective-permute-start | bytes 1769480 | tf_op jit(solution)/shard_map/ppermute | solution.py:1252
  395.7 41.4 %collective-permute-start.8 = (bf16[4,24,3072]{2,1,0:T(8,128)(2,1)}, bf16[4,24,3072]{2,1,0:T(8,128)(2,1)}, u32[]{:S(2)}, u32[]{:S(2)}) collective-permute-start(bf16[4,24,3072]{2,1,0:T(8,128)(2,1)} %get-tuple-element.164), channel_id=1, source_target_pairs={{0,16},{8,24},{16,0},{24,8},{1,17},{9,25},{17,1},{25,9},{2,18},{10... | collective-permute-start | bytes 1769480 | tf_op jit(solution)/shard_map/ppermute | solution.py:1252
  397.1 39.9 %collective-permute-start.9 = (bf16[4,24,3072]{2,1,0:T(8,128)(2,1)S(1)}, bf16[4,24,3072]{2,1,0:T(8,128)(2,1)}, u32[]{:S(2)}, u32[]{:S(2)}) collective-permute-start(bf16[4,24,3072]{2,1,0:T(8,128)(2,1)S(1)} %get-tuple-element.163), channel_id=1, source_target_pairs={{0,24},{8,16},{16,8},{24,0},{1,25},{9,17},{17,9},{25,1},{2,26},{10... | collective-permute-start | bytes 1769480 | tf_op jit(solution)/shard_map/ppermute | solution.py:1252
  419.5 17.2 %all-to-all-start.7 = ((bf16[32,2,1728]{2,1,0:T(2,128)(2,1)}), bf16[32,2,1728]{2,1,0:T(2,128)(2,1)S(1)}, u32[]{:S(2)}, u32[]{:S(2)}) async-start(bf16[32,2,1728]{2,1,0:T(2,128)(2,1)} %reshape.402), calls=%async_computation.7 | async-start | bytes 458752 | tf_op jit(solution)/shard_map/all_to_all | solution.py:1533
  439.7 13.9 %collective-permute-start.10 = (bf16[24,3072]{1,0:T(8,128)(2,1)}, bf16[24,3072]{1,0:T(8,128)(2,1)S(1)}, u32[]{:S(2)}, u32[]{:S(2)}) collective-permute-start(bf16[24,3072]{1,0:T(8,128)(2,1)} %get-tuple-element.173), channel_id=1, source_target_pairs={{0,2},{1,3},{2,0},{3,1},{4,6},{5,7},{6,4},{7,5},{8,10},{9,11},{10,... | collective-permute-start | bytes 442376 | tf_op jit(solution)/shard_map/ppermute | solution.py:1252
  439.8 14.0 %collective-permute-start.11 = (bf16[24,3072]{1,0:T(8,128)(2,1)S(1)}, bf16[24,3072]{1,0:T(8,128)(2,1)S(1)}, u32[]{:S(2)}, u32[]{:S(2)}) collective-permute-start(bf16[24,3072]{1,0:T(8,128)(2,1)S(1)} %get-tuple-element.175), channel_id=1, source_target_pairs={{0,4},{1,5},{2,6},{3,7},{4,0},{5,1},{6,2},{7,3},{8,12},{9,13},{10,... | collective-permute-start | bytes 442376 | tf_op jit(solution)/shard_map/ppermute | solution.py:1252
  439.8 14.0 %collective-permute-start.12 = (bf16[24,3072]{1,0:T(8,128)(2,1)S(1)}, bf16[24,3072]{1,0:T(8,128)(2,1)S(1)}, u32[]{:S(2)}, u32[]{:S(2)}) collective-permute-start(bf16[24,3072]{1,0:T(8,128)(2,1)S(1)} %get-tuple-element.174), channel_id=1, source_target_pairs={{0,6},{1,7},{2,4},{3,5},{4,2},{5,3},{6,0},{7,1},{8,14},{9,15},{10,... | collective-permute-start | bytes 442376 | tf_op jit(solution)/shard_map/ppermute | solution.py:1252
  (38 other events, 206.3 us)
Sparse Core Ops, SparseCore 0:
  267.1 168.9 reduce-scatter.1

commit v5 on v4

--- a/solution.py
+++ b/solution.py
@@ -12,7 +12,7 @@
 HEAD_DIM = 64
 LANES = 128
 COLUMN_PARTS = 4
-CHUNKS = 2
+CHUNKS = (2, 3, 1)
 
 highest = lax.Precision.HIGHEST
 epsilon = 1e-06
@@ -237,15 +237,20 @@
 ):
     tokens = x_ref.shape[0]
     base = math.log2(math.e) / math.sqrt(HEAD_DIM)
-    x = x_ref[...]
-    q_ref[...] = (dot(x, wq_ref[...]) + bq_ref[...]).astype(bfloat)
-    k_ref[...] = dot(x, wk_ref[...]).astype(bfloat)
-    v_ref[...] = (dot(x, wv_ref[...]) + bv_ref[...]).astype(bfloat)
-    keys = k_ref[...]
-    values = v_ref[...].T
+
+    @pl.when(pl.program_id(0) == 0)
+    def _():
+        x = x_ref[...]
+        q_ref[...] = (dot(x, wq_ref[...]) + bq_ref[...]).astype(bfloat)
+        k_ref[...] = dot(x, wk_ref[...]).astype(bfloat)
+        v_ref[...] = (dot(x, wv_ref[...]) + bv_ref[...]).astype(bfloat)
+
+    pair = pl.ds(pl.multiple_of(pl.program_id(0) * LANES, LANES), LANES)
+    keys = k_ref[:, pair]
+    values = v_ref[:, pair].T
     lane = lax.broadcasted_iota(jnp.int32, (QUERY_STEP, LANES), 1)
     for at in range(0, tokens, QUERY_STEP):
-        part = q_ref[at : at + QUERY_STEP]
+        part = q_ref[at : at + QUERY_STEP, pair]
         outs = []
         for head in range(LANES // HEAD_DIM):
             own = jnp.where(lane // HEAD_DIM == head, part, jnp.zeros_like(part))
@@ -262,10 +267,11 @@
 def attend(x, weights, biases, first, width):
     tokens, features = x.shape
     pairs = width // LANES
-    start = first // LANES
-    stride = weights.shape[1] // 3 // LANES
-    weight = lambda i: pl.BlockSpec((features, LANES), lambda h: (0, i * stride + start + h))
-    bias = lambda i: pl.BlockSpec((1, LANES), lambda h: (0, i * stride + start + h))
+    start = first // width
+    stride = weights.shape[1] // 3 // width
+    weight = lambda i: pl.BlockSpec((features, width), lambda h: (0, i * stride + start))
+    bias = lambda i: pl.BlockSpec((1, width), lambda h: (0, i * stride + start))
+    full = pl.BlockSpec((tokens, width), lambda h: (0, 0))
     column = pl.BlockSpec((tokens, LANES), lambda h: (0, h))
     lows = jax.ShapeDtypeStruct((tokens, width), bfloat)
     return pl.pallas_call(
@@ -273,7 +279,7 @@
         grid=(pairs,),
         in_specs=[pl.BlockSpec((tokens, features), lambda h: (0, 0))]
         + [weight(0), weight(1), weight(2), bias(0), bias(1)],
-        out_specs=[column] * 4 + [pl.BlockSpec((1, 2, tokens), lambda h: (h, 0, 0))],
+        out_specs=[full] * 3 + [column] + [pl.BlockSpec((1, 2, tokens), lambda h: (h, 0, 0))],
         out_shape=[lows] * 4 + [jax.ShapeDtypeStruct((pairs, 2, tokens), single)],
         compiler_params=params(60),
         cost_estimate=cost(
@@ -285,9 +291,25 @@
     )(x, weights, weights, weights, biases, biases)
 
 
-def attend_back_kernel(
-    q_ref, k_ref, v_ref, mixed_ref, grad_ref, log_ref, dq_ref, dk_ref, dv_ref, dk_sum, dv_sum
-):
+def attend_back_kernel(others, *refs):
+    q_ref, k_ref, v_ref, mixed_ref, grad_ref, log_ref = refs[:6]
+    if others is None:
+        dq_ref, dk_ref, dv_ref, dk_sum, dv_sum = refs[6:]
+    else:
+        sources = refs[6 : 7 + others]
+        dq_ref, dk_ref, dv_ref, out_ref, dk_sum, dv_sum, own_grads = refs[7 + others : 14 + others]
+        held = refs[14 + others : 15 + 2 * others]
+        sems = refs[15 + 2 * others]
+        copies = [
+            pltpu.make_async_copy(source, kept, sems.at[n])
+            for n, (source, kept) in enumerate(zip(sources, held))
+        ]
+
+        @pl.when(pl.program_id(0) == 0)
+        def _():
+            for c in copies:
+                c.start()
+
     tokens = q_ref.shape[0]
     scale = 1.0 / math.sqrt(HEAD_DIM)
     base = math.log2(math.e) * scale
@@ -322,57 +344,60 @@
         dq_ref[rows] = (jnp.concatenate(outs, axis=0) * scale).T.astype(bfloat)
     dk_ref[...] = (dk_sum[...] * scale).astype(bfloat)
     dv_ref[...] = dv_sum[...].astype(bfloat)
-
-
-def attend_back(q, k, v, mixed, grad, logs):
+    if others is None:
+        return
+    pair = pl.ds(pl.multiple_of(pl.program_id(0) * LANES, LANES), LANES)
+    for i, ref in enumerate((dq_ref, dk_ref, dv_ref)):
+        own_grads[i, :, pair] = ref[...]
+
+    @pl.when(pl.program_id(0) == pl.num_programs(0) - 1)
+    def _():
+        for c in copies:
+            c.wait()
+        weight = held[0]
+        third = weight.shape[1] // 3
+        piece = own_grads.shape[2]
+        total = None
+        for i in range(3):
+            parts = [held[1 + 3 * c + i][...] for c in range(others // 3)] + [own_grads[i]]
+            for c, part in enumerate(parts):
+                at = i * third + c * piece
+                term = dot_nt(part, weight[:, at : at + piece])
+                total = term if total is None else total + term
+        out_ref[...] = total.astype(bfloat)
+
+
+def attend_back(q, k, v, mixed, grad, logs, weight=None, earlier=()):
     tokens, width = q.shape
     pairs = width // LANES
     column = pl.BlockSpec((tokens, LANES), lambda h: (0, h))
     lows = jax.ShapeDtypeStruct((tokens, width), bfloat)
+    sums = [pltpu.VMEM((tokens, LANES), single)] * 2
+    sources, outs, shapes, scratch = (), [], [], []
+    if weight is not None:
+        sources = (weight,) + tuple(earlier)
+        outs = [pl.BlockSpec((tokens, weight.shape[0]), lambda h: (0, 0))]
+        shapes = [jax.ShapeDtypeStruct((tokens, weight.shape[0]), bfloat)]
+        scratch = (
+            [pltpu.VMEM((3, tokens, width), bfloat)]
+            + [pltpu.VMEM(a.shape, bfloat) for a in sources]
+            + [pltpu.SemaphoreType.DMA((len(sources),))]
+        )
     return pl.pallas_call(
-        attend_back_kernel,
+        partial(attend_back_kernel, None if weight is None else len(earlier)),
         grid=(pairs,),
-        in_specs=[column] * 5 + [pl.BlockSpec((1, 2, tokens), lambda h: (h, 0, 0))],
-        out_specs=[column] * 3,
-        out_shape=[lows] * 3,
-        scratch_shapes=[pltpu.VMEM((tokens, LANES), single)] * 2,
+        in_specs=[column] * 5
+        + [pl.BlockSpec((1, 2, tokens), lambda h: (h, 0, 0))]
+        + [pl.BlockSpec(memory_space=pl.ANY)] * len(sources),
+        out_specs=[column] * 3 + outs,
+        out_shape=[lows] * 3 + shapes,
+        scratch_shapes=sums + scratch,
         compiler_params=params(60),
         cost_estimate=cost(
             40 * tokens * tokens * width, 16 * tokens * width, 2 * pairs * tokens * tokens
         ),
         name="attend_back",
-    )(q, k, v, mixed, grad, logs)
-
-
-def regroup_kernel(*refs):
-    parts, weight_ref, out_ref = refs[:-2], refs[-2], refs[-1]
-    count = len(parts) // 3
-    piece = parts[0].shape[1]
-    third = weight_ref.shape[1] // 3
-    total = None
-    for c in range(count):
-        for i in range(3):
-            at = i * third + c * piece
-            term = dot_nt(parts[3 * c + i][...], weight_ref[:, at : at + piece])
-            total = term if total is None else total + term
-    out_ref[...] = total.astype(bfloat)
-
-
-def regroup(parts, weight):
-    tokens, piece = parts[0].shape
-    features = weight.shape[0]
-    step = min(256, tokens)
-    return pl.pallas_call(
-        regroup_kernel,
-        grid=(tokens // step,),
-        in_specs=[pl.BlockSpec((step, piece), lambda t: (t, 0))] * len(parts)
-        + [pl.BlockSpec(weight.shape, lambda t: (0, 0))],
-        out_specs=pl.BlockSpec((step, features), lambda t: (t, 0)),
-        out_shape=jax.ShapeDtypeStruct((tokens, features), bfloat),
-        compiler_params=params(60),
-        cost_estimate=cost(2 * tokens * features * weight.shape[1], 2 * tokens * features * 4),
-        name="regroup",
-    )(*parts, weight)
+    )(q, k, v, mixed, grad, logs, *sources)
 
 
 def input_grad_kernel(*refs):
@@ -1369,7 +1394,8 @@
     own_bias = jnp.concatenate(
         [own_columns(row_vector(b), 1) for b in (query_bias, value_bias)], axis=1
     )
-    piece = width // CHUNKS
+    chunks = next(c for c in CHUNKS if width // LANES % c == 0)
+    piece = width // chunks
     saved = []
     mixed = []
     d_act = feed_upstream(d_branch, shrink_weight)
@@ -1386,7 +1412,7 @@
             )
         )
     )
-    for c in range(CHUNKS):
+    for c in range(chunks):
         saved.append(attend(group, own_weight, own_bias, c * piece, piece))
         mixed.append(collect(saved[c][3]))
     if share == 1:
@@ -1435,13 +1461,20 @@
         parts = d_mixed[0].reshape(groups, quarter, share, width).transpose(0, 2, 1, 3)
         got = lax.all_to_all(parts.reshape(strips, quarter, width), "strips", 0, 0, tiled=True)
         got = got.reshape(strips * quarter, width)
-        d_mixed = [got[:, c * piece : (c + 1) * piece] for c in range(CHUNKS)]
+        d_mixed = [got[:, c * piece : (c + 1) * piece] for c in range(chunks)]
     grads = []
-    for c in range(CHUNKS):
+    for c in range(chunks):
         if c == 0:
             d_mixed[c], _ = lax.optimization_barrier((d_mixed[c], early))
         q, k, v, out, logs = saved[c]
-        grads.append(attend_back(q, k, v, out, d_mixed[c], logs))
+        if c < chunks - 1:
+            grads.append(attend_back(q, k, v, out, d_mixed[c], logs))
+        else:
+            earlier = [g for chunk in grads for g in chunk]
+            *last_grads, d_group = attend_back(
+                q, k, v, out, d_mixed[c], logs, own_weight, earlier
+            )
+            grads.append(last_grads)
     size = features // devices
     narrow = jnp.stack([jnp.sum(turn_sums[:, 4], axis=0), jnp.sum(grad_shrink_bias[:, 0], axis=0)])
     to_all = jnp.concatenate(
@@ -1462,11 +1495,10 @@
         ],
         axis=1,
     ).astype(bfloat)
-    early_small = after(early_small, grads[0][0], *d_mixed)
+    early_small = after(early_small, *(grads[0][:1] if chunks > 1 else ()), *d_mixed)
     early_got = lax.all_to_all(early_small, both, 0, 0, tiled=True)
 
     parts = [g for chunk in grads for g in chunk]
-    d_group = regroup(parts, own_weight)
     d_reduced = collect(d_group)
     if share > 1:
         d_reduced = jnp.sum(

time: 468 us -> 465 us (level); the launches traced: 465 us -> 456 us
  starting transfers between devices: 72.1 us -> 61.8 us
    all_to_all x3, starting transfers between devices: 23.4 us -> 12.9 us  [collect(): return lax.all_to_all(flat, 'strips', 0, 0, tiled=True)]
    pallas_call x3 -> x2, Pallas kernels: 45.5 us -> 42.4 us  [attend_back(): pl.pallas_call(partial(attend_back_kernel, None if weight is None else le...]
  transfers between devices with their start and end apart: 22 -> 22, of which waited for: 9 -> 9; matrix products, arithmetic and copies ran while one was open for 11% -> 12% of each run, Pallas kernels for 26% -> 26%
where the time goes in v5:
time: 465 us; the launch traced here: 456 us
  Pallas kernels  216 us (46%)
  waiting for transfers between devices  83.6 us (18%)
  local copies, waits for them, and re-layouts  62.5 us (13%)
  starting transfers between devices  61.8 us (13%)
  other arithmetic  17.1 us (4%)
  between operations  15.1 us (3%)
    pallas_call x1, Pallas kernels, feed_turn(): pl.pallas_call(partial(feed_turn_kernel, len(mixed), feeds, turns), grid=...  69.1 us
    all_to_all x3, waiting for transfers between devices, collect(): return lax.all_to_all(flat, 'strips', 0, 0, tiled=True)  48.1 us
    pallas_call x2, Pallas kernels, attend_back(): pl.pallas_call(partial(attend_back_kernel, None if weight is None else le...  42.4 us
    unnamed x92, local copies, waits for them, and re-layouts  31.2 us
    pallas_call x2, Pallas kernels, attend(): pl.pallas_call(attend_kernel, grid=(pairs,), in_specs=[pl.BlockSpec((toke...  31 us
    all_to_all x3, waiting for transfers between devices, spread(): got = lax.all_to_all(flat, 'strips', 0, 0, tiled=True)  22.4 us
    all_to_all x3, starting transfers between devices, spread(): got = lax.all_to_all(flat, 'strips', 0, 0, tiled=True)  18.9 us
    pallas_call x1, Pallas kernels, feed_grads(): pl.pallas_call(feed_grads_kernel, grid=(steps,), in_specs=[pl.BlockSpec((...  16.1 us
  transfers between devices with their start and end apart: 22, of which 9 were waited for; matrix products, arithmetic and copies ran while one was open for 12% of the time, Pallas kernels for 26%

profile of v5, /device:TPU:0, one launch (start us, length us, event | category | flops | bytes accessed | tf_op | source)
XLA Modules:
  0.0 455.7 jit_solution(3405893078145037005)
XLA Ops:
  28.2 5.8 %front.1 = (bf16[2,4,128,768]{3,2,1,0:T(8,128)(2,1)}, bf16[2,10,64,768]{3,2,1,0:T(8,128)(2,1)S(1)}, bf16[2,8,64,768]{3,2,1,0:T(8,128)(2,1)S(1)}) custom-call(f32[2]{0:T(128)S(1)} %add_convert_fusion.1.edge_ref.refs_0_, bf16[2,8,64,768]{3,2,1,0:T(8,128)(2,1)S(1)} %copy-done.5, bf16[2,1,64,768]{3,2,1,0:T(8,128)(2,1)S(1)} %get-tuple-element.181.top_ref, ...), custom_call_target="tpu_custom_call" | custom-call | flops 117964800 | bytes 6291456 | tf_op jit(solution)/shard_map/front/pallas_call | solution.py:162
  36.6 6.4 %all-to-all-start = ((bf16[8,128,768]{2,1,0:T(8,128)(2,1)}), bf16[8,128,768]{2,1,0:T(8,128)(2,1)}, u32[]{:S(2)}, u32[]{:S(2)}) async-start(bf16[8,128,768]{2,1,0:T(8,128)(2,1)} %bitcast.6), calls=%async_computation | async-start | bytes 3145728 | tf_op jit(solution)/shard_map/all_to_all | solution.py:1375
  51.5 10.7 %feed_upstream.1.refs_4_ = bf16[1280,3072]{1,0:T(8,128)(2,1)} custom-call(bf16[1280,768]{1,0:T(8,128)(2,1)} %bitcast.113, bf16[3072,768]{1,0:T(8,128)(2,1)} %refs_16_.1), custom_call_target="tpu_custom_call" | custom-call | flops 6039797760 | bytes 9830400 | tf_op jit(solution)/shard_map/feed_upstream/pallas_call | solution.py:531
  62.2 18.7 %all-to-all-done = bf16[8,128,768]{2,1,0:T(8,128)(2,1)} async-done(((bf16[8,128,768]{2,1,0:T(8,128)(2,1)}), bf16[8,128,768]{2,1,0:T(8,128)(2,1)}, u32[]{:S(2)}, u32[]{:S(2)}) %all-to-all-start) | async-done | bytes 1572896 | tf_op jit(solution)/shard_map/all_to_all | solution.py:1375
  80.9 15.5 %attend.2 = (bf16[1024,384]{1,0:T(8,128)(2,1)}, bf16[1024,384]{1,0:T(8,128)(2,1)}, bf16[1024,384]{1,0:T(8,128)(2,1)}, bf16[1024,384]{1,0:T(8,128)(2,1)}, f32[3,2,1024]{2,1,0:T(2,128)}) custom-call(bf16[1024,768]{1,0:T(8,128)(2,1)} %bitcast.7.x_ref.refs_0_, bf16[768,2304]{1,0:T(8,128)(2,1)} %refs_6_.1, bf16[768,2304]{1,0:T(8,128)(2,1)} %refs_6_.1, ...), custom_call_target="tpu_custom_call" | custom-call | flops 8254390272 | bytes 6488064 | tf_op jit(solution)/shard_map/attend/pallas_call | solution.py:277
  96.4 4.1 all-to-all-start.1
  100.5 15.5 %attend.3 = (bf16[1024,384]{1,0:T(8,128)(2,1)}, bf16[1024,384]{1,0:T(8,128)(2,1)}, bf16[1024,384]{1,0:T(8,128)(2,1)}, bf16[1024,384]{1,0:T(8,128)(2,1)}, f32[3,2,1024]{2,1,0:T(2,128)}) custom-call(bf16[1024,768]{1,0:T(8,128)(2,1)} %bitcast.7.x_ref.refs_0_, bf16[768,2304]{1,0:T(8,128)(2,1)} %refs_6_.1, bf16[768,2304]{1,0:T(8,128)(2,1)} %refs_6_.1, ...), custom_call_target="tpu_custom_call" | custom-call | flops 8254390272 | bytes 6488064 | tf_op jit(solution)/shard_map/attend/pallas_call | solution.py:277
  116.0 5.4 %all-to-all-done.1 = bf16[8,128,384]{2,1,0:T(8,128)(2,1)S(1)} async-done(((bf16[8,128,384]{2,1,0:T(8,128)(2,1)}), bf16[8,128,384]{2,1,0:T(8,128)(2,1)S(1)}, u32[]{:S(2)}, u32[]{:S(2)}) %all-to-all-start.1) | async-done | bytes 786464 | tf_op jit(solution)/shard_map/all_to_all | solution.py:1380
  127.6 18.3 %all-to-all-done.2 = bf16[8,128,384]{2,1,0:T(8,128)(2,1)S(1)} async-done(((bf16[8,128,384]{2,1,0:T(8,128)(2,1)}), bf16[8,128,384]{2,1,0:T(8,128)(2,1)S(1)}, u32[]{:S(2)}, u32[]{:S(2)}) %all-to-all-start.2) | async-done | bytes 786464 | tf_op jit(solution)/shard_map/all_to_all | solution.py:1380
  146.7 6.5 %middle.1 = (f32[2,8,64,768]{3,2,1,0:T(8,128)}, f32[2,8,64,768]{3,2,1,0:T(8,128)}, bf16[2,8,64,768]{3,2,1,0:T(8,128)(2,1)}, bf16[2,2,64,768]{3,2,1,0:T(8,128)(2,1)}, bf16[2,2,64,768]{3,2,1,0:T(8,128)(2,1)}) custom-call(bf16[2,4,128,384]{3,2,1,0:T(8,128)(2,1)} %bitcast.124, bf16[2,4,128,384]{3,2,1,0:T(8,128)(2,1)} %bitcast.126, bf16[768,768]{1,0:T(8,128)(2,1)} %refs_18_.1, ...), custom_call_target="tpu_custom_call" | custom-call | flops 1207959552 | bytes 11010048 | tf_op jit(solution)/shard_map/middle/pallas_call | solution.py:497
  159.5 69.1 %feed_turn.1 = (f32[16,3072]{1,0:T(8,128)}, bf16[1024,3072]{1,0:T(8,128)(2,1)}, bf16[1024,3072]{1,0:T(8,128)(2,1)}, bf16[2,8,64,768]{3,2,1,0:T(8,128)(2,1)}, f32...) custom-call(f32[2]{0:T(128)} %copy-done.13, ...), custom_call_target="tpu_custom_call" | custom-call | flops 19327352832 | bytes 61341696 | tf_op jit(solution)/shard_map/feed_turn/pallas_call | solution.py:793
  228.6 7.9 %all-to-all-start.4 = ((bf16[8,128,384]{2,1,0:T(8,128)(2,1)}), bf16[8,128,384]{2,1,0:T(8,128)(2,1)}, u32[]{:S(2)}, u32[]{:S(2)}) async-start(bf16[8,128,384]{2,1,0:T(8,128)(2,1)} %bitcast.129), calls=%async_computation.4 | async-start | bytes 1572864 | tf_op jit(solution)/shard_map/all_to_all | solution.py:1375
  240.6 16.1 %feed_grads.1 = bf16[32,8,24,768]{3,2,1,0:T(8,128)(2,1)} custom-call(bf16[1024,3072]{1,0:T(8,128)(2,1)} %get-tuple-element.120.act_ref, bf16[1024,3072]{1,0:T(8,128)(2,1)} %get-tuple-element.121.d_hid_ref, bf16[2,8,64,768]{3,2,1,0:T(8,128)(2,1)} %get-tuple-element.99.refs_1_.nb_ref, bf16[2,10,64,768]{3,2,1,0:T(8,128)(2,1)} %copy-done.14), custom_call_target="tpu_custom_call" | custom-call | flops 9663676416 | bytes 31457280 | tf_op jit(solution)/shard_map/feed_grads/pallas_call | solution.py:911
  257.7 4.5 all-to-all-start.3
  262.3 18.1 %attend_back.2 = (bf16[1024,384]{1,0:T(8,128)(2,1)}, bf16[1024,384]{1,0:T(8,128)(2,1)}, bf16[1024,384]{1,0:T(8,128)(2,1)}) custom-call(bf16[1024,384]{1,0:T(8,128)(2,1)} %get-tuple-element.116.refs_0_, bf16[1024,384]{1,0:T(8,128)(2,1)} %get-tuple-element.117.refs_1_, bf16[1024,384]{1,0:T(8,128)(2,1)} %get-tuple-element.118.refs_2_, ...), custom_call_target="tpu_custom_call" | custom-call | flops 16106127360 | bytes 6291456 | tf_op jit(solution)/shard_map/attend_back/pallas_call | solution.py:386
  289.9 24.3 %attend_back.3 = (bf16[1024,384]{1,0:T(8,128)(2,1)}, bf16[1024,384]{1,0:T(8,128)(2,1)}, bf16[1024,384]{1,0:T(8,128)(2,1)}, bf16[1024,768]{1,0:T(8,128)(2,1)}) custom-call(bf16[1024,384]{1,0:T(8,128)(2,1)} %get-tuple-element.111.refs_0_, bf16[1024,384]{1,0:T(8,128)(2,1)} %get-tuple-element.112.refs_1_, bf16[1024,384]{1,0:T(8,128)(2,1)} %get-tuple-element.113.refs_2_, ...), custom_call_target="tpu_custom_call" | custom-call | flops 16106127360 | bytes 6291456 | tf_op jit(solution)/shard_map/attend_back/pallas_call | solution.py:386
  314.3 5.3 %all-to-all-start.5 = ((bf16[8,128,768]{2,1,0:T(8,128)(2,1)}), bf16[8,128,768]{2,1,0:T(8,128)(2,1)}, u32[]{:S(2)}, u32[]{:S(2)}) async-start(bf16[8,128,768]{2,1,0:T(8,128)(2,1)} %bitcast.119), calls=%async_computation.5 | async-start | bytes 3145728 | tf_op jit(solution)/shard_map/all_to_all | solution.py:1380
  319.6 10.0 %input_grad.1 = (bf16[768,3072]{1,0:T(8,128)(2,1)}, f32[8,1536]{1,0:T(8,128)}) custom-call(bf16[1024,768]{1,0:T(8,128)(2,1)} %bitcast.7.x_ref.refs_0_, bf16[768,768]{1,0:T(8,128)(2,1)} %get-tuple-element.134.refs_1_, bf16[1024,384]{1,0:T(8,128)(2,1)} %get-tuple-element.124.refs_7_.refs_2_, bf16[1024,384]{1,0:T(8,128)(2,1)} %get-tuple-element.125.refs_8_.refs_3_, ...), custom_call_target="tpu_custom_call" | custom-call | flops 3623878656 | bytes 7864320 | tf_op jit(solution)/shard_map/input_grad/pallas_call | solution.py:431
  329.5 5.0 %dynamic-slice_bitcast_fusion = (bf16[4,4,24,3072]{3,2,1,0:T(8,128)(2,1)}, bf16[4,4,24,3072]{3,2,1,0:T(8,128)(2,1)}) fusion(bf16[4,4,2,24,3072]{4,3,2,1,0:T(8,128)(2,1)} %bitcast.114, s32[]{:T(128)S(6)} %select_n.75, s32[]{:T(128)S(6)} %select_n.74), kind=kLoop, calls=%fused_computation.1 | loop fusion | bytes 9437192 | tf_op jit(solution)/shard_map/jit(dynamic_index_in_dim)/squeeze | solution.py:1523
  347.9 24.4 %all-to-all-done.5 = bf16[8,128,768]{2,1,0:T(8,128)(2,1)} async-done(((bf16[8,128,768]{2,1,0:T(8,128)(2,1)}), bf16[8,128,768]{2,1,0:T(8,128)(2,1)}, u32[]{:S(2)}, u32[]{:S(2)}) %all-to-all-start.5) | async-done | bytes 1572896 | tf_op jit(solution)/shard_map/all_to_all | solution.py:1380
  390.0 13.2 %final.1 = (bf16[2,8,64,768]{3,2,1,0:T(8,128)(2,1)}, f32[16,768]{1,0:T(8,128)}, f32[2,8,768]{2,1,0:T(8,128)}) custom-call(bf16[2,4,128,768]{3,2,1,0:T(8,128)(2,1)} %bitcast.25.d_ref, bf16[2,2,32,768]{3,2,1,0:T(8,128)(2,1)} %copy-done.22, bf16[2,2,32,768]{3,2,1,0:T(8,128)(2,1)} %copy-done.23, bf16[2,10,64,768]{3,2,1,0:T(8,128)(2,1)} %copy-done.7, ...), custom_call_target="tpu_custom_call" | custom-call | flops 141557760 | bytes 9437184 | tf_op jit(solution)/shard_map/final/pallas_call | solution.py:1029
  409.4 5.6 %all-to-all-start.7 = ((bf16[32,2,1728]{2,1,0:T(2,128)(2,1)}), bf16[32,2,1728]{2,1,0:T(2,128)(2,1)S(1)}, u32[]{:S(2)}, u32[]{:S(2)}) async-start(bf16[32,2,1728]{2,1,0:T(2,128)(2,1)} %reshape.402), calls=%async_computation.7 | async-start | bytes 458752 | tf_op jit(solution)/shard_map/all_to_all | solution.py:1565
  416.2 11.4 %all-to-all-done.7 = bf16[32,2,1728]{2,1,0:T(2,128)(2,1)S(1)} async-done(((bf16[32,2,1728]{2,1,0:T(2,128)(2,1)}), bf16[32,2,1728]{2,1,0:T(2,128)(2,1)S(1)}, u32[]{:S(2)}, u32[]{:S(2)}) %all-to-all-start.7) | async-done | bytes 221216 | tf_op jit(solution)/shard_map/all_to_all | solution.py:1565
  430.8 4.1 collective-permute-start.12
  (228 shorter events, 114.6 us)
Async XLA Ops:
  9.3 15.4 %collective-permute-start.1 = (bf16[2,2,64,768]{3,2,1,0:T(8,128)(2,1)}, bf16[2,2,64,768]{3,2,1,0:T(8,128)(2,1)}, u32[]{:S(2)}, u32[]{:S(2)}) collective-permute-start(bf16[2,2,64,768]{3,2,1,0:T(8,128)(2,1)} %pad_maximum_fusion.1), channel_id=1, source_target_pairs={{1,0},{2,1},{3,2},{4,3},{5,4},{6,5},{7,6},{9,8},{10,9},{11,10},{12... | collective-permute-start | bytes 1179656 | tf_op jit(solution)/shard_map/ppermute | solution.py:1061
  11.5 14.2 %collective-permute-start = (bf16[2,2,64,768]{3,2,1,0:T(8,128)(2,1)}, bf16[2,2,64,768]{3,2,1,0:T(8,128)(2,1)}, u32[]{:S(2)}, u32[]{:S(2)}) collective-permute-start(bf16[2,2,64,768]{3,2,1,0:T(8,128)(2,1)} %pad_maximum_fusion), channel_id=1, source_target_pairs={{0,1},{1,2},{2,3},{3,4},{4,5},{5,6},{6,7},{8,9},{9,10},{10,11},{11... | collective-permute-start | bytes 1179656 | tf_op jit(solution)/shard_map/ppermute | solution.py:1056
  24.5 22.2 %copy-start.12 = (f32[2,1,768]{2,1,0:T(1,128)}, f32[2,1,768]{2,1,0:T(1,128)S(1)}, u32[]{:S(2)}) copy-start(f32[2,1,768]{2,1,0:T(1,128)S(1)} %get-tuple-element.216.gate_ref.refs_12_) | copy-start | bytes 18436
  36.6 44.4 %all-to-all-start = ((bf16[8,128,768]{2,1,0:T(8,128)(2,1)}), bf16[8,128,768]{2,1,0:T(8,128)(2,1)}, u32[]{:S(2)}, u32[]{:S(2)}) async-start(bf16[8,128,768]{2,1,0:T(8,128)(2,1)} %bitcast.6), calls=%async_computation | async-start | bytes 3145728 | tf_op jit(solution)/shard_map/all_to_all | solution.py:1375
  96.4 25.0 %all-to-all-start.1 = ((bf16[8,128,384]{2,1,0:T(8,128)(2,1)}), bf16[8,128,384]{2,1,0:T(8,128)(2,1)S(1)}, u32[]{:S(2)}, u32[]{:S(2)}) async-start(bf16[8,128,384]{2,1,0:T(8,128)(2,1)} %bitcast.123), calls=%async_computation.1 | async-start | bytes 1572864 | tf_op jit(solution)/shard_map/all_to_all | solution.py:1380
  121.4 24.5 %copy-start.20 = (bf16[8,128,384]{2,1,0:T(8,128)(2,1)}, bf16[8,128,384]{2,1,0:T(8,128)(2,1)S(1)}, u32[]{:S(2)}) copy-start(bf16[8,128,384]{2,1,0:T(8,128)(2,1)S(1)} %all-to-all-done.1) | copy-start | bytes 2359300
  121.4 24.5 %all-to-all-start.2 = ((bf16[8,128,384]{2,1,0:T(8,128)(2,1)}), bf16[8,128,384]{2,1,0:T(8,128)(2,1)S(1)}, u32[]{:S(2)}, u32[]{:S(2)}) async-start(bf16[8,128,384]{2,1,0:T(8,128)(2,1)} %bitcast.122), calls=%async_computation.2 | async-start | bytes 1572864 | tf_op jit(solution)/shard_map/all_to_all | solution.py:1380
  153.3 4.7 %collective-permute-start.2 = (bf16[2,2,64,768]{3,2,1,0:T(8,128)(2,1)}, bf16[2,2,64,768]{3,2,1,0:T(8,128)(2,1)}, u32[]{:S(2)}, u32[]{:S(2)}) collective-permute-start(bf16[2,2,64,768]{3,2,1,0:T(8,128)(2,1)} %get-tuple-element.100), channel_id=1, source_target_pairs={{0,1},{1,2},{2,3},{3,4},{4,5},{5,6},{6,7},{8,9},{9,10},{10,11},{11... | collective-permute-start | bytes 1179656 | tf_op jit(solution)/shard_map/ppermute | solution.py:1056
  155.5 3.9 collective-permute-start.3
  228.6 29.1 %all-to-all-start.4 = ((bf16[8,128,384]{2,1,0:T(8,128)(2,1)}), bf16[8,128,384]{2,1,0:T(8,128)(2,1)}, u32[]{:S(2)}, u32[]{:S(2)}) async-start(bf16[8,128,384]{2,1,0:T(8,128)(2,1)} %bitcast.129), calls=%async_computation.4 | async-start | bytes 1572864 | tf_op jit(solution)/shard_map/all_to_all | solution.py:1375
  236.5 209.6 %reduce-scatter.2.cloned.1.call-start = ((), (), s32[]{:S(2)}) async-start(), calls=%async_computation.9 | async-start | bytes 9732096 | tf_op jit(solution)/shard_map/reduce_scatter | solution.py:1456
  257.7 25.6 %all-to-all-start.3 = ((bf16[8,128,384]{2,1,0:T(8,128)(2,1)}), bf16[8,128,384]{2,1,0:T(8,128)(2,1)}, u32[]{:S(2)}, u32[]{:S(2)}) async-start(bf16[8,128,384]{2,1,0:T(8,128)(2,1)} %bitcast.128), calls=%async_computation.3 | async-start | bytes 1572864 | tf_op jit(solution)/shard_map/all_to_all | solution.py:1375
  286.0 28.3 %all-to-all-start.6 = ((bf16[32,2,3648]{2,1,0:T(2,128)(2,1)}), bf16[32,2,3648]{2,1,0:T(2,128)(2,1)S(1)}, u32[]{:S(2)}, u32[]{:S(2)}) async-start(bf16[32,2,3648]{2,1,0:T(2,128)(2,1)} %reshape.400), calls=%async_computation.6 | async-start | bytes 950272 | tf_op jit(solution)/shard_map/all_to_all | solution.py:1499
  314.3 58.1 %all-to-all-start.5 = ((bf16[8,128,768]{2,1,0:T(8,128)(2,1)}), bf16[8,128,768]{2,1,0:T(8,128)(2,1)}, u32[]{:S(2)}, u32[]{:S(2)}) async-start(bf16[8,128,768]{2,1,0:T(8,128)(2,1)} %bitcast.119), calls=%async_computation.5 | async-start | bytes 3145728 | tf_op jit(solution)/shard_map/all_to_all | solution.py:1380
  372.3 5.7 %collective-permute-start.6 = (bf16[4,4,24,3072]{3,2,1,0:T(8,128)(2,1)}, bf16[4,4,24,3072]{3,2,1,0:T(8,128)(2,1)}, u32[]{:S(2)}, u32[]{:S(2)}) collective-permute-start(bf16[4,4,24,3072]{3,2,1,0:T(8,128)(2,1)} %get-tuple-element.147), channel_id=1, source_target_pairs={{0,1},{1,0},{2,3},{3,2},{4,5},{5,4},{6,7},{7,6},{8,9},{9,8},{10,11... | collective-permute-start | bytes 7077896 | tf_op jit(solution)/shard_map/ppermute | solution.py:1269
  374.4 14.8 %collective-permute-start.4 = (bf16[2,2,32,768]{3,2,1,0:T(8,128)(2,1)S(1)}, bf16[2,2,32,768]{3,2,1,0:T(8,128)(2,1)S(1)}, u32[]{:S(2)}, u32[]{:S(2)}) collective-permute-start(bf16[2,2,32,768]{3,2,1,0:T(8,128)(2,1)S(1)} %get-tuple-element.168), channel_id=1, source_target_pairs={{0,1},{1,2},{2,3},{3,4},{4,5},{5,6},{6,7},{8,9},{9,10},{10,11},{11... | collective-permute-start | bytes 589832 | tf_op jit(solution)/shard_map/ppermute | solution.py:1056
  376.8 12.4 %collective-permute-start.5 = (bf16[2,2,32,768]{3,2,1,0:T(8,128)(2,1)S(1)}, bf16[2,2,32,768]{3,2,1,0:T(8,128)(2,1)S(1)}, u32[]{:S(2)}, u32[]{:S(2)}) collective-permute-start(bf16[2,2,32,768]{3,2,1,0:T(8,128)(2,1)S(1)} %get-tuple-element.167), channel_id=1, source_target_pairs={{1,0},{2,1},{3,2},{4,3},{5,4},{6,5},{7,6},{9,8},{10,9},{11,10},{12... | collective-permute-start | bytes 589832 | tf_op jit(solution)/shard_map/ppermute | solution.py:1061
  384.0 43.8 %collective-permute-start.7 = (bf16[4,24,3072]{2,1,0:T(8,128)(2,1)}, bf16[4,24,3072]{2,1,0:T(8,128)(2,1)}, u32[]{:S(2)}, u32[]{:S(2)}) collective-permute-start(bf16[4,24,3072]{2,1,0:T(8,128)(2,1)} %get-tuple-element.164), channel_id=1, source_target_pairs={{0,8},{8,0},{16,24},{24,16},{1,9},{9,1},{17,25},{25,17},{2,10},{10... | collective-permute-start | bytes 1769480 | tf_op jit(solution)/shard_map/ppermute | solution.py:1277
  385.6 42.3 %collective-permute-start.8 = (bf16[4,24,3072]{2,1,0:T(8,128)(2,1)}, bf16[4,24,3072]{2,1,0:T(8,128)(2,1)}, u32[]{:S(2)}, u32[]{:S(2)}) collective-permute-start(bf16[4,24,3072]{2,1,0:T(8,128)(2,1)} %get-tuple-element.166), channel_id=1, source_target_pairs={{0,16},{8,24},{16,0},{24,8},{1,17},{9,25},{17,1},{25,9},{2,18},{10... | collective-permute-start | bytes 1769480 | tf_op jit(solution)/shard_map/ppermute | solution.py:1277
  387.1 40.8 %collective-permute-start.9 = (bf16[4,24,3072]{2,1,0:T(8,128)(2,1)S(1)}, bf16[4,24,3072]{2,1,0:T(8,128)(2,1)}, u32[]{:S(2)}, u32[]{:S(2)}) collective-permute-start(bf16[4,24,3072]{2,1,0:T(8,128)(2,1)S(1)} %get-tuple-element.165), channel_id=1, source_target_pairs={{0,24},{8,16},{16,8},{24,0},{1,25},{9,17},{17,9},{25,1},{2,26},{10... | collective-permute-start | bytes 1769480 | tf_op jit(solution)/shard_map/ppermute | solution.py:1277
  409.4 18.2 %all-to-all-start.7 = ((bf16[32,2,1728]{2,1,0:T(2,128)(2,1)}), bf16[32,2,1728]{2,1,0:T(2,128)(2,1)S(1)}, u32[]{:S(2)}, u32[]{:S(2)}) async-start(bf16[32,2,1728]{2,1,0:T(2,128)(2,1)} %reshape.402), calls=%async_computation.7 | async-start | bytes 458752 | tf_op jit(solution)/shard_map/all_to_all | solution.py:1565
  430.6 13.9 %collective-permute-start.10 = (bf16[24,3072]{1,0:T(8,128)(2,1)}, bf16[24,3072]{1,0:T(8,128)(2,1)S(1)}, u32[]{:S(2)}, u32[]{:S(2)}) collective-permute-start(bf16[24,3072]{1,0:T(8,128)(2,1)} %get-tuple-element.175), channel_id=1, source_target_pairs={{0,2},{1,3},{2,0},{3,1},{4,6},{5,7},{6,4},{7,5},{8,10},{9,11},{10,... | collective-permute-start | bytes 442376 | tf_op jit(solution)/shard_map/ppermute | solution.py:1277
  430.7 14.0 %collective-permute-start.11 = (bf16[24,3072]{1,0:T(8,128)(2,1)S(1)}, bf16[24,3072]{1,0:T(8,128)(2,1)S(1)}, u32[]{:S(2)}, u32[]{:S(2)}) collective-permute-start(bf16[24,3072]{1,0:T(8,128)(2,1)S(1)} %get-tuple-element.177), channel_id=1, source_target_pairs={{0,4},{1,5},{2,6},{3,7},{4,0},{5,1},{6,2},{7,3},{8,12},{9,13},{10,... | collective-permute-start | bytes 442376 | tf_op jit(solution)/shard_map/ppermute | solution.py:1277
  430.8 13.8 %collective-permute-start.12 = (bf16[24,3072]{1,0:T(8,128)(2,1)S(1)}, bf16[24,3072]{1,0:T(8,128)(2,1)S(1)}, u32[]{:S(2)}, u32[]{:S(2)}) collective-permute-start(bf16[24,3072]{1,0:T(8,128)(2,1)S(1)} %get-tuple-element.176), channel_id=1, source_target_pairs={{0,6},{1,7},{2,4},{3,5},{4,2},{5,3},{6,0},{7,1},{8,14},{9,15},{10,... | collective-permute-start | bytes 442376 | tf_op jit(solution)/shard_map/ppermute | solution.py:1277
  (38 other events, 206.4 us)
Sparse Core Ops, SparseCore 0:
  256.8 169.2 reduce-scatter.1

commit v6 on v5

--- a/solution.py
+++ b/solution.py
@@ -543,7 +543,7 @@
     )(db.reshape(lines, features), ws)
 
 
-TURN_ROWS = 4
+TURN_ROWS = 8
 
 
 def feed_turn_kernel(parts, feeds, turns, *refs):

time: 465 us -> 463 us (level)
  no operation moved by 1% of the time
where the time goes in v6:
time: 463 us; the launch traced here: 454 us
  Pallas kernels  214 us (46%)
  waiting for transfers between devices  83.6 us (18%)
  local copies, waits for them, and re-layouts  62.6 us (14%)
  starting transfers between devices  62 us (13%)
  other arithmetic  17.1 us (4%)
  between operations  15.1 us (3%)
    pallas_call x1, Pallas kernels, feed_turn(): pl.pallas_call(partial(feed_turn_kernel, len(mixed), feeds, turns), grid=...  67.1 us
    all_to_all x3, waiting for transfers between devices, collect(): return lax.all_to_all(flat, 'strips', 0, 0, tiled=True)  48.2 us
    pallas_call x2, Pallas kernels, attend_back(): pl.pallas_call(partial(attend_back_kernel, None if weight is None else le...  42.4 us
    unnamed x92, local copies, waits for them, and re-layouts  31.3 us
    pallas_call x2, Pallas kernels, attend(): pl.pallas_call(attend_kernel, grid=(pairs,), in_specs=[pl.BlockSpec((toke...  31 us
    all_to_all x3, waiting for transfers between devices, spread(): got = lax.all_to_all(flat, 'strips', 0, 0, tiled=True)  22.3 us
    all_to_all x3, starting transfers between devices, spread(): got = lax.all_to_all(flat, 'strips', 0, 0, tiled=True)  18.8 us
    pallas_call x1, Pallas kernels, feed_grads(): pl.pallas_call(feed_grads_kernel, grid=(steps,), in_specs=[pl.BlockSpec((...  16.1 us
  transfers between devices with their start and end apart: 22, of which 9 were waited for; matrix products, arithmetic and copies ran while one was open for 12% of the time, Pallas kernels for 26%

profile of v6, /device:TPU:0, one launch (start us, length us, event | category | flops | bytes accessed | tf_op | source)
XLA Modules:
  0.0 454.0 jit_solution(24819069918108988)
XLA Ops:
  28.2 5.8 %front.1 = (bf16[2,4,128,768]{3,2,1,0:T(8,128)(2,1)}, bf16[2,10,64,768]{3,2,1,0:T(8,128)(2,1)S(1)}, bf16[2,8,64,768]{3,2,1,0:T(8,128)(2,1)S(1)}) custom-call(f32[2]{0:T(128)S(1)} %add_convert_fusion.1.edge_ref.refs_0_, bf16[2,8,64,768]{3,2,1,0:T(8,128)(2,1)S(1)} %copy-done.5, bf16[2,1,64,768]{3,2,1,0:T(8,128)(2,1)S(1)} %get-tuple-element.181.top_ref, ...), custom_call_target="tpu_custom_call" | custom-call | flops 117964800 | bytes 6291456 | tf_op jit(solution)/shard_map/front/pallas_call | solution.py:162
  36.6 6.4 %all-to-all-start = ((bf16[8,128,768]{2,1,0:T(8,128)(2,1)}), bf16[8,128,768]{2,1,0:T(8,128)(2,1)}, u32[]{:S(2)}, u32[]{:S(2)}) async-start(bf16[8,128,768]{2,1,0:T(8,128)(2,1)} %bitcast.6), calls=%async_computation | async-start | bytes 3145728 | tf_op jit(solution)/shard_map/all_to_all | solution.py:1375
  51.5 10.7 %feed_upstream.1.refs_4_ = bf16[1280,3072]{1,0:T(8,128)(2,1)} custom-call(bf16[1280,768]{1,0:T(8,128)(2,1)} %bitcast.113, bf16[3072,768]{1,0:T(8,128)(2,1)} %refs_16_.1), custom_call_target="tpu_custom_call" | custom-call | flops 6039797760 | bytes 9830400 | tf_op jit(solution)/shard_map/feed_upstream/pallas_call | solution.py:531
  62.2 18.7 %all-to-all-done = bf16[8,128,768]{2,1,0:T(8,128)(2,1)} async-done(((bf16[8,128,768]{2,1,0:T(8,128)(2,1)}), bf16[8,128,768]{2,1,0:T(8,128)(2,1)}, u32[]{:S(2)}, u32[]{:S(2)}) %all-to-all-start) | async-done | bytes 1572896 | tf_op jit(solution)/shard_map/all_to_all | solution.py:1375
  80.9 15.5 %attend.2 = (bf16[1024,384]{1,0:T(8,128)(2,1)}, bf16[1024,384]{1,0:T(8,128)(2,1)}, bf16[1024,384]{1,0:T(8,128)(2,1)}, bf16[1024,384]{1,0:T(8,128)(2,1)}, f32[3,2,1024]{2,1,0:T(2,128)}) custom-call(bf16[1024,768]{1,0:T(8,128)(2,1)} %bitcast.7.x_ref.refs_0_, bf16[768,2304]{1,0:T(8,128)(2,1)} %refs_6_.1, bf16[768,2304]{1,0:T(8,128)(2,1)} %refs_6_.1, ...), custom_call_target="tpu_custom_call" | custom-call | flops 8254390272 | bytes 6488064 | tf_op jit(solution)/shard_map/attend/pallas_call | solution.py:277
  96.4 4.1 all-to-all-start.1
  100.5 15.5 %attend.3 = (bf16[1024,384]{1,0:T(8,128)(2,1)}, bf16[1024,384]{1,0:T(8,128)(2,1)}, bf16[1024,384]{1,0:T(8,128)(2,1)}, bf16[1024,384]{1,0:T(8,128)(2,1)}, f32[3,2,1024]{2,1,0:T(2,128)}) custom-call(bf16[1024,768]{1,0:T(8,128)(2,1)} %bitcast.7.x_ref.refs_0_, bf16[768,2304]{1,0:T(8,128)(2,1)} %refs_6_.1, bf16[768,2304]{1,0:T(8,128)(2,1)} %refs_6_.1, ...), custom_call_target="tpu_custom_call" | custom-call | flops 8254390272 | bytes 6488064 | tf_op jit(solution)/shard_map/attend/pallas_call | solution.py:277
  116.0 5.4 %all-to-all-done.1 = bf16[8,128,384]{2,1,0:T(8,128)(2,1)S(1)} async-done(((bf16[8,128,384]{2,1,0:T(8,128)(2,1)}), bf16[8,128,384]{2,1,0:T(8,128)(2,1)S(1)}, u32[]{:S(2)}, u32[]{:S(2)}) %all-to-all-start.1) | async-done | bytes 786464 | tf_op jit(solution)/shard_map/all_to_all | solution.py:1380
  127.6 18.3 %all-to-all-done.2 = bf16[8,128,384]{2,1,0:T(8,128)(2,1)S(1)} async-done(((bf16[8,128,384]{2,1,0:T(8,128)(2,1)}), bf16[8,128,384]{2,1,0:T(8,128)(2,1)S(1)}, u32[]{:S(2)}, u32[]{:S(2)}) %all-to-all-start.2) | async-done | bytes 786464 | tf_op jit(solution)/shard_map/all_to_all | solution.py:1380
  146.7 6.5 %middle.1 = (f32[2,8,64,768]{3,2,1,0:T(8,128)}, f32[2,8,64,768]{3,2,1,0:T(8,128)}, bf16[2,8,64,768]{3,2,1,0:T(8,128)(2,1)}, bf16[2,2,64,768]{3,2,1,0:T(8,128)(2,1)}, bf16[2,2,64,768]{3,2,1,0:T(8,128)(2,1)}) custom-call(bf16[2,4,128,384]{3,2,1,0:T(8,128)(2,1)} %bitcast.124, bf16[2,4,128,384]{3,2,1,0:T(8,128)(2,1)} %bitcast.126, bf16[768,768]{1,0:T(8,128)(2,1)} %refs_18_.1, ...), custom_call_target="tpu_custom_call" | custom-call | flops 1207959552 | bytes 11010048 | tf_op jit(solution)/shard_map/middle/pallas_call | solution.py:497
  159.5 67.1 %feed_turn.1 = (f32[16,3072]{1,0:T(8,128)}, bf16[1024,3072]{1,0:T(8,128)(2,1)}, bf16[1024,3072]{1,0:T(8,128)(2,1)}, bf16[2,8,64,768]{3,2,1,0:T(8,128)(2,1)}, f32...) custom-call(f32[2]{0:T(128)} %copy-done.13, ...), custom_call_target="tpu_custom_call" | custom-call | flops 19327352832 | bytes 61341696 | tf_op jit(solution)/shard_map/feed_turn/pallas_call | solution.py:793
  226.6 7.9 %all-to-all-start.4 = ((bf16[8,128,384]{2,1,0:T(8,128)(2,1)}), bf16[8,128,384]{2,1,0:T(8,128)(2,1)}, u32[]{:S(2)}, u32[]{:S(2)}) async-start(bf16[8,128,384]{2,1,0:T(8,128)(2,1)} %bitcast.129), calls=%async_computation.4 | async-start | bytes 1572864 | tf_op jit(solution)/shard_map/all_to_all | solution.py:1375
  238.8 16.1 %feed_grads.1 = bf16[32,8,24,768]{3,2,1,0:T(8,128)(2,1)} custom-call(bf16[1024,3072]{1,0:T(8,128)(2,1)} %get-tuple-element.120.act_ref, bf16[1024,3072]{1,0:T(8,128)(2,1)} %get-tuple-element.121.d_hid_ref, bf16[2,8,64,768]{3,2,1,0:T(8,128)(2,1)} %get-tuple-element.99.refs_1_.nb_ref, bf16[2,10,64,768]{3,2,1,0:T(8,128)(2,1)} %copy-done.14), custom_call_target="tpu_custom_call" | custom-call | flops 9663676416 | bytes 31457280 | tf_op jit(solution)/shard_map/feed_grads/pallas_call | solution.py:911
  255.7 4.5 all-to-all-start.3
  260.2 18.1 %attend_back.2 = (bf16[1024,384]{1,0:T(8,128)(2,1)}, bf16[1024,384]{1,0:T(8,128)(2,1)}, bf16[1024,384]{1,0:T(8,128)(2,1)}) custom-call(bf16[1024,384]{1,0:T(8,128)(2,1)} %get-tuple-element.116.refs_0_, bf16[1024,384]{1,0:T(8,128)(2,1)} %get-tuple-element.117.refs_1_, bf16[1024,384]{1,0:T(8,128)(2,1)} %get-tuple-element.118.refs_2_, ...), custom_call_target="tpu_custom_call" | custom-call | flops 16106127360 | bytes 6291456 | tf_op jit(solution)/shard_map/attend_back/pallas_call | solution.py:386
  287.9 24.3 %attend_back.3 = (bf16[1024,384]{1,0:T(8,128)(2,1)}, bf16[1024,384]{1,0:T(8,128)(2,1)}, bf16[1024,384]{1,0:T(8,128)(2,1)}, bf16[1024,768]{1,0:T(8,128)(2,1)}) custom-call(bf16[1024,384]{1,0:T(8,128)(2,1)} %get-tuple-element.111.refs_0_, bf16[1024,384]{1,0:T(8,128)(2,1)} %get-tuple-element.112.refs_1_, bf16[1024,384]{1,0:T(8,128)(2,1)} %get-tuple-element.113.refs_2_, ...), custom_call_target="tpu_custom_call" | custom-call | flops 16106127360 | bytes 6291456 | tf_op jit(solution)/shard_map/attend_back/pallas_call | solution.py:386
  312.3 5.3 %all-to-all-start.5 = ((bf16[8,128,768]{2,1,0:T(8,128)(2,1)}), bf16[8,128,768]{2,1,0:T(8,128)(2,1)}, u32[]{:S(2)}, u32[]{:S(2)}) async-start(bf16[8,128,768]{2,1,0:T(8,128)(2,1)} %bitcast.119), calls=%async_computation.5 | async-start | bytes 3145728 | tf_op jit(solution)/shard_map/all_to_all | solution.py:1380
  317.5 10.0 %input_grad.1 = (bf16[768,3072]{1,0:T(8,128)(2,1)}, f32[8,1536]{1,0:T(8,128)}) custom-call(bf16[1024,768]{1,0:T(8,128)(2,1)} %bitcast.7.x_ref.refs_0_, bf16[768,768]{1,0:T(8,128)(2,1)} %get-tuple-element.134.refs_1_, bf16[1024,384]{1,0:T(8,128)(2,1)} %get-tuple-element.124.refs_7_.refs_2_, bf16[1024,384]{1,0:T(8,128)(2,1)} %get-tuple-element.125.refs_8_.refs_3_, ...), custom_call_target="tpu_custom_call" | custom-call | flops 3623878656 | bytes 7864320 | tf_op jit(solution)/shard_map/input_grad/pallas_call | solution.py:431
  327.5 5.0 %dynamic-slice_bitcast_fusion = (bf16[4,4,24,3072]{3,2,1,0:T(8,128)(2,1)}, bf16[4,4,24,3072]{3,2,1,0:T(8,128)(2,1)}) fusion(bf16[4,4,2,24,3072]{4,3,2,1,0:T(8,128)(2,1)} %bitcast.114, s32[]{:T(128)S(6)} %select_n.75, s32[]{:T(128)S(6)} %select_n.74), kind=kLoop, calls=%fused_computation.1 | loop fusion | bytes 9437192 | tf_op jit(solution)/shard_map/jit(dynamic_index_in_dim)/squeeze | solution.py:1523
  346.0 24.5 %all-to-all-done.5 = bf16[8,128,768]{2,1,0:T(8,128)(2,1)} async-done(((bf16[8,128,768]{2,1,0:T(8,128)(2,1)}), bf16[8,128,768]{2,1,0:T(8,128)(2,1)}, u32[]{:S(2)}, u32[]{:S(2)}) %all-to-all-start.5) | async-done | bytes 1572896 | tf_op jit(solution)/shard_map/all_to_all | solution.py:1380
  388.2 13.2 %final.1 = (bf16[2,8,64,768]{3,2,1,0:T(8,128)(2,1)}, f32[16,768]{1,0:T(8,128)}, f32[2,8,768]{2,1,0:T(8,128)}) custom-call(bf16[2,4,128,768]{3,2,1,0:T(8,128)(2,1)} %bitcast.25.d_ref, bf16[2,2,32,768]{3,2,1,0:T(8,128)(2,1)} %copy-done.22, bf16[2,2,32,768]{3,2,1,0:T(8,128)(2,1)} %copy-done.23, bf16[2,10,64,768]{3,2,1,0:T(8,128)(2,1)} %copy-done.7, ...), custom_call_target="tpu_custom_call" | custom-call | flops 141557760 | bytes 9437184 | tf_op jit(solution)/shard_map/final/pallas_call | solution.py:1029
  407.6 5.6 %all-to-all-start.7 = ((bf16[32,2,1728]{2,1,0:T(2,128)(2,1)}), bf16[32,2,1728]{2,1,0:T(2,128)(2,1)S(1)}, u32[]{:S(2)}, u32[]{:S(2)}) async-start(bf16[32,2,1728]{2,1,0:T(2,128)(2,1)} %reshape.402), calls=%async_computation.7 | async-start | bytes 458752 | tf_op jit(solution)/shard_map/all_to_all | solution.py:1565
  414.4 11.4 %all-to-all-done.7 = bf16[32,2,1728]{2,1,0:T(2,128)(2,1)S(1)} async-done(((bf16[32,2,1728]{2,1,0:T(2,128)(2,1)}), bf16[32,2,1728]{2,1,0:T(2,128)(2,1)S(1)}, u32[]{:S(2)}, u32[]{:S(2)}) %all-to-all-start.7) | async-done | bytes 221216 | tf_op jit(solution)/shard_map/all_to_all | solution.py:1565
  429.2 4.0 collective-permute-start.12
  (228 shorter events, 115.0 us)
Async XLA Ops:
  9.3 15.4 %collective-permute-start.1 = (bf16[2,2,64,768]{3,2,1,0:T(8,128)(2,1)}, bf16[2,2,64,768]{3,2,1,0:T(8,128)(2,1)}, u32[]{:S(2)}, u32[]{:S(2)}) collective-permute-start(bf16[2,2,64,768]{3,2,1,0:T(8,128)(2,1)} %pad_maximum_fusion.1), channel_id=1, source_target_pairs={{1,0},{2,1},{3,2},{4,3},{5,4},{6,5},{7,6},{9,8},{10,9},{11,10},{12... | collective-permute-start | bytes 1179656 | tf_op jit(solution)/shard_map/ppermute | solution.py:1061
  11.5 14.2 %collective-permute-start = (bf16[2,2,64,768]{3,2,1,0:T(8,128)(2,1)}, bf16[2,2,64,768]{3,2,1,0:T(8,128)(2,1)}, u32[]{:S(2)}, u32[]{:S(2)}) collective-permute-start(bf16[2,2,64,768]{3,2,1,0:T(8,128)(2,1)} %pad_maximum_fusion), channel_id=1, source_target_pairs={{0,1},{1,2},{2,3},{3,4},{4,5},{5,6},{6,7},{8,9},{9,10},{10,11},{11... | collective-permute-start | bytes 1179656 | tf_op jit(solution)/shard_map/ppermute | solution.py:1056
  24.5 22.2 %copy-start.12 = (f32[2,1,768]{2,1,0:T(1,128)}, f32[2,1,768]{2,1,0:T(1,128)S(1)}, u32[]{:S(2)}) copy-start(f32[2,1,768]{2,1,0:T(1,128)S(1)} %get-tuple-element.216.gate_ref.refs_12_) | copy-start | bytes 18436
  36.6 44.4 %all-to-all-start = ((bf16[8,128,768]{2,1,0:T(8,128)(2,1)}), bf16[8,128,768]{2,1,0:T(8,128)(2,1)}, u32[]{:S(2)}, u32[]{:S(2)}) async-start(bf16[8,128,768]{2,1,0:T(8,128)(2,1)} %bitcast.6), calls=%async_computation | async-start | bytes 3145728 | tf_op jit(solution)/shard_map/all_to_all | solution.py:1375
  96.4 25.0 %all-to-all-start.1 = ((bf16[8,128,384]{2,1,0:T(8,128)(2,1)}), bf16[8,128,384]{2,1,0:T(8,128)(2,1)S(1)}, u32[]{:S(2)}, u32[]{:S(2)}) async-start(bf16[8,128,384]{2,1,0:T(8,128)(2,1)} %bitcast.123), calls=%async_computation.1 | async-start | bytes 1572864 | tf_op jit(solution)/shard_map/all_to_all | solution.py:1380
  121.4 24.5 %copy-start.20 = (bf16[8,128,384]{2,1,0:T(8,128)(2,1)}, bf16[8,128,384]{2,1,0:T(8,128)(2,1)S(1)}, u32[]{:S(2)}) copy-start(bf16[8,128,384]{2,1,0:T(8,128)(2,1)S(1)} %all-to-all-done.1) | copy-start | bytes 2359300
  121.4 24.5 %all-to-all-start.2 = ((bf16[8,128,384]{2,1,0:T(8,128)(2,1)}), bf16[8,128,384]{2,1,0:T(8,128)(2,1)S(1)}, u32[]{:S(2)}, u32[]{:S(2)}) async-start(bf16[8,128,384]{2,1,0:T(8,128)(2,1)} %bitcast.122), calls=%async_computation.2 | async-start | bytes 1572864 | tf_op jit(solution)/shard_map/all_to_all | solution.py:1380
  153.3 4.7 %collective-permute-start.2 = (bf16[2,2,64,768]{3,2,1,0:T(8,128)(2,1)}, bf16[2,2,64,768]{3,2,1,0:T(8,128)(2,1)}, u32[]{:S(2)}, u32[]{:S(2)}) collective-permute-start(bf16[2,2,64,768]{3,2,1,0:T(8,128)(2,1)} %get-tuple-element.100), channel_id=1, source_target_pairs={{0,1},{1,2},{2,3},{3,4},{4,5},{5,6},{6,7},{8,9},{9,10},{10,11},{11... | collective-permute-start | bytes 1179656 | tf_op jit(solution)/shard_map/ppermute | solution.py:1056
  155.5 3.9 collective-permute-start.3
  226.6 29.1 %all-to-all-start.4 = ((bf16[8,128,384]{2,1,0:T(8,128)(2,1)}), bf16[8,128,384]{2,1,0:T(8,128)(2,1)}, u32[]{:S(2)}, u32[]{:S(2)}) async-start(bf16[8,128,384]{2,1,0:T(8,128)(2,1)} %bitcast.129), calls=%async_computation.4 | async-start | bytes 1572864 | tf_op jit(solution)/shard_map/all_to_all | solution.py:1375
  234.5 209.8 %reduce-scatter.2.cloned.1.call-start = ((), (), s32[]{:S(2)}) async-start(), calls=%async_computation.9 | async-start | bytes 9732096 | tf_op jit(solution)/shard_map/reduce_scatter | solution.py:1456
  255.7 25.6 %all-to-all-start.3 = ((bf16[8,128,384]{2,1,0:T(8,128)(2,1)}), bf16[8,128,384]{2,1,0:T(8,128)(2,1)}, u32[]{:S(2)}, u32[]{:S(2)}) async-start(bf16[8,128,384]{2,1,0:T(8,128)(2,1)} %bitcast.128), calls=%async_computation.3 | async-start | bytes 1572864 | tf_op jit(solution)/shard_map/all_to_all | solution.py:1375
  284.0 28.3 %all-to-all-start.6 = ((bf16[32,2,3648]{2,1,0:T(2,128)(2,1)}), bf16[32,2,3648]{2,1,0:T(2,128)(2,1)S(1)}, u32[]{:S(2)}, u32[]{:S(2)}) async-start(bf16[32,2,3648]{2,1,0:T(2,128)(2,1)} %reshape.400), calls=%async_computation.6 | async-start | bytes 950272 | tf_op jit(solution)/shard_map/all_to_all | solution.py:1499
  312.3 58.3 %all-to-all-start.5 = ((bf16[8,128,768]{2,1,0:T(8,128)(2,1)}), bf16[8,128,768]{2,1,0:T(8,128)(2,1)}, u32[]{:S(2)}, u32[]{:S(2)}) async-start(bf16[8,128,768]{2,1,0:T(8,128)(2,1)} %bitcast.119), calls=%async_computation.5 | async-start | bytes 3145728 | tf_op jit(solution)/shard_map/all_to_all | solution.py:1380
  370.6 5.8 %collective-permute-start.6 = (bf16[4,4,24,3072]{3,2,1,0:T(8,128)(2,1)}, bf16[4,4,24,3072]{3,2,1,0:T(8,128)(2,1)}, u32[]{:S(2)}, u32[]{:S(2)}) collective-permute-start(bf16[4,4,24,3072]{3,2,1,0:T(8,128)(2,1)} %get-tuple-element.147), channel_id=1, source_target_pairs={{0,1},{1,0},{2,3},{3,2},{4,5},{5,4},{6,7},{7,6},{8,9},{9,8},{10,11... | collective-permute-start | bytes 7077896 | tf_op jit(solution)/shard_map/ppermute | solution.py:1269
  372.7 14.7 %collective-permute-start.4 = (bf16[2,2,32,768]{3,2,1,0:T(8,128)(2,1)S(1)}, bf16[2,2,32,768]{3,2,1,0:T(8,128)(2,1)S(1)}, u32[]{:S(2)}, u32[]{:S(2)}) collective-permute-start(bf16[2,2,32,768]{3,2,1,0:T(8,128)(2,1)S(1)} %get-tuple-element.168), channel_id=1, source_target_pairs={{0,1},{1,2},{2,3},{3,4},{4,5},{5,6},{6,7},{8,9},{9,10},{10,11},{11... | collective-permute-start | bytes 589832 | tf_op jit(solution)/shard_map/ppermute | solution.py:1056
  375.0 12.4 %collective-permute-start.5 = (bf16[2,2,32,768]{3,2,1,0:T(8,128)(2,1)S(1)}, bf16[2,2,32,768]{3,2,1,0:T(8,128)(2,1)S(1)}, u32[]{:S(2)}, u32[]{:S(2)}) collective-permute-start(bf16[2,2,32,768]{3,2,1,0:T(8,128)(2,1)S(1)} %get-tuple-element.167), channel_id=1, source_target_pairs={{1,0},{2,1},{3,2},{4,3},{5,4},{6,5},{7,6},{9,8},{10,9},{11,10},{12... | collective-permute-start | bytes 589832 | tf_op jit(solution)/shard_map/ppermute | solution.py:1061
  382.3 43.8 %collective-permute-start.7 = (bf16[4,24,3072]{2,1,0:T(8,128)(2,1)}, bf16[4,24,3072]{2,1,0:T(8,128)(2,1)}, u32[]{:S(2)}, u32[]{:S(2)}) collective-permute-start(bf16[4,24,3072]{2,1,0:T(8,128)(2,1)} %get-tuple-element.164), channel_id=1, source_target_pairs={{0,8},{8,0},{16,24},{24,16},{1,9},{9,1},{17,25},{25,17},{2,10},{10... | collective-permute-start | bytes 1769480 | tf_op jit(solution)/shard_map/ppermute | solution.py:1277
  383.7 42.4 %collective-permute-start.8 = (bf16[4,24,3072]{2,1,0:T(8,128)(2,1)}, bf16[4,24,3072]{2,1,0:T(8,128)(2,1)}, u32[]{:S(2)}, u32[]{:S(2)}) collective-permute-start(bf16[4,24,3072]{2,1,0:T(8,128)(2,1)} %get-tuple-element.166), channel_id=1, source_target_pairs={{0,16},{8,24},{16,0},{24,8},{1,17},{9,25},{17,1},{25,9},{2,18},{10... | collective-permute-start | bytes 1769480 | tf_op jit(solution)/shard_map/ppermute | solution.py:1277
  385.2 40.9 %collective-permute-start.9 = (bf16[4,24,3072]{2,1,0:T(8,128)(2,1)S(1)}, bf16[4,24,3072]{2,1,0:T(8,128)(2,1)}, u32[]{:S(2)}, u32[]{:S(2)}) collective-permute-start(bf16[4,24,3072]{2,1,0:T(8,128)(2,1)S(1)} %get-tuple-element.165), channel_id=1, source_target_pairs={{0,24},{8,16},{16,8},{24,0},{1,25},{9,17},{17,9},{25,1},{2,26},{10... | collective-permute-start | bytes 1769480 | tf_op jit(solution)/shard_map/ppermute | solution.py:1277
  407.6 18.1 %all-to-all-start.7 = ((bf16[32,2,1728]{2,1,0:T(2,128)(2,1)}), bf16[32,2,1728]{2,1,0:T(2,128)(2,1)S(1)}, u32[]{:S(2)}, u32[]{:S(2)}) async-start(bf16[32,2,1728]{2,1,0:T(2,128)(2,1)} %reshape.402), calls=%async_computation.7 | async-start | bytes 458752 | tf_op jit(solution)/shard_map/all_to_all | solution.py:1565
  428.8 13.9 %collective-permute-start.10 = (bf16[24,3072]{1,0:T(8,128)(2,1)}, bf16[24,3072]{1,0:T(8,128)(2,1)S(1)}, u32[]{:S(2)}, u32[]{:S(2)}) collective-permute-start(bf16[24,3072]{1,0:T(8,128)(2,1)} %get-tuple-element.175), channel_id=1, source_target_pairs={{0,2},{1,3},{2,0},{3,1},{4,6},{5,7},{6,4},{7,5},{8,10},{9,11},{10,... | collective-permute-start | bytes 442376 | tf_op jit(solution)/shard_map/ppermute | solution.py:1277
  428.9 14.0 %collective-permute-start.11 = (bf16[24,3072]{1,0:T(8,128)(2,1)S(1)}, bf16[24,3072]{1,0:T(8,128)(2,1)S(1)}, u32[]{:S(2)}, u32[]{:S(2)}) collective-permute-start(bf16[24,3072]{1,0:T(8,128)(2,1)S(1)} %get-tuple-element.177), channel_id=1, source_target_pairs={{0,4},{1,5},{2,6},{3,7},{4,0},{5,1},{6,2},{7,3},{8,12},{9,13},{10,... | collective-permute-start | bytes 442376 | tf_op jit(solution)/shard_map/ppermute | solution.py:1277
  429.2 13.7 %collective-permute-start.12 = (bf16[24,3072]{1,0:T(8,128)(2,1)S(1)}, bf16[24,3072]{1,0:T(8,128)(2,1)S(1)}, u32[]{:S(2)}, u32[]{:S(2)}) collective-permute-start(bf16[24,3072]{1,0:T(8,128)(2,1)S(1)} %get-tuple-element.176), channel_id=1, source_target_pairs={{0,6},{1,7},{2,4},{3,5},{4,2},{5,3},{6,0},{7,1},{8,14},{9,15},{10,... | collective-permute-start | bytes 442376 | tf_op jit(solution)/shard_map/ppermute | solution.py:1277
  (38 other events, 206.5 us)
Sparse Core Ops, SparseCore 0:
  255.0 169.2 reduce-scatter.1
